TPU v7x, 32 devices: a whole 2x2x4 slice. The times are simulated.
32 devices in a mesh: ctx: 8 (over z, y), head: 4 (over x, core).
Axes of the slice: x: 2, y: 2, z: 4, core: 2. Of those that a mesh axis runs over, the one named last changes fastest.
Arguments:
- queries: bfloat16 [1024, 32, 128], P('ctx', 'head'), may hold values from -70 to 70
- keys: bfloat16 [1024, 32, 128], P('ctx', 'head'), may hold values from -6 to 6
- values: bfloat16 [1024, 32, 128], P('ctx', 'head'), may hold values from -6 to 6
- teacher: bfloat16 [1024, 32, 128], P('ctx', 'head'), may hold values from -18 to 18
- wq: bfloat16 [32, 64, 128], P('head'), may hold values from -0.5 to 0.5
- wk: bfloat16 [32, 64, 128], P('head'), may hold values from -0.5 to 0.5
Outputs:
- student: bfloat16 [1024, 32, 128], P('ctx', 'head')
- loss: float32 [], replicated
- grad_wq: float32 [32, 64, 128], P('head')
- grad_wk: float32 [32, 64, 128], P('head')
All inputs are finite; a program needn't handle non-finite values.
Results may differ from a plain program's by a relative error of at most 0.006.
Values may be sent and summed in bfloat16 or wider, within the bound.
No kernel may reach another device: no remote copies, remote signals or barrier semaphores. Data moves between devices by JAX's collectives and lax.ppermute only.
A program may use at most 128 MiB of HBM per device.

v0:
```python
import jax
import jax.numpy as jnp
from jax import lax
from jax.sharding import PartitionSpec as P

WIN = 64


def shifted(array, axis, by):
    length = lax.axis_size(axis)
    pairs = [(i, i + by) for i in range(length) if 0 <= i + by < length]
    return lax.ppermute(array, axis, pairs)


def carried_in(value, axis, join, neutral):
    count, mine = (lax.axis_size(axis), lax.axis_index(axis))
    pieces = jax.tree.map(lambda part: lax.all_gather(part, axis), value)
    subtotal = jax.tree.map(
        lambda part, zero: jnp.full_like(part, 0) + jnp.asarray(zero, part.dtype), value, neutral
    )

    def hop(position, subtotal):
        longer = join(subtotal, jax.tree.map(lambda part: part[position], pieces))
        return jax.tree.map(lambda new, old: jnp.where(position < mine, new, old), longer, subtotal)

    return lax.fori_loop(0, count - 1, hop, subtotal)


def carried_in_2(array, axis, combine, identity):
    length, index = (lax.axis_size(axis), lax.axis_index(axis))
    everything = jax.tree.map(
        lambda part, kind: lax.all_gather(part.astype(kind), axis),
        array,
        jax.tree.map(lambda a: jnp.bfloat16 if a.dtype == jnp.float32 else a.dtype, array),
    )
    start = jax.tree.map(
        lambda part, zero: jnp.broadcast_to(jnp.asarray(zero, part.dtype), part.shape),
        array,
        identity,
    )

    def hop(k, before):
        at = length - 1 - k
        reached = at > index
        new = combine(
            before, jax.tree.map(lambda part, own: part[at].astype(own.dtype), everything, array)
        )
        return jax.tree.map(lambda a, b: jnp.where(reached, a, b), new, before)

    return lax.fori_loop(0, length, hop, start)


def phi_parts(x, w):
    proj = jnp.einsum("thd,hfd->thf", x, w, preferred_element_type=jnp.float32)
    return (jax.nn.softmax(proj, axis=-1), jax.nn.softmax(-proj, axis=-1))


def phi_grad(x, parts, grad_feat):
    half = grad_feat.shape[-1] // 2
    up_part, down_part = parts
    g_up = grad_feat[..., :half]
    g_down = grad_feat[..., half:]
    d_proj = up_part * (g_up - jnp.sum(up_part * g_up, axis=-1, keepdims=True))
    d_proj = d_proj - down_part * (g_down - jnp.sum(down_part * g_down, axis=-1, keepdims=True))
    return jnp.einsum(
        "thf,thd->hfd", d_proj, x.astype(jnp.float32), precision=lax.Precision.HIGHEST
    )


def add_pair(earlier, later):
    return (earlier[0] + later[0], earlier[1] + later[1])


def per_device(queries, keys, values, teacher, wq, wk):
    high = lax.Precision.HIGHEST
    ntok, nhead, hdim = queries.shape
    width = WIN
    scale = 1.0 / hdim**0.5
    tail = jnp.stack([keys[ntok - width :], values[ntok - width :]])
    halo = shifted(tail, "ctx", 1)
    key_all = jnp.concatenate([halo[0], keys], axis=0)
    val_all = jnp.concatenate([halo[1], values], axis=0).astype(jnp.float32)
    first = lax.axis_index("ctx") * ntok
    pos = first - width + jnp.arange(width + ntok, dtype=jnp.int32)
    valid = (pos >= 0).astype(jnp.float32)
    early = first + jnp.arange(ntok, dtype=jnp.int32) < width
    rows = jnp.arange(ntok, dtype=jnp.int32)[:, None]
    cols = jnp.arange(width + ntok, dtype=jnp.int32)[None, :]
    inwin = (cols > rows) & (cols <= rows + width) & (pos[None, :] >= 0)
    lower = cols[:, :ntok] <= rows
    score = jnp.einsum("ihd,chd->hic", queries, key_all, preferred_element_type=jnp.float32) * scale
    score = jnp.where(inwin[None], score, -jnp.inf)
    top = jnp.max(score, axis=-1)
    weight = jnp.where(inwin[None], jnp.exp(score - top[..., None]), 0.0)
    win_num = jnp.einsum("hic,chd->ihd", weight, val_all, precision=high)
    win_den = jnp.sum(weight, axis=-1).T
    q_parts = phi_parts(queries, wq)
    fq = jnp.concatenate(q_parts, axis=-1)
    k_parts = phi_parts(key_all[:ntok], wk)
    fk = jnp.concatenate(k_parts, axis=-1) * valid[:ntok, None, None]
    val_own = val_all[:ntok]
    local_state = jnp.einsum("chf,chd->hfd", fk, val_own, precision=high)
    local_norm = jnp.sum(fk, axis=0)
    empty = (jnp.zeros_like(local_state), jnp.zeros_like(local_norm))
    state, norm = carried_in((local_state, local_norm), "ctx", add_pair, empty)
    amat = jnp.where(lower[None], jnp.einsum("ihf,chf->hic", fq, fk, precision=high), 0.0)
    lin_num = jnp.einsum("hic,chd->ihd", amat, val_own, precision=high) + jnp.einsum(
        "ihf,hfd->ihd", fq, state, precision=high
    )
    lin_den = jnp.sum(amat, axis=-1).T + jnp.einsum("ihf,hf->ih", fq, norm, precision=high)
    top_t = top.T
    win_scale = jnp.where(early[:, None], 1.0, jnp.exp(jnp.minimum(top_t, 0.0)))
    lin_scale = jnp.where(early[:, None], 0.0, jnp.exp(-jnp.maximum(top_t, 0.0)))
    denom = win_scale * win_den + lin_scale * lin_den
    out = (win_scale[..., None] * win_num + lin_scale[..., None] * lin_num) / denom[..., None]
    diff = out - teacher.astype(jnp.float32)
    grad_out = 2.0 * diff / hdim
    coef = lin_scale / denom
    grad_num = coef[..., None] * grad_out
    grad_den = -coef * jnp.sum(grad_out * out, axis=-1)
    mix = jnp.einsum("ihd,chd->hic", grad_num, val_own, precision=high) + grad_den.T[:, :, None]
    mix = jnp.where(lower[None], mix, 0.0)
    grad_fq = jnp.einsum("hic,chf->ihf", mix, fk, precision=high)
    grad_fq = (
        grad_fq
        + jnp.einsum("hfd,ihd->ihf", state, grad_num, precision=high)
        + norm[None] * grad_den[..., None]
    )
    later_state = jnp.einsum("ihf,ihd->hfd", fq, grad_num, precision=high)
    later_norm = jnp.einsum("ihf,ih->hf", fq, grad_den, precision=high)
    after_state, after_norm = carried_in_2((later_state, later_norm), "ctx", add_pair, empty)
    grad_fk = jnp.einsum("hic,ihf->chf", mix, fq, precision=high)
    grad_fk = (
        grad_fk
        + jnp.einsum("hfd,chd->chf", after_state, val_own, precision=high)
        + after_norm[None]
    )
    grad_fk = grad_fk * valid[:ntok, None, None]
    grad_q = phi_grad(queries, q_parts, grad_fq)
    grad_k = phi_grad(key_all[:ntok], k_parts, grad_fk)
    squared = jnp.sum(diff * diff)
    entries = ntok * lax.axis_size("ctx") * nhead * lax.axis_size("head") * hdim
    grad_q, grad_k, partial_value = lax.psum((grad_q, grad_k, squared), "ctx")
    total = lax.psum(partial_value, "head")
    return (out.astype(jnp.bfloat16), total / entries, grad_q, grad_k)


def solution(mesh):
    placed = (
        P("ctx", "head", None),
        P("ctx", "head", None),
        P("ctx", "head", None),
        P("ctx", "head", None),
        P("head", None, None),
        P("head", None, None),
    )
    return jax.shard_map(
        per_device,
        mesh=mesh,
        in_specs=placed,
        out_specs=(P("ctx", "head", None), P(), P("head", None, None), P("head", None, None)),
        check_vma=False,
    )
```

profile of v0, /device:TPU:0, one launch (start us, length us, event | category | flops | bytes accessed | tf_op | source)
XLA Modules:
  0.0 263.7 jit_solution(11217355819062300662)
XLA Ops:
  7.2 1.0 copy.32
  8.3 1.0 copy.31
  9.4 4.9 %collective-permute-start = (bf16[2,64,8,128]{3,1,2,0:T(8,128)(2,1)S(1)}, bf16[2,64,8,128]{3,1,2,0:T(8,128)(2,1)S(1)}, u32[]{:S(2)}, u32[]{:S(2)}) collective-permute-start(bf16[2,64,8,128]{3,1,2,0:T(8,128)(2,1)S(1)} %pad_maximum_fusion.3), channel_id=1, source_target_pairs={{0,4},{4,8},{8,12},{12,16},{16,20},{20,24},{24,28},{1,5},{5,9},{9,... | collective-permute-start | bytes 786440 | tf_op jit(solution)/shard_map/ppermute | solution.py:12
  14.3 5.5 %collective-permute-done = bf16[2,64,8,128]{3,1,2,0:T(8,128)(2,1)S(1)} collective-permute-done((bf16[2,64,8,128]{3,1,2,0:T(8,128)(2,1)S(1)}, bf16[2,64,8,128]{3,1,2,0:T(8,128)(2,1)S(1)}, u32[]{:S(2)}, u32[]{:S(2)}) %collective-permute-start) | collective-permute-done | bytes 262176 | tf_op jit(solution)/shard_map/ppermute | solution.py:12
  19.8 1.3 fusion.95
  21.1 1.3 fusion.94
  22.5 1.2 fusion.58
  23.9 0.2 copy.43
  24.4 0.3 fusion.96
  24.7 1.2 fusion.97
  26.0 0.2 fusion.57
  26.2 33.0 %all-gather.1 = f32[64,128]{1,0:T(8,128)S(1)} all-gather(f32[8,128]{1,0:T(8,128)S(1)} %fusion.57), channel_id=3, replica_groups=mesh['ctx'=8,'head'=4] {'ctx'}, dimensions={0}, use_global_device_ids=true | all-gather | bytes 36864 | tf_op jit(solution)/shard_map/all_gather | solution.py:17
  59.2 0.3 fusion.99
  59.8 0.7 copy-done.7
  60.5 1.0 fusion.98
  61.5 38.2 %all-gather.7.cloned.1.call-done = f32[64,128,128]{2,1,0:T(8,128)} async-done(((f32[8,128,128]{2,1,0:T(8,128)}), f32[64,128,128]{2,1,0:T(8,128)}) %all-gather.7.cloned.1.call-update) | async-done | bytes 4194320 | tf_op jit(solution)/shard_map/all_gather | solution.py:17
  99.7 8.9 %while.34 = (s32[]{:T(128)}, f32[8,128,128]{2,1,0:T(8,128)S(1)}, f32[8,128]{1,0:T(8,128)S(1)}, s32[]{:T(128)}, f32[8,8,128,128]{3,2,1,0:T(8,128)}, /*index=5*/f32[8,8,128]{2,1,0:T(8,128)S(1)}, s32[]{:T(128)}, s32[]{:T(128)}) while((s32[]{:T(128)}, f32[8,128,128]{2,1,0:T(8,128)S(1)}, f32[8,128]{1,0:T(8,128)S(1)}, s32[]{:T(128)}, ...), condition=%wide.region_11.12_spmd.clone, body=%wide.region_10.11_spmd.clone.sunk | while | flops 396292 | bytes 1585267 | solution.py:26
  99.7 1.2 add_select_fusion.8
  101.0 1.2 add_select_fusion.8
  102.3 1.2 add_select_fusion.8
  103.6 1.2 add_select_fusion.8
  104.8 1.2 add_select_fusion.8
  106.1 1.2 add_select_fusion.8
  107.4 1.2 add_select_fusion.8
  108.6 1.0 fusion.70
  109.7 0.5 fusion.69
  110.3 0.5 fusion.16
  110.8 3.4 %multiply_reduce_fusion = (f32[128,8]{0,1:T(8,128)}, f32[]{:T(128)}, bf16[128,8,128]{0,2,1:T(8,128)(2,1)}, f32[128,8,128]{0,2,1:T(8,128)S(1)}) fusion(bf16[128,8,128]{0,2,1:T(8,128)(2,1)S(1)} %copy.43, f32[128,8]{0,1:T(8,128)S(1)} %get-tuple-element.356, f32[128,8,128]{0,2,1:T(8,128)S(1)} %fusion.16, f32[8,128,192]{1,2,0:T(8,128)} %copy-done.7, ...), kind=kOutput, calls=%fused_computation.45 | convolution fusion | flops 304610304 | bytes 2793476 | tf_op jit(solution)/shard_map/hic,chd->ihd/dot_general | solution.py:95
  114.3 1.9 convolution_convert_fusion
  116.2 0.7 negate_multiply_fusion
  116.9 0.9 fusion.68
  117.9 27.0 %all-gather.3 = bf16[64,128]{1,0:T(8,128)(2,1)} all-gather(bf16[8,128]{1,0:T(8,128)(2,1)S(1)} %convert_element_type.45), channel_id=5, replica_groups=mesh['ctx'=8,'head'=4] {'ctx'}, dimensions={0}, use_global_device_ids=true | all-gather | bytes 18432 | tf_op jit(solution)/shard_map/all_gather | solution.py:32
  144.9 0.7 bitcast_multiply_fusion
  145.6 1.2 fusion.14
  146.8 1.3 convolution_bitcast_fusion.4
  148.2 0.7 fusion.10
  149.0 1.2 convolution_bitcast_fusion.2
  150.2 1.1 fusion.42
  151.3 12.8 %all-gather.9.cloned.1.call-done = bf16[64,128,128]{2,1,0:T(8,128)(2,1)} async-done(((bf16[8,128,128]{2,1,0:T(8,128)(2,1)}), bf16[64,128,128]{2,1,0:T(8,128)(2,1)}) %all-gather.9.cloned.1.call-update) | async-done | bytes 2097168 | tf_op jit(solution)/shard_map/all_gather | solution.py:32
  164.1 15.4 %while.35 = (s32[]{:T(128)}, f32[8,128,128]{2,1,0:T(8,128)S(1)}, f32[8,128]{1,0:T(8,128)S(1)}, s32[]{:T(128)}, bf16[8,8,128,128]{3,2,1,0:T(8,128)(2,1)}, /*index...) while((s32[]{:T(128)}, f32[8,128,128]{2,1,0:T(8,128)S(1)}, ...), condition=%wide.region_22.23_spmd.clone, body=%wide.region_21.22_spmd.clone.sunk | while | flops 528392 | bytes 1321137 | solution.py:50
  164.2 1.3 add_select_fusion.10
  165.5 0.7 add_select_fusion.11
  166.2 1.2 add_select_fusion.10
  167.4 0.7 add_select_fusion.11
  168.1 1.2 add_select_fusion.10
  169.3 0.7 add_select_fusion.11
  170.0 1.2 add_select_fusion.10
  171.2 0.7 add_select_fusion.11
  171.9 1.2 add_select_fusion.10
  173.1 0.7 add_select_fusion.11
  173.8 1.2 add_select_fusion.10
  175.1 0.7 add_select_fusion.11
  175.8 1.2 add_select_fusion.10
  177.0 0.7 add_select_fusion.11
  177.7 1.2 add_select_fusion.10
  178.9 0.7 add_select_fusion.11
  179.6 0.7 fusion.13
  180.4 1.1 fusion.36
  181.5 19.5 %psum.28 = f32[]{:T(128)} all-reduce(f32[]{:T(128)} %get-tuple-element.324), channel_id=1, replica_groups=mesh['ctx'=8,'head'=4] {'ctx'}, use_global_device_ids=true, to_apply=%region_15.16 | all-reduce | flops 1 | bytes 8 | tf_op jit(solution)/shard_map/psum | solution.py:143
  201.1 6.3 %psum.29 = f32[]{:T(128)} all-reduce(f32[]{:T(128)} %psum.28), channel_id=1, replica_groups=mesh['ctx'=8,'head'=4] {'head'}, use_global_device_ids=true, to_apply=%region_16.17 | all-reduce | flops 1 | bytes 8 | tf_op jit(solution)/shard_map/psum | solution.py:144
  207.3 0.9 copy.51
  208.9 43.8 %all-reduce.3.cloned.1.call-done = (f32[8,64,128]{2,1,0:T(8,128)}, f32[8,64,128]{2,1,0:T(8,128)}) async-done(((f32[8,64,128]{2,1,0:T(8,128)}, f32[8,64,128]{2,1,0:T(8,128)}), (f32[8,64,128]{2,1,0:T(8,128)}, f32[8,64,128]{2,1,0:T(8,128)})) %all-reduce.3.cloned.1.call-update) | async-done | bytes 524304 | tf_op jit(solution)/shard_map/psum | solution.py:143
  252.7 1.7 copy.102
  254.3 1.7 copy.103
  (88 shorter events, 1.2 us)
Async XLA Ops:
  7.2 17.2 %copy-start = (bf16[128,8,128]{2,1,0:T(8,128)(2,1)S(1)}, bf16[128,8,128]{2,1,0:T(8,128)(2,1)}, u32[]{:S(2)}) copy-start(bf16[128,8,128]{2,1,0:T(8,128)(2,1)} %param.10) | copy-start | bytes 786436
  7.2 16.7 %copy-start.10 = (bf16[128,8,128]{2,1,0:T(8,128)(2,1)S(1)}, bf16[128,8,128]{2,1,0:T(8,128)(2,1)}, u32[]{:S(2)}) copy-start(bf16[128,8,128]{2,1,0:T(8,128)(2,1)} %param.13) | copy-start | bytes 786436
  7.2 17.2 %copy-start.26 = (bf16[8,64,128]{2,1,0:T(8,128)(2,1)S(1)}, bf16[8,64,128]{2,1,0:T(8,128)(2,1)}, u32[]{:S(2)}) copy-start(bf16[8,64,128]{2,1,0:T(8,128)(2,1)} %param.14) | copy-start | bytes 393220
  7.2 92.5 %all-gather.7.cloned.1.call-start = ((), (), s32[]{:S(2)}) async-start(), calls=%async_computation | async-start | bytes 4718592 | tf_op jit(solution)/shard_map/all_gather | solution.py:17
  9.3 50.0 %copy-start.1 = (bf16[128,8,128]{2,0,1:T(8,128)(2,1)}, bf16[128,8,128]{2,0,1:T(8,128)(2,1)S(1)}, u32[]{:S(2)}) copy-start(bf16[128,8,128]{2,0,1:T(8,128)(2,1)S(1)} %copy.31) | copy-start | bytes 786436
  9.4 10.4 %collective-permute-start = (bf16[2,64,8,128]{3,1,2,0:T(8,128)(2,1)S(1)}, bf16[2,64,8,128]{3,1,2,0:T(8,128)(2,1)S(1)}, u32[]{:S(2)}, u32[]{:S(2)}) collective-permute-start(bf16[2,64,8,128]{3,1,2,0:T(8,128)(2,1)S(1)} %pad_maximum_fusion.3), channel_id=1, source_target_pairs={{0,4},{4,8},{8,12},{12,16},{16,20},{20,24},{24,28},{1,5},{5,9},{9,... | collective-permute-start | bytes 786440 | tf_op jit(solution)/shard_map/ppermute | solution.py:12
  14.3 46.2 %copy-start.23 = (f32[128]{0:T(128)}, f32[128]{0:T(128)S(1)}, u32[]{:S(2)}) copy-start(f32[128]{0:T(128)S(1)} %slice_convert_fusion) | copy-start | bytes 1540
  19.8 39.4 %copy-start.8 = (bf16[64,8,128]{2,0,1:T(8,128)(2,1)}, bf16[64,8,128]{2,0,1:T(8,128)(2,1)S(1)}, u32[]{:S(2)}) copy-start(bf16[64,8,128]{2,0,1:T(8,128)(2,1)S(1)} %get-tuple-element.361) | copy-start | bytes 393220
  21.1 1.4 copy-start.3
  21.1 2.7 %copy-start.18 = (f32[128,8]{0,1:T(8,128)}, f32[128,8]{0,1:T(8,128)S(1)}, u32[]{:S(2)}) copy-start(f32[128,8]{0,1:T(8,128)S(1)} %get-tuple-element.364) | copy-start | bytes 12292
  22.4 1.3 copy-start.5
  22.5 1.3 copy-start.20
  23.8 140.3 %all-gather.9.cloned.1.call-start = ((), (), s32[]{:S(2)}) async-start(), calls=%async_computation.1 | async-start | bytes 2359296 | tf_op jit(solution)/shard_map/all_gather | solution.py:32
  24.1 86.1 %copy-start.25 = (pred[128]{0:T(512)(128)(4,1)}, pred[128]{0:T(512)(128)(4,1)S(1)}, u32[]{:S(2)}) copy-start(pred[128]{0:T(512)(128)(4,1)S(1)} %add_compare_fusion.1) | copy-start | bytes 388
  24.2 75.5 %copy-start.12 = (pred[128,128]{0,1:T(8,128)(4,1)}, pred[128,128]{0,1:T(8,128)(4,1)S(1)}, u32[]{:S(2)}) copy-start(pred[128,128]{0,1:T(8,128)(4,1)S(1)} %iota_compare_fusion.2) | copy-start | bytes 49156
  24.4 75.4 %copy-start.13 = (pred[128,192]{0,1:T(8,128)(4,1)}, pred[128,192]{0,1:T(8,128)(4,1)S(1)}, u32[]{:S(2)}) copy-start(pred[128,192]{0,1:T(8,128)(4,1)S(1)} %fusion.67) | copy-start | bytes 73732
  59.6 0.9 copy-start.7
  59.7 50.5 %copy-start.14 = (f32[8,128]{1,0:T(8,128)}, f32[8,128]{1,0:T(8,128)S(1)}, u32[]{:S(2)}) copy-start(f32[8,128]{1,0:T(8,128)S(1)} %fusion.25) | copy-start | bytes 12292
  61.5 48.7 %copy-start.15 = (f32[8,128]{1,0:T(8,128)}, f32[8,128]{1,0:T(8,128)S(1)}, u32[]{:S(2)}) copy-start(f32[8,128]{1,0:T(8,128)S(1)} %get-tuple-element.370) | copy-start | bytes 12292
  110.2 0.6 copy-start.16
  110.2 0.6 copy-start.17
  110.2 6.0 %copy-start.22 = (f32[128,8]{0,1:T(8,128)}, f32[128,8]{0,1:T(8,128)S(1)}, u32[]{:S(2)}) copy-start(f32[128,8]{0,1:T(8,128)S(1)} %get-tuple-element.356) | copy-start | bytes 12292
  116.2 136.5 %all-reduce.3.cloned.1.call-start = ((), (), s32[]{:S(2)}) async-start(), calls=%async_computation.2 | async-start | bytes 1048576 | tf_op jit(solution)/shard_map/psum | solution.py:143
  150.2 29.4 %copy-start.24 = (f32[128]{0:T(128)S(1)}, f32[128]{0:T(128)}, u32[]{:S(2)}) copy-start(f32[128]{0:T(128)} %copy-done.23) | copy-start | bytes 1540
  164.1 16.2 %copy-start.4 = (f32[128,8,64]{0,2,1:T(8,128)S(1)}, f32[128,8,64]{0,2,1:T(8,128)}, u32[]{:S(2)}) copy-start(f32[128,8,64]{0,2,1:T(8,128)} %copy-done.3) | copy-start | bytes 786436
  164.1 16.2 %copy-start.6 = (f32[128,8,64]{0,2,1:T(8,128)S(1)}, f32[128,8,64]{0,2,1:T(8,128)}, u32[]{:S(2)}) copy-start(f32[128,8,64]{0,2,1:T(8,128)} %copy-done.5) | copy-start | bytes 786436
  164.1 16.2 %copy-start.19 = (f32[128,8]{0,1:T(8,128)S(1)}, f32[128,8]{0,1:T(8,128)}, u32[]{:S(2)}) copy-start(f32[128,8]{0,1:T(8,128)} %copy-done.18) | copy-start | bytes 12292
  164.1 16.2 %copy-start.21 = (f32[128,8]{0,1:T(8,128)S(1)}, f32[128,8]{0,1:T(8,128)}, u32[]{:S(2)}) copy-start(f32[128,8]{0,1:T(8,128)} %copy-done.20) | copy-start | bytes 12292
  164.1 16.3 %copy-start.2 = (bf16[128,8,128]{2,0,1:T(8,128)(2,1)S(1)}, bf16[128,8,128]{2,0,1:T(8,128)(2,1)}, u32[]{:S(2)}) copy-start(bf16[128,8,128]{2,0,1:T(8,128)(2,1)} %copy-done.1) | copy-start | bytes 786436
  164.1 16.3 %copy-start.9 = (bf16[64,8,128]{2,0,1:T(8,128)(2,1)S(1)}, bf16[64,8,128]{2,0,1:T(8,128)(2,1)}, u32[]{:S(2)}) copy-start(bf16[64,8,128]{2,0,1:T(8,128)(2,1)} %copy-done.8) | copy-start | bytes 393220
  179.6 27.7 %copy-start.11 = (bf16[128,8,128]{0,2,1:T(8,128)(2,1)S(1)}, bf16[128,8,128]{0,2,1:T(8,128)(2,1)}, u32[]{:S(2)}) copy-start(bf16[128,8,128]{0,2,1:T(8,128)(2,1)} %get-tuple-element.359) | copy-start | bytes 786436
Sparse Core Ops, SparseCore 0:
  23.9 75.8 all-gather.6
  116.3 47.7 all-gather.8
  181.6 70.9 all-reduce.2
where the time goes:
time: 265 us; the launch traced here: 264 us
  waiting for transfers between devices  100 us (38%)
  blocking collectives  85.9 us (32%)
  other arithmetic  26.4 us (10%)
  matrix products  22.2 us (8%)
  between operations  16.1 us (6%)
  local copies, waits for them, and re-layouts  7.47 us (3%)
  starting transfers between devices  5.01 us (2%)
    psum x1, waiting for transfers between devices, per_device(): grad_q, grad_k, partial_value = lax.psum((grad_q, grad_k, squared), 'ctx')  43.8 us
    all_gather x1, waiting for transfers between devices, carried_in(): pieces = jax.tree.map(lambda part: lax.all_gather(part, axis), value)  38.2 us
    all_gather x1, blocking collectives, carried_in(): pieces = jax.tree.map(lambda part: lax.all_gather(part, axis), value)  33 us
    all_gather x1, blocking collectives, carried_in_2(): lax.all_gather(part.astype(kind), axis)  27 us
    psum x1, blocking collectives, per_device(): grad_q, grad_k, partial_value = lax.psum((grad_q, grad_k, squared), 'ctx')  19.5 us
    select_n x16, other arithmetic, hop(): return jax.tree.map(lambda a, b: jnp.where(reached, a, b), new, before)  15.4 us
    all_gather x1, waiting for transfers between devices, carried_in_2(): lax.all_gather(part.astype(kind), axis)  12.8 us
    select_n x14, other arithmetic, hop(): jnp.where(position < mine, new, old)  8.67 us
  transfers between devices with their start and end apart: 4, of which 4 were waited for; matrix products, arithmetic and copies ran while one was open for 5% of the time, Pallas kernels for 0%

commit v1 on v0

v1 whole, which is shorter than its diff:
```python
import functools

import jax
import jax.numpy as jnp
from jax import lax
from jax.experimental import pallas as pl
from jax.experimental.pallas import tpu as pltpu
from jax.sharding import PartitionSpec as P

WIN = 64
QUAD = 4
F32 = jnp.float32
BF16 = jnp.bfloat16


def nt(a, b):
    return lax.dot_general(a, b, (((1,), (1,)), ((), ())), preferred_element_type=F32)


def nn(a, b):
    return lax.dot_general(a, b, (((1,), (0,)), ((), ())), preferred_element_type=F32)


def split2(a):
    high = a.astype(BF16)
    return high, (a - high.astype(F32)).astype(BF16)


def identity(n):
    return (
        lax.broadcasted_iota(jnp.int32, (n, n), 0) == lax.broadcasted_iota(jnp.int32, (n, n), 1)
    ).astype(BF16)


def phi_t(x, w):
    proj = nt(w, x)
    up = jnp.exp(proj - jnp.max(proj, axis=0, keepdims=True))
    down = jnp.exp(jnp.min(proj, axis=0, keepdims=True) - proj)
    up = up * (1.0 / jnp.sum(up, axis=0, keepdims=True))
    down = down * (1.0 / jnp.sum(down, axis=0, keepdims=True))
    return up, down


def phi_pull(up, down, grad):
    half = up.shape[0]
    g_up, g_down = grad[:half], grad[half:]
    d = up * (g_up - jnp.sum(up * g_up, axis=0, keepdims=True))
    return d - down * (g_down - jnp.sum(down * g_down, axis=0, keepdims=True))


def extended(vt):
    row = lax.broadcasted_iota(jnp.int32, (16, vt.shape[1]), 0)
    return jnp.concatenate([vt, (row == 0).astype(BF16)], axis=0)


def to_heads(x_ref, wide):
    tok, heads, d = x_ref.shape
    wide[...] = x_ref[...].astype(F32).reshape(tok * heads, d)
    return [wide[pl.ds(h, tok, stride=heads), :].astype(BF16) for h in range(heads)]


def pack_kernel(where, *refs):
    ins, outs, wide, held = refs[:-6], refs[-6:-2], refs[-2], refs[-1]
    mine = where[0]
    for a, x_ref in enumerate(ins):
        parts = to_heads(x_ref, wide)
        per = len(parts) // QUAD
        for h, part in enumerate(parts):
            held[h // per, a, h % per] = part
    for j, out in enumerate(outs):
        out[...] = held[lax.bitwise_xor(mine, j)]


def key_kernel(where, c0, c1, c2, c3, wk_ref, kv_ref, msg_ref):
    mine = where[0]
    narr, per, tok, d = c0.shape
    for j, c in enumerate((c0, c1, c2, c3)):
        b = lax.bitwise_xor(mine, j)
        kv_ref[:, :, b] = c[...]
    total = QUAD * tok
    eye = identity(d)
    for hh in range(per):
        k = kv_ref[0, hh].reshape(total, d)
        v = kv_ref[1, hh].reshape(total, d)
        up, down = phi_t(k, wk_ref[per * mine + hh])
        feat = jnp.concatenate([up, down], axis=0)
        lane = lax.broadcasted_iota(jnp.int32, feat.shape, 1)
        feat = jnp.where(lane < total - WIN, feat, 0.0).astype(BF16)
        vt = extended(nt(eye, v).astype(BF16))
        state = nt(vt, feat).astype(BF16)
        rows = state.shape[0]
        msg_ref[hh, :rows] = state
        msg_ref[hh, rows : rows + WIN] = k[total - WIN :]
        msg_ref[hh, rows + WIN :] = v[total - WIN :]


def main_kernel(where, kv_ref, c0, c1, c2, c3, msg_ref, wq_ref, wk_ref,
                s0, s1, s2, s3, later_ref, gq_ref, gk_ref, loss_ref, qt, outs, gfk):
    mine, group = where[0], where[1]
    has_past = group > 0
    narr, per, tok, d = c0.shape
    total = QUAD * tok
    for j, c in enumerate((c0, c1, c2, c3)):
        qt[:, :, lax.bitwise_xor(mine, j)] = c[...]
    eye = identity(d)
    scale = 1.0 / d**0.5
    first_key = jnp.where(has_past, tok - WIN, tok)
    loss = jnp.zeros((8, tok), F32)
    for hh in range(per):
        q = qt[0, hh].reshape(total, d)
        teach = nt(eye, qt[1, hh].reshape(total, d))
        halo_k = msg_ref[hh, d + 16 : d + 16 + WIN]
        halo_v = msg_ref[hh, d + 16 + WIN :]
        state = jnp.where(has_past, msg_ref[hh, : d + 16].astype(F32), 0.0)
        state_b = state.astype(BF16)
        state_t = state.T.astype(BF16)
        pad = jnp.zeros((tok - WIN, d), BF16)
        k_all = jnp.concatenate([pad, halo_k, kv_ref[0, hh].reshape(total, d)], axis=0)
        v_all = jnp.concatenate([pad, halo_v, kv_ref[1, hh].reshape(total, d)], axis=0)
        vt_all = extended(nt(eye, v_all).astype(BF16))
        q_up, q_down = phi_t(q, wq_ref[per * mine + hh])
        k_up, k_down = phi_t(k_all, wk_ref[per * mine + hh])
        fq = jnp.concatenate([q_up, q_down], axis=0).astype(BF16)
        fk = jnp.concatenate([k_up, k_down], axis=0)
        fk_rows = fk.T.astype(BF16)
        fk = fk.astype(BF16)
        gfk[...] = jnp.zeros_like(gfk)
        later = jnp.zeros((d + 16, fq.shape[0]), F32)
        gfq = []
        for b in range(QUAD):
            here = slice(b * tok, (b + 1) * tok)
            reach = (b + 2) * tok
            lo = b * tok + WIN
            qb, fqb = q[here], fq[:, here]
            score = nt(k_all[lo:reach], qb) * scale
            row = lax.broadcasted_iota(jnp.int32, score.shape, 0) + lo
            col = lax.broadcasted_iota(jnp.int32, score.shape, 1) + b * tok
            inwin = (row > col + (tok - WIN)) & (row <= col + tok) & (row >= first_key)
            score = jnp.where(inwin, score, -jnp.inf)
            top = jnp.max(score, axis=0, keepdims=True)
            weight = jnp.exp(score - top).astype(BF16)
            weight = jnp.concatenate([jnp.zeros((WIN, tok), BF16), weight], axis=0)
            win = nn(vt_all[:, b * tok : reach], weight)
            row = lax.broadcasted_iota(jnp.int32, (reach, tok), 0)
            col = lax.broadcasted_iota(jnp.int32, (reach, tok), 1) + b * tok
            reached = (row >= first_key) & (row <= col + WIN)
            amat = jnp.where(reached, nn(fk_rows[:reach], fqb), 0.0).astype(BF16)
            lin = nn(vt_all[:, :reach], amat) + nn(state_b, fqb)
            token = lax.broadcasted_iota(jnp.int32, (1, tok), 1) + b * tok
            early = jnp.logical_and(token < WIN, jnp.logical_not(has_past))
            win_scale = jnp.where(early, 1.0, jnp.exp(jnp.minimum(top, 0.0)))
            lin_scale = jnp.where(early, 0.0, jnp.exp(-jnp.maximum(top, 0.0)))
            both = win_scale * win + lin_scale * lin
            denom = both[d : d + 1]
            out = both[:d] / denom
            outs[b, hh] = out.T.astype(BF16)
            diff = out - teach[:, here]
            loss = loss + jnp.sum((diff * diff).reshape(d // 8, 8, tok), axis=0)
            g = diff * (2.0 / d)
            coef = lin_scale / denom
            g_num = coef * g
            g_den = -coef * jnp.sum(g * out, axis=0, keepdims=True)
            pad_row = lax.broadcasted_iota(jnp.int32, (16, tok), 0)
            g_ext = jnp.concatenate([g_num, jnp.where(pad_row == 0, g_den, 0.0)], axis=0).astype(BF16)
            mix = nn(v_all[:reach], g_num.astype(BF16)) + g_den
            mix = jnp.where(reached, mix, 0.0).astype(BF16)
            gfq.append(nn(fk[:, :reach], mix) + nn(state_t, g_ext))
            gfk[:, :reach] += nt(fqb, mix)
            later = later + nt(g_ext, fqb)
        later_ref[hh] = later.astype(BF16)
        for x, up, down, grad, ref in (
            (q, q_up, q_down, jnp.concatenate(gfq, axis=1), gq_ref),
            (k_all, k_up, k_down, gfk[...], gk_ref),
        ):
            high, low = split2(phi_pull(up, down, grad))
            ref[hh] = nn(high, x) + nn(low, x)
    loss_ref[...] = loss
    for j, s in enumerate((s0, s1, s2, s3)):
        s[...] = outs[lax.bitwise_xor(mine, j)]


def put_loss(out_ref, first, loss):
    high, low = split2(loss)
    out_ref[first:] = jnp.concatenate([high, low], axis=0)


def take_loss(ref, first):
    return ref[first : first + 8].astype(F32) + ref[first + 8 : first + 16].astype(F32)


def last_kernel(where, kv_ref, msg_ref, later_ref, wk_ref, gq_ref, gk_ref, l0, l1, l2, l3, out_ref):
    mine, has_past, has_future = where[0], where[1] > 0, where[2] > 0
    per, d = kv_ref.shape[1], kv_ref.shape[-1]
    total = kv_ref.shape[2] * kv_ref.shape[3]
    half = gq_ref.shape[1]
    for hh in range(per):
        after = jnp.where(has_future, later_ref[hh].astype(F32), 0.0)
        after_t = after.T
        k_all = jnp.concatenate([msg_ref[hh, d + 16 : d + 16 + WIN], kv_ref[0, hh].reshape(total, d)], axis=0)
        v_all = jnp.concatenate([msg_ref[hh, d + 16 + WIN :], kv_ref[1, hh].reshape(total, d)], axis=0)
        k_all, v_all = k_all[:total], v_all[:total]
        up, down = phi_t(k_all, wk_ref[per * mine + hh])
        grad = nt(after_t[:, :d].astype(BF16), v_all) + after_t[:, d : d + 1]
        row = lax.broadcasted_iota(jnp.int32, grad.shape, 1)
        grad = jnp.where((row >= WIN) | has_past, grad, 0.0)
        high, low = split2(phi_pull(up, down, grad))
        more = nn(high, k_all) + nn(low, k_all)
        out_ref[hh * half : (hh + 1) * half] = gq_ref[hh].astype(BF16)
        out_ref[(per + hh) * half : (per + hh + 1) * half] = (gk_ref[hh] + more).astype(BF16)
    put_loss(out_ref, 2 * per * half, (l0[...] + l1[...]) + (l2[...] + l3[...]))


def sum_kernel(where, *refs):
    *parts, out_ref = refs
    first = out_ref.shape[0] - 16
    total = sum(part[:first].astype(F32) for part in parts)
    out_ref[:first] = total.astype(BF16)
    put_loss(out_ref, first, sum(take_loss(part, first) for part in parts))


def finish_kernel(entries, where, g0, g1, g2, g3, s0, s1, s2, s3, student, loss, gq, gk, held, wide):
    mine = where[0]
    per, tok, d = s0.shape
    half = gq.shape[1]
    first = 2 * per * half
    l0, l1, l2, l3 = [take_loss(g, first) for g in (g0, g1, g2, g3)]
    loss[0, 0] = jnp.sum((l0 + l1) + (l2 + l3)) / entries
    for j, (g, s) in enumerate(zip((g0, g1, g2, g3), (s0, s1, s2, s3))):
        pair = lax.bitwise_xor(mine, j)
        held[pair] = s[...]
        gq[pl.ds(per * pair, per)] = g[: per * half].astype(F32).reshape(per, half, d)
        gk[pl.ds(per * pair, per)] = g[per * half : first].astype(F32).reshape(per, half, d)
    heads = QUAD * per
    for h in range(heads):
        wide[pl.ds(h, tok, stride=heads), :] = held[h // per, h % per].astype(F32)
    student[...] = wide[...].reshape(tok, heads, d).astype(BF16)


def call(kernel, out_shape, scratch=(), ins=1):
    vmem = pl.BlockSpec(memory_space=pltpu.VMEM)
    return pl.pallas_call(
        kernel,
        out_shape=out_shape,
        in_specs=[pl.BlockSpec(memory_space=pltpu.SMEM)] + [vmem] * ins,
        out_specs=jax.tree.map(
            lambda o: pl.BlockSpec(memory_space=pltpu.SMEM) if o.shape == (1, 1) else vmem, out_shape
        ),
        scratch_shapes=list(scratch),
        compiler_params=pltpu.CompilerParams(vmem_limit_bytes=24 * 2**20),
    )


def shape(*dims, dtype=BF16):
    return jax.ShapeDtypeStruct(dims, dtype)


def flip(x, axis, by):
    return lax.ppermute(x, axis, [(i, i ^ by) for i in range(lax.axis_size(axis))])


def state_over_groups(msg, d, wk_pair, group, groups, members):
    if groups == 2:
        return flip(msg, "ctx", QUAD)
    every = lax.all_gather(msg, "ctx", axis_index_groups=members)
    k, v = every[:, :, d + 16 : d + 16 + WIN], every[:, :, d + 16 + WIN :]
    proj = jnp.einsum("gptd,pfd->gptf", k, wk_pair, preferred_element_type=F32)
    feat = jnp.concatenate([jax.nn.softmax(proj, axis=-1), jax.nn.softmax(-proj, axis=-1)], axis=-1)
    tail = jnp.einsum("gptd,gptf->gpdf", v.astype(F32), feat, precision=lax.Precision.HIGHEST)
    place = jnp.arange(groups)[:, None, None, None]
    norm = jnp.sum(feat, axis=2)[:, :, None, :]
    tail = jnp.concatenate([tail, jnp.pad(norm, ((0, 0), (0, 0), (0, 15), (0, 0)))], axis=2)
    state = jnp.sum(jnp.where(place < group, every[:, :, : d + 16].astype(F32), 0.0), axis=0)
    state = state + jnp.sum(jnp.where(place < group - 1, tail, 0.0), axis=0)
    halo = lax.dynamic_index_in_dim(every, jnp.maximum(group - 1, 0), 0, keepdims=False)
    return jnp.concatenate([state.astype(BF16), halo[:, d + 16 :]], axis=1)


def later_over_groups(later, group, groups, members):
    if groups == 2:
        return flip(later, "ctx", QUAD)
    every = lax.all_gather(later, "ctx", axis_index_groups=members).astype(F32)
    place = jnp.arange(groups)[:, None, None, None]
    return jnp.sum(jnp.where(place > group, every, 0.0), axis=0).astype(BF16)


def sum_over_groups(part, groups, members):
    if groups == 2:
        return [part, flip(part, "ctx", QUAD)]
    every = lax.all_gather(part, "ctx", axis_index_groups=members)
    return [every[g] for g in range(groups)]


def per_device(queries, keys, values, teacher, wq, wk):
    tok, heads, d = queries.shape
    half = wq.shape[1]
    per = heads // QUAD
    place = lax.axis_index("ctx")
    shards = lax.axis_size("ctx")
    groups = shards // QUAD
    members = [[g * QUAD + p for g in range(groups)] for p in range(QUAD)]
    mine, group = place % QUAD, place // QUAD
    where = jnp.stack([mine, group, (group < groups - 1).astype(jnp.int32)]).astype(jnp.int32)

    block = shape(2, per, tok, d)
    pack = call(
        pack_kernel, [block] * QUAD,
        [pltpu.VMEM((tok * heads, d), F32), pltpu.VMEM((QUAD, 2, per, tok, d), BF16)], ins=2,
    )
    kv = pack(where, keys, values)
    kv = [kv[0]] + [flip(kv[j], "ctx", j) for j in range(1, QUAD)]
    qt = pack(where, queries, teacher)
    qt = [qt[0]] + [flip(qt[j], "ctx", j) for j in range(1, QUAD)]

    rows = d + 16 + 2 * WIN
    kv, msg = call(key_kernel, [shape(2, per, QUAD, tok, d), shape(per, rows, d)], ins=5)(where, *kv, wk)
    wk_pair = lax.dynamic_slice_in_dim(wk, per * mine, per, 0) if groups != 2 else None
    msg = state_over_groups(msg, d, wk_pair, group, groups, members)

    grad = shape(per, half, d, dtype=F32)
    out = shape(per, tok, d)
    *out, later, gq, gk, loss = call(
        main_kernel,
        [out] * QUAD + [shape(per, d + 16, 2 * half), grad, grad, shape(8, tok, dtype=F32)],
        [
            pltpu.VMEM((2, per, QUAD, tok, d), BF16),
            pltpu.VMEM((QUAD, per, tok, d), BF16),
            pltpu.VMEM((2 * half, (QUAD + 1) * tok), F32),
        ],
        ins=8,
    )(where, kv, *qt, msg, wq, wk)
    later = later_over_groups(later, group, groups, members)
    losses = [loss] + [flip(loss, "head", j) for j in range(1, lax.axis_size("head"))]
    rows = 2 * per * half + 16
    grads = call(last_kernel, shape(rows, d), ins=10)(where, kv, msg, later, wk, gq, gk, *losses)
    grads = sum_over_groups(grads, groups, members)
    grads = call(sum_kernel, shape(rows, d), ins=len(grads))(where, *grads)
    grads = [grads] + [flip(grads, "ctx", j) for j in range(1, QUAD)]
    out = [out[0]] + [flip(out[j], "ctx", j) for j in range(1, QUAD)]
    entries = tok * shards * heads * lax.axis_size("head") * d
    student, loss, grad_q, grad_k = call(
        functools.partial(finish_kernel, entries),
        [shape(tok, heads, d), shape(1, 1, dtype=F32), shape(heads, half, d, dtype=F32), shape(heads, half, d, dtype=F32)],
        [pltpu.VMEM((QUAD, per, tok, d), BF16), pltpu.VMEM((tok * heads, d), F32)],
        ins=8,
    )(where, *grads, *out)
    return student, loss.reshape(()), grad_q, grad_k


def solution(mesh):
    wide = P("ctx", "head", None)
    narrow = P("head", None, None)
    return jax.shard_map(
        per_device,
        mesh=mesh,
        in_specs=(wide, wide, wide, wide, narrow, narrow),
        out_specs=(wide, P(), narrow, narrow),
        check_vma=False,
    )
```

time: 265 us -> 62.2 us (0.23)
  blocking collectives: 85.9 us -> 0 us
  waiting for transfers between devices: 100 us -> 22.2 us
  other arithmetic: 26.4 us -> 0.08 us
  matrix products: 22.2 us -> 0 us
  starting transfers between devices: 5.01 us -> 22.9 us
  between operations: 16.1 us -> 0.72 us
  Pallas kernels: 0 us -> 14.2 us
  local copies, waits for them, and re-layouts: 7.47 us -> 1.92 us
    all_gather x2 -> x0, blocking collectives: 60.1 us -> none  [the longest x1 33 us: carried_in(): pieces = jax.tree.map(lambda part: lax.all_gather(part, axis), value)]
    all_gather x2 -> x0, waiting for transfers between devices: 51.1 us -> none  [the longest x1 38.2 us: carried_in(): pieces = jax.tree.map(lambda part: lax.all_gather(part, axis), value)]
    psum x1 -> x0, waiting for transfers between devices: 43.8 us -> none  [per_device(): grad_q, grad_k, partial_value = lax.psum((grad_q, grad_k, squared), 'ctx')]
    psum x2 -> x0, blocking collectives: 25.8 us -> none  [the longest x1 19.5 us: per_device(): grad_q, grad_k, partial_value = lax.psum((grad_q, grad_k, squared), 'ctx')]
    select_n x30 -> x0, other arithmetic: 24.1 us -> none  [the longest x16 15.4 us: hop(): return jax.tree.map(lambda a, b: jnp.where(reached, a, b), new, before)]
    dot_general x16 -> x0, matrix products: 18 us -> none  [the longest x1 3.42 us: per_device(): win_num = jnp.einsum('hic,chd->ihd', weight, val_all, precision=high)]
    ppermute x1 -> x18, starting transfers between devices: 4.89 us -> 22.9 us  [flip(): lax.ppermute(x, axis, [(i, i ^ by) for i in range(lax.axis_size(axis))])]
    ppermute x1 -> x18, waiting for transfers between devices: 5.49 us -> 22.2 us  [flip(): lax.ppermute(x, axis, [(i, i ^ by) for i in range(lax.axis_size(axis))])]
  transfers between devices with their start and end apart: 4 -> 18, of which waited for: 4 -> 12; matrix products, arithmetic and copies ran while one was open for 5% -> 0% of each run, Pallas kernels for 0% -> 2%
where the time goes in v1:
time: 62.2 us; the launch traced here: 62 us
  starting transfers between devices  22.9 us (37%)
  waiting for transfers between devices  22.2 us (36%)
  Pallas kernels  14.2 us (23%)
  local copies, waits for them, and re-layouts  1.92 us (3%)
  between operations  0.72 us (1%)
    ppermute x18, starting transfers between devices, flip(): lax.ppermute(x, axis, [(i, i ^ by) for i in range(lax.axis_size(axis))])  22.9 us
    ppermute x18, waiting for transfers between devices, flip(): lax.ppermute(x, axis, [(i, i ^ by) for i in range(lax.axis_size(axis))])  22.2 us
    pallas_call x1, Pallas kernels, per_device(): call(main_kernel, [out] * QUAD + [shape(per, d + 16, 2 * half), grad, gra...  7.95 us
    unnamed x12, local copies, waits for them, and re-layouts  1.92 us
    pallas_call x1, Pallas kernels, per_device(): call(functools.partial(finish_kernel, entries), [shape(tok, heads, d), sh...  1.47 us
    pallas_call x1, Pallas kernels, per_device(): call(last_kernel, shape(rows, d), ins=10)  1.38 us
  transfers between devices with their start and end apart: 18, of which 12 were waited for; matrix products, arithmetic and copies ran while one was open for 0% of the time, Pallas kernels for 2%

profile of v1, /device:TPU:0, one launch (start us, length us, event | category | flops | bytes accessed | tf_op | source)
XLA Modules:
  0.0 62.0 jit_solution(3148206205478089485)
XLA Ops:
  0.7 0.1 pad_add_fusion.where
  0.7 0.0 copy-start.1
  0.7 0.9 %copy-done.1 = bf16[128,8,128]{2,1,0:T(8,128)(2,1)S(1)} copy-done((bf16[128,8,128]{2,1,0:T(8,128)(2,1)S(1)}, bf16[128,8,128]{2,1,0:T(8,128)(2,1)}, u32[]{:S(2)}) %copy-start.1) | copy-done | bytes 262168
  1.7 0.0 copy-start.2
  1.7 0.9 %copy-done.2 = bf16[128,8,128]{2,1,0:T(8,128)(2,1)S(1)} copy-done((bf16[128,8,128]{2,1,0:T(8,128)(2,1)S(1)}, bf16[128,8,128]{2,1,0:T(8,128)(2,1)}, u32[]{:S(2)}) %copy-start.2) | copy-done | bytes 262168
  2.6 0.0 copy-start
  2.6 0.8 %shard_map.93 = (bf16[2,2,128,128]{3,2,1,0:T(8,128)(2,1)S(1)}, bf16[2,2,128,128]{3,2,1,0:T(8,128)(2,1)S(1)}, bf16[2,2,128,128]{3,2,1,0:T(8,128)(2,1)S(1)}, bf16[2,2,128,128]{3,2,1,0:T(8,128)(2,1)S(1)}) custom-call(s32[3]{0:T(128)S(1)} %pad_add_fusion.where, bf16[128,8,128]{2,1,0:T(8,128)(2,1)S(1)} %copy-done.1, bf16[128,8,128]{2,1,0:T(8,128)(2,1)S(1)} %copy-done.2), custom_call_target="tpu_custom_call" | custom-call | tf_op jit(solution)/shard_map/pallas_call | solution.py:309
  3.4 3.0 %collective-permute-start = (bf16[2,2,128,128]{3,2,1,0:T(8,128)(2,1)S(1)}, bf16[2,2,128,128]{3,2,1,0:T(8,128)(2,1)S(1)}, u32[]{:S(2)}, u32[]{:S(2)}) collective-permute-start(bf16[2,2,128,128]{3,2,1,0:T(8,128)(2,1)S(1)} %get-tuple-element.27), channel_id=1, source_target_pairs={{0,4},{4,0},{8,12},{12,8},{16,20},{20,16},{24,28},{28,24},{1,5},{5... | collective-permute-start | bytes 393224 | tf_op jit(solution)/shard_map/ppermute | solution.py:258
  6.5 1.6 %collective-permute-start.1 = (bf16[2,2,128,128]{3,2,1,0:T(8,128)(2,1)S(1)}, bf16[2,2,128,128]{3,2,1,0:T(8,128)(2,1)S(1)}, u32[]{:S(2)}, u32[]{:S(2)}) collective-permute-start(bf16[2,2,128,128]{3,2,1,0:T(8,128)(2,1)S(1)} %get-tuple-element.28), channel_id=1, source_target_pairs={{0,8},{4,12},{8,0},{12,4},{16,24},{20,28},{24,16},{28,20},{1,9},{5... | collective-permute-start | bytes 393224 | tf_op jit(solution)/shard_map/ppermute | solution.py:258
  8.1 0.0 collective-permute-start.2
  8.1 1.9 %collective-permute-done.c1 = bf16[2,2,128,128]{3,2,1,0:T(8,128)(2,1)S(1)} collective-permute-done((bf16[2,2,128,128]{3,2,1,0:T(8,128)(2,1)S(1)}, bf16[2,2,128,128]{3,2,1,0:T(8,128)(2,1)S(1)}, u32[]{:S(2)}, u32[]{:S(2)}) %collective-permute-start) | collective-permute-done | bytes 131104 | tf_op jit(solution)/shard_map/ppermute | solution.py:258
  10.0 2.9 %collective-permute-done.1.c2 = bf16[2,2,128,128]{3,2,1,0:T(8,128)(2,1)S(1)} collective-permute-done((bf16[2,2,128,128]{3,2,1,0:T(8,128)(2,1)S(1)}, bf16[2,2,128,128]{3,2,1,0:T(8,128)(2,1)S(1)}, u32[]{:S(2)}, u32[]{:S(2)}) %collective-permute-start.1) | collective-permute-done | bytes 131104 | tf_op jit(solution)/shard_map/ppermute | solution.py:258
  12.8 1.2 %collective-permute-done.2.c3 = bf16[2,2,128,128]{3,2,1,0:T(8,128)(2,1)S(1)} collective-permute-done((bf16[2,2,128,128]{3,2,1,0:T(8,128)(2,1)S(1)}, bf16[2,2,128,128]{3,2,1,0:T(8,128)(2,1)S(1)}, u32[]{:S(2)}, u32[]{:S(2)}) %collective-permute-start.2) | collective-permute-done | bytes 131104 | tf_op jit(solution)/shard_map/ppermute | solution.py:258
  14.0 0.0 copy-done
  14.0 0.0 copy-start.3
  14.0 0.0 copy-start.4
  14.0 1.2 %shard_map.94 = (bf16[2,2,4,128,128]{4,3,2,1,0:T(8,128)(2,1)S(1)}, bf16[2,272,128]{2,1,0:T(8,128)(2,1)S(1)}) custom-call(s32[3]{0:T(128)S(1)} %pad_add_fusion.where, bf16[2,2,128,128]{3,2,1,0:T(8,128)(2,1)S(1)} %get-tuple-element.26.c0, bf16[2,2,128,128]{3,2,1,0:T(8,128)(2,1)S(1)} %collective-permute-done.c1, ...), custom_call_target="tpu_custom_call" | custom-call | tf_op jit(solution)/shard_map/pallas_call | solution.py:315
  15.2 0.0 copy-start.5
  15.3 2.8 %collective-permute-start.3 = (bf16[2,272,128]{2,1,0:T(8,128)(2,1)S(1)}, bf16[2,272,128]{2,1,0:T(8,128)(2,1)S(1)}, u32[]{:S(2)}, u32[]{:S(2)}) collective-permute-start(bf16[2,272,128]{2,1,0:T(8,128)(2,1)S(1)} %get-tuple-element.31), channel_id=1, source_target_pairs={{0,16},{4,20},{8,24},{12,28},{16,0},{20,4},{24,8},{28,12},{1,17},{... | collective-permute-start | bytes 417800 | tf_op jit(solution)/shard_map/ppermute | solution.py:258
  18.1 0.0 copy-done.3
  18.1 0.0 copy-done.4
  18.1 0.8 %shard_map.95 = (bf16[2,2,128,128]{3,2,1,0:T(8,128)(2,1)S(1)}, bf16[2,2,128,128]{3,2,1,0:T(8,128)(2,1)S(1)}, bf16[2,2,128,128]{3,2,1,0:T(8,128)(2,1)S(1)}, bf16[2,2,128,128]{3,2,1,0:T(8,128)(2,1)S(1)}) custom-call(s32[3]{0:T(128)S(1)} %pad_add_fusion.where, bf16[128,8,128]{2,1,0:T(8,128)(2,1)S(1)} %copy-done.3, bf16[128,8,128]{2,1,0:T(8,128)(2,1)S(1)} %copy-done.4), custom_call_target="tpu_custom_call" | custom-call | tf_op jit(solution)/shard_map/pallas_call | solution.py:311
  18.9 1.6 %collective-permute-start.4 = (bf16[2,2,128,128]{3,2,1,0:T(8,128)(2,1)S(1)}, bf16[2,2,128,128]{3,2,1,0:T(8,128)(2,1)S(1)}, u32[]{:S(2)}, u32[]{:S(2)}) collective-permute-start(bf16[2,2,128,128]{3,2,1,0:T(8,128)(2,1)S(1)} %get-tuple-element.33), channel_id=1, source_target_pairs={{0,4},{4,0},{8,12},{12,8},{16,20},{20,16},{24,28},{28,24},{1,5},{5... | collective-permute-start | bytes 393224 | tf_op jit(solution)/shard_map/ppermute | solution.py:258
  20.5 1.6 %collective-permute-start.5 = (bf16[2,2,128,128]{3,2,1,0:T(8,128)(2,1)S(1)}, bf16[2,2,128,128]{3,2,1,0:T(8,128)(2,1)S(1)}, u32[]{:S(2)}, u32[]{:S(2)}) collective-permute-start(bf16[2,2,128,128]{3,2,1,0:T(8,128)(2,1)S(1)} %get-tuple-element.34), channel_id=1, source_target_pairs={{0,8},{4,12},{8,0},{12,4},{16,24},{20,28},{24,16},{28,20},{1,9},{5... | collective-permute-start | bytes 393224 | tf_op jit(solution)/shard_map/ppermute | solution.py:258
  22.0 0.4 collective-permute-start.6
  22.4 1.5 %collective-permute-done.4.c1 = bf16[2,2,128,128]{3,2,1,0:T(8,128)(2,1)S(1)} collective-permute-done((bf16[2,2,128,128]{3,2,1,0:T(8,128)(2,1)S(1)}, bf16[2,2,128,128]{3,2,1,0:T(8,128)(2,1)S(1)}, u32[]{:S(2)}, u32[]{:S(2)}) %collective-permute-start.4) | collective-permute-done | bytes 131104 | tf_op jit(solution)/shard_map/ppermute | solution.py:258
  23.9 2.6 %collective-permute-done.5.c2 = bf16[2,2,128,128]{3,2,1,0:T(8,128)(2,1)S(1)} collective-permute-done((bf16[2,2,128,128]{3,2,1,0:T(8,128)(2,1)S(1)}, bf16[2,2,128,128]{3,2,1,0:T(8,128)(2,1)S(1)}, u32[]{:S(2)}, u32[]{:S(2)}) %collective-permute-start.5) | collective-permute-done | bytes 131104 | tf_op jit(solution)/shard_map/ppermute | solution.py:258
  26.5 1.8 %collective-permute-done.6.c3 = bf16[2,2,128,128]{3,2,1,0:T(8,128)(2,1)S(1)} collective-permute-done((bf16[2,2,128,128]{3,2,1,0:T(8,128)(2,1)S(1)}, bf16[2,2,128,128]{3,2,1,0:T(8,128)(2,1)S(1)}, u32[]{:S(2)}, u32[]{:S(2)}) %collective-permute-start.6) | collective-permute-done | bytes 131104 | tf_op jit(solution)/shard_map/ppermute | solution.py:258
  28.4 0.0 collective-permute-done.3.msg_ref
  28.4 0.0 copy-done.5
  28.4 8.0 %shard_map.96 = (bf16[2,128,128]{2,1,0:T(8,128)(2,1)S(1)}, bf16[2,128,128]{2,1,0:T(8,128)(2,1)S(1)}, bf16[2,128,128]{2,1,0:T(8,128)(2,1)S(1)}, bf16[2,128,128]{2...) custom-call(s32[3]{0:T(128)S(1)} %pad_add_fusion.where, ...), custom_call_target="tpu_custom_call" | custom-call | tf_op jit(solution)/shard_map/pallas_call | solution.py:321
  36.3 0.5 collective-permute-start.7
  36.8 0.0 collective-permute-start.10
  36.8 1.6 %collective-permute-start.8 = (f32[8,128]{1,0:T(8,128)S(1)}, f32[8,128]{1,0:T(8,128)S(1)}, u32[]{:S(2)}, u32[]{:S(2)}) collective-permute-start(f32[8,128]{1,0:T(8,128)S(1)} %get-tuple-element.39.l0), channel_id=1, source_target_pairs={{0,1},{1,0},{2,3},{3,2},{4,5},{5,4},{6,7},{7,6},{8,9},{9,8},{10,11... | collective-permute-start | bytes 12296 | tf_op jit(solution)/shard_map/ppermute | solution.py:258
  38.5 0.5 collective-permute-start.9
  39.0 0.9 %collective-permute-done.10.l3 = f32[8,128]{1,0:T(8,128)S(1)} collective-permute-done((f32[8,128]{1,0:T(8,128)S(1)}, f32[8,128]{1,0:T(8,128)S(1)}, u32[]{:S(2)}, u32[]{:S(2)}) %collective-permute-start.10) | collective-permute-done | bytes 4128 | tf_op jit(solution)/shard_map/ppermute | solution.py:258
  39.9 0.0 collective-permute-done.8.l1
  39.9 2.2 %collective-permute-done.9.l2 = f32[8,128]{1,0:T(8,128)S(1)} collective-permute-done((f32[8,128]{1,0:T(8,128)S(1)}, f32[8,128]{1,0:T(8,128)S(1)}, u32[]{:S(2)}, u32[]{:S(2)}) %collective-permute-start.9) | collective-permute-done | bytes 4128 | tf_op jit(solution)/shard_map/ppermute | solution.py:258
  42.1 0.4 collective-permute-done.7.later_ref
  42.4 1.4 %shard_map.97.refs_0_ = bf16[272,128]{1,0:T(8,128)(2,1)S(1)} custom-call(s32[3]{0:T(128)S(1)} %pad_add_fusion.where, bf16[2,2,4,128,128]{4,3,2,1,0:T(8,128)(2,1)S(1)} %get-tuple-element.30.kv_ref, bf16[2,272,128]{2,1,0:T(8,128)(2,1)S(1)} %collective-permute-done.3.msg_ref, bf16[2,144,128]{2,1,0:T(8,128)(2,1)S(1)} %collective-permute-done.7.later_ref, ...), custom_call_target="tpu_custom_call" | custom-call | tf_op jit(solution)/shard_map/pallas_call | solution.py:334
  43.8 2.2 %collective-permute-start.11 = (bf16[272,128]{1,0:T(8,128)(2,1)S(1)}, bf16[272,128]{1,0:T(8,128)(2,1)S(1)}, u32[]{:S(2)}, u32[]{:S(2)}) collective-permute-start(bf16[272,128]{1,0:T(8,128)(2,1)S(1)} %shard_map.97.refs_0_), channel_id=1, source_target_pairs={{0,16},{4,20},{8,24},{12,28},{16,0},{20,4},{24,8},{28,12},{1,17},{... | collective-permute-start | bytes 208904 | tf_op jit(solution)/shard_map/ppermute | solution.py:258
  46.0 1.1 %collective-permute-start.15 = (bf16[2,128,128]{2,1,0:T(8,128)(2,1)S(1)}, bf16[2,128,128]{2,1,0:T(8,128)(2,1)S(1)}, u32[]{:S(2)}, u32[]{:S(2)}) collective-permute-start(bf16[2,128,128]{2,1,0:T(8,128)(2,1)S(1)} %get-tuple-element.41), channel_id=1, source_target_pairs={{0,4},{4,0},{8,12},{12,8},{16,20},{20,16},{24,28},{28,24},{1,5},{5... | collective-permute-start | bytes 196616 | tf_op jit(solution)/shard_map/ppermute | solution.py:258
  47.1 2.2 %collective-permute-done.11.refs_1_ = bf16[272,128]{1,0:T(8,128)(2,1)S(1)} collective-permute-done((bf16[272,128]{1,0:T(8,128)(2,1)S(1)}, bf16[272,128]{1,0:T(8,128)(2,1)S(1)}, u32[]{:S(2)}, u32[]{:S(2)}) %collective-permute-start.11) | collective-permute-done | bytes 69664 | tf_op jit(solution)/shard_map/ppermute | solution.py:258
  49.3 0.6 shard_map.98.g0
  49.8 1.0 %collective-permute-start.12 = (bf16[272,128]{1,0:T(8,128)(2,1)S(1)}, bf16[272,128]{1,0:T(8,128)(2,1)S(1)}, u32[]{:S(2)}, u32[]{:S(2)}) collective-permute-start(bf16[272,128]{1,0:T(8,128)(2,1)S(1)} %shard_map.98.g0), channel_id=1, source_target_pairs={{0,4},{4,0},{8,12},{12,8},{16,20},{20,16},{24,28},{28,24},{1,5},{5... | collective-permute-start | bytes 208904 | tf_op jit(solution)/shard_map/ppermute | solution.py:258
  50.9 1.9 %collective-permute-start.13 = (bf16[272,128]{1,0:T(8,128)(2,1)S(1)}, bf16[272,128]{1,0:T(8,128)(2,1)S(1)}, u32[]{:S(2)}, u32[]{:S(2)}) collective-permute-start(bf16[272,128]{1,0:T(8,128)(2,1)S(1)} %shard_map.98.g0), channel_id=1, source_target_pairs={{0,8},{4,12},{8,0},{12,4},{16,24},{20,28},{24,16},{28,20},{1,9},{5... | collective-permute-start | bytes 208904 | tf_op jit(solution)/shard_map/ppermute | solution.py:258
  52.8 0.6 collective-permute-start.14
  53.4 1.9 %collective-permute-start.16 = (bf16[2,128,128]{2,1,0:T(8,128)(2,1)S(1)}, bf16[2,128,128]{2,1,0:T(8,128)(2,1)S(1)}, u32[]{:S(2)}, u32[]{:S(2)}) collective-permute-start(bf16[2,128,128]{2,1,0:T(8,128)(2,1)S(1)} %get-tuple-element.42), channel_id=1, source_target_pairs={{0,8},{4,12},{8,0},{12,4},{16,24},{20,28},{24,16},{28,20},{1,9},{5... | collective-permute-start | bytes 196616 | tf_op jit(solution)/shard_map/ppermute | solution.py:258
  55.3 0.0 collective-permute-done.15.s1
  55.3 0.5 collective-permute-start.17
  55.8 2.5 %collective-permute-done.16.s2 = bf16[2,128,128]{2,1,0:T(8,128)(2,1)S(1)} collective-permute-done((bf16[2,128,128]{2,1,0:T(8,128)(2,1)S(1)}, bf16[2,128,128]{2,1,0:T(8,128)(2,1)S(1)}, u32[]{:S(2)}, u32[]{:S(2)}) %collective-permute-start.16) | collective-permute-done | bytes 65568 | tf_op jit(solution)/shard_map/ppermute | solution.py:258
  58.3 2.2 %collective-permute-done.17.s3 = bf16[2,128,128]{2,1,0:T(8,128)(2,1)S(1)} collective-permute-done((bf16[2,128,128]{2,1,0:T(8,128)(2,1)S(1)}, bf16[2,128,128]{2,1,0:T(8,128)(2,1)S(1)}, u32[]{:S(2)}, u32[]{:S(2)}) %collective-permute-start.17) | collective-permute-done | bytes 65568 | tf_op jit(solution)/shard_map/ppermute | solution.py:258
  60.5 0.0 collective-permute-done.12.g1
  60.5 0.0 collective-permute-done.13.g2
  60.5 0.0 collective-permute-done.14.g3
  60.5 1.5 %shard_map.99 = (bf16[128,8,128]{2,1,0:T(8,128)(2,1)}, f32[1,1]{1,0:T(1,128)}, f32[8,64,128]{2,1,0:T(8,128)}, f32[8,64,128]{2,1,0:T(8,128)}) custom-call(s32[3]{0:T(128)S(1)} %pad_add_fusion.where, bf16[272,128]{1,0:T(8,128)(2,1)S(1)} %shard_map.98.g0, bf16[272,128]{1,0:T(8,128)(2,1)S(1)} %collective-permute-done.12.g1, ...), custom_call_target="tpu_custom_call" | custom-call | tf_op jit(solution)/shard_map/pallas_call | solution.py:340
Async XLA Ops:
  0.7 1.0 %copy-start.1 = (bf16[128,8,128]{2,1,0:T(8,128)(2,1)S(1)}, bf16[128,8,128]{2,1,0:T(8,128)(2,1)}, u32[]{:S(2)}) copy-start(bf16[128,8,128]{2,1,0:T(8,128)(2,1)} %refs_0_.2) | copy-start | bytes 786436
  1.7 0.9 %copy-start.2 = (bf16[128,8,128]{2,1,0:T(8,128)(2,1)S(1)}, bf16[128,8,128]{2,1,0:T(8,128)(2,1)}, u32[]{:S(2)}) copy-start(bf16[128,8,128]{2,1,0:T(8,128)(2,1)} %refs_1_.2) | copy-start | bytes 786436
  2.6 11.4 %copy-start = (bf16[8,64,128]{2,1,0:T(8,128)(2,1)S(1)}, bf16[8,64,128]{2,1,0:T(8,128)(2,1)}, u32[]{:S(2)}) copy-start(bf16[8,64,128]{2,1,0:T(8,128)(2,1)} %wk_ref.5) | copy-start | bytes 393220
  3.4 6.5 %collective-permute-start = (bf16[2,2,128,128]{3,2,1,0:T(8,128)(2,1)S(1)}, bf16[2,2,128,128]{3,2,1,0:T(8,128)(2,1)S(1)}, u32[]{:S(2)}, u32[]{:S(2)}) collective-permute-start(bf16[2,2,128,128]{3,2,1,0:T(8,128)(2,1)S(1)} %get-tuple-element.27), channel_id=1, source_target_pairs={{0,4},{4,0},{8,12},{12,8},{16,20},{20,16},{24,28},{28,24},{1,5},{5... | collective-permute-start | bytes 393224 | tf_op jit(solution)/shard_map/ppermute | solution.py:258
  6.5 6.4 %collective-permute-start.1 = (bf16[2,2,128,128]{3,2,1,0:T(8,128)(2,1)S(1)}, bf16[2,2,128,128]{3,2,1,0:T(8,128)(2,1)S(1)}, u32[]{:S(2)}, u32[]{:S(2)}) collective-permute-start(bf16[2,2,128,128]{3,2,1,0:T(8,128)(2,1)S(1)} %get-tuple-element.28), channel_id=1, source_target_pairs={{0,8},{4,12},{8,0},{12,4},{16,24},{20,28},{24,16},{28,20},{1,9},{5... | collective-permute-start | bytes 393224 | tf_op jit(solution)/shard_map/ppermute | solution.py:258
  8.1 6.0 %collective-permute-start.2 = (bf16[2,2,128,128]{3,2,1,0:T(8,128)(2,1)S(1)}, bf16[2,2,128,128]{3,2,1,0:T(8,128)(2,1)S(1)}, u32[]{:S(2)}, u32[]{:S(2)}) collective-permute-start(bf16[2,2,128,128]{3,2,1,0:T(8,128)(2,1)S(1)} %get-tuple-element.29), channel_id=1, source_target_pairs={{0,12},{4,8},{8,4},{12,0},{16,28},{20,24},{24,20},{28,16},{1,13},{... | collective-permute-start | bytes 393224 | tf_op jit(solution)/shard_map/ppermute | solution.py:258
  14.0 4.0 %copy-start.3 = (bf16[128,8,128]{2,1,0:T(8,128)(2,1)S(1)}, bf16[128,8,128]{2,1,0:T(8,128)(2,1)}, u32[]{:S(2)}) copy-start(bf16[128,8,128]{2,1,0:T(8,128)(2,1)} %refs_0_.3) | copy-start | bytes 786436
  14.0 4.0 %copy-start.4 = (bf16[128,8,128]{2,1,0:T(8,128)(2,1)S(1)}, bf16[128,8,128]{2,1,0:T(8,128)(2,1)}, u32[]{:S(2)}) copy-start(bf16[128,8,128]{2,1,0:T(8,128)(2,1)} %refs_1_.3) | copy-start | bytes 786436
  15.2 13.1 %copy-start.5 = (bf16[8,64,128]{2,1,0:T(8,128)(2,1)S(1)}, bf16[8,64,128]{2,1,0:T(8,128)(2,1)}, u32[]{:S(2)}) copy-start(bf16[8,64,128]{2,1,0:T(8,128)(2,1)} %wq_ref.1) | copy-start | bytes 393220
  15.3 13.1 %collective-permute-start.3 = (bf16[2,272,128]{2,1,0:T(8,128)(2,1)S(1)}, bf16[2,272,128]{2,1,0:T(8,128)(2,1)S(1)}, u32[]{:S(2)}, u32[]{:S(2)}) collective-permute-start(bf16[2,272,128]{2,1,0:T(8,128)(2,1)S(1)} %get-tuple-element.31), channel_id=1, source_target_pairs={{0,16},{4,20},{8,24},{12,28},{16,0},{20,4},{24,8},{28,12},{1,17},{... | collective-permute-start | bytes 417800 | tf_op jit(solution)/shard_map/ppermute | solution.py:258
  18.9 5.0 %collective-permute-start.4 = (bf16[2,2,128,128]{3,2,1,0:T(8,128)(2,1)S(1)}, bf16[2,2,128,128]{3,2,1,0:T(8,128)(2,1)S(1)}, u32[]{:S(2)}, u32[]{:S(2)}) collective-permute-start(bf16[2,2,128,128]{3,2,1,0:T(8,128)(2,1)S(1)} %get-tuple-element.33), channel_id=1, source_target_pairs={{0,4},{4,0},{8,12},{12,8},{16,20},{20,16},{24,28},{28,24},{1,5},{5... | collective-permute-start | bytes 393224 | tf_op jit(solution)/shard_map/ppermute | solution.py:258
  20.5 6.1 %collective-permute-start.5 = (bf16[2,2,128,128]{3,2,1,0:T(8,128)(2,1)S(1)}, bf16[2,2,128,128]{3,2,1,0:T(8,128)(2,1)S(1)}, u32[]{:S(2)}, u32[]{:S(2)}) collective-permute-start(bf16[2,2,128,128]{3,2,1,0:T(8,128)(2,1)S(1)} %get-tuple-element.34), channel_id=1, source_target_pairs={{0,8},{4,12},{8,0},{12,4},{16,24},{20,28},{24,16},{28,20},{1,9},{5... | collective-permute-start | bytes 393224 | tf_op jit(solution)/shard_map/ppermute | solution.py:258
  22.0 6.3 %collective-permute-start.6 = (bf16[2,2,128,128]{3,2,1,0:T(8,128)(2,1)S(1)}, bf16[2,2,128,128]{3,2,1,0:T(8,128)(2,1)S(1)}, u32[]{:S(2)}, u32[]{:S(2)}) collective-permute-start(bf16[2,2,128,128]{3,2,1,0:T(8,128)(2,1)S(1)} %get-tuple-element.35), channel_id=1, source_target_pairs={{0,12},{4,8},{8,4},{12,0},{16,28},{20,24},{24,20},{28,16},{1,13},{... | collective-permute-start | bytes 393224 | tf_op jit(solution)/shard_map/ppermute | solution.py:258
  36.3 6.1 %collective-permute-start.7 = (bf16[2,144,128]{2,1,0:T(8,128)(2,1)S(1)}, bf16[2,144,128]{2,1,0:T(8,128)(2,1)S(1)}, u32[]{:S(2)}, u32[]{:S(2)}) collective-permute-start(bf16[2,144,128]{2,1,0:T(8,128)(2,1)S(1)} %get-tuple-element.36), channel_id=1, source_target_pairs={{0,16},{4,20},{8,24},{12,28},{16,0},{20,4},{24,8},{28,12},{1,17},{... | collective-permute-start | bytes 221192 | tf_op jit(solution)/shard_map/ppermute | solution.py:258
  36.8 3.0 %collective-permute-start.10 = (f32[8,128]{1,0:T(8,128)S(1)}, f32[8,128]{1,0:T(8,128)S(1)}, u32[]{:S(2)}, u32[]{:S(2)}) collective-permute-start(f32[8,128]{1,0:T(8,128)S(1)} %get-tuple-element.39.l0), channel_id=1, source_target_pairs={{0,3},{1,2},{2,1},{3,0},{4,7},{5,6},{6,5},{7,4},{8,11},{9,10},{10,... | collective-permute-start | bytes 12296 | tf_op jit(solution)/shard_map/ppermute | solution.py:258
  36.8 3.0 %collective-permute-start.8 = (f32[8,128]{1,0:T(8,128)S(1)}, f32[8,128]{1,0:T(8,128)S(1)}, u32[]{:S(2)}, u32[]{:S(2)}) collective-permute-start(f32[8,128]{1,0:T(8,128)S(1)} %get-tuple-element.39.l0), channel_id=1, source_target_pairs={{0,1},{1,0},{2,3},{3,2},{4,5},{5,4},{6,7},{7,6},{8,9},{9,8},{10,11... | collective-permute-start | bytes 12296 | tf_op jit(solution)/shard_map/ppermute | solution.py:258
  38.5 3.6 %collective-permute-start.9 = (f32[8,128]{1,0:T(8,128)S(1)}, f32[8,128]{1,0:T(8,128)S(1)}, u32[]{:S(2)}, u32[]{:S(2)}) collective-permute-start(f32[8,128]{1,0:T(8,128)S(1)} %get-tuple-element.39.l0), channel_id=1, source_target_pairs={{0,2},{1,3},{2,0},{3,1},{4,6},{5,7},{6,4},{7,5},{8,10},{9,11},{10,... | collective-permute-start | bytes 12296 | tf_op jit(solution)/shard_map/ppermute | solution.py:258
  43.8 5.4 %collective-permute-start.11 = (bf16[272,128]{1,0:T(8,128)(2,1)S(1)}, bf16[272,128]{1,0:T(8,128)(2,1)S(1)}, u32[]{:S(2)}, u32[]{:S(2)}) collective-permute-start(bf16[272,128]{1,0:T(8,128)(2,1)S(1)} %shard_map.97.refs_0_), channel_id=1, source_target_pairs={{0,16},{4,20},{8,24},{12,28},{16,0},{20,4},{24,8},{28,12},{1,17},{... | collective-permute-start | bytes 208904 | tf_op jit(solution)/shard_map/ppermute | solution.py:258
  46.0 9.3 %collective-permute-start.15 = (bf16[2,128,128]{2,1,0:T(8,128)(2,1)S(1)}, bf16[2,128,128]{2,1,0:T(8,128)(2,1)S(1)}, u32[]{:S(2)}, u32[]{:S(2)}) collective-permute-start(bf16[2,128,128]{2,1,0:T(8,128)(2,1)S(1)} %get-tuple-element.41), channel_id=1, source_target_pairs={{0,4},{4,0},{8,12},{12,8},{16,20},{20,16},{24,28},{28,24},{1,5},{5... | collective-permute-start | bytes 196616 | tf_op jit(solution)/shard_map/ppermute | solution.py:258
  49.8 10.7 %collective-permute-start.12 = (bf16[272,128]{1,0:T(8,128)(2,1)S(1)}, bf16[272,128]{1,0:T(8,128)(2,1)S(1)}, u32[]{:S(2)}, u32[]{:S(2)}) collective-permute-start(bf16[272,128]{1,0:T(8,128)(2,1)S(1)} %shard_map.98.g0), channel_id=1, source_target_pairs={{0,4},{4,0},{8,12},{12,8},{16,20},{20,16},{24,28},{28,24},{1,5},{5... | collective-permute-start | bytes 208904 | tf_op jit(solution)/shard_map/ppermute | solution.py:258
  50.9 9.6 %collective-permute-start.13 = (bf16[272,128]{1,0:T(8,128)(2,1)S(1)}, bf16[272,128]{1,0:T(8,128)(2,1)S(1)}, u32[]{:S(2)}, u32[]{:S(2)}) collective-permute-start(bf16[272,128]{1,0:T(8,128)(2,1)S(1)} %shard_map.98.g0), channel_id=1, source_target_pairs={{0,8},{4,12},{8,0},{12,4},{16,24},{20,28},{24,16},{28,20},{1,9},{5... | collective-permute-start | bytes 208904 | tf_op jit(solution)/shard_map/ppermute | solution.py:258
  52.8 7.7 %collective-permute-start.14 = (bf16[272,128]{1,0:T(8,128)(2,1)S(1)}, bf16[272,128]{1,0:T(8,128)(2,1)S(1)}, u32[]{:S(2)}, u32[]{:S(2)}) collective-permute-start(bf16[272,128]{1,0:T(8,128)(2,1)S(1)} %shard_map.98.g0), channel_id=1, source_target_pairs={{0,12},{4,8},{8,4},{12,0},{16,28},{20,24},{24,20},{28,16},{1,13},{... | collective-permute-start | bytes 208904 | tf_op jit(solution)/shard_map/ppermute | solution.py:258
  53.4 4.9 %collective-permute-start.16 = (bf16[2,128,128]{2,1,0:T(8,128)(2,1)S(1)}, bf16[2,128,128]{2,1,0:T(8,128)(2,1)S(1)}, u32[]{:S(2)}, u32[]{:S(2)}) collective-permute-start(bf16[2,128,128]{2,1,0:T(8,128)(2,1)S(1)} %get-tuple-element.42), channel_id=1, source_target_pairs={{0,8},{4,12},{8,0},{12,4},{16,24},{20,28},{24,16},{28,20},{1,9},{5... | collective-permute-start | bytes 196616 | tf_op jit(solution)/shard_map/ppermute | solution.py:258
  55.3 5.2 %collective-permute-start.17 = (bf16[2,128,128]{2,1,0:T(8,128)(2,1)S(1)}, bf16[2,128,128]{2,1,0:T(8,128)(2,1)S(1)}, u32[]{:S(2)}, u32[]{:S(2)}) collective-permute-start(bf16[2,128,128]{2,1,0:T(8,128)(2,1)S(1)} %get-tuple-element.43), channel_id=1, source_target_pairs={{0,12},{4,8},{8,4},{12,0},{16,28},{20,24},{24,20},{28,16},{1,13},{... | collective-permute-start | bytes 196616 | tf_op jit(solution)/shard_map/ppermute | solution.py:258

commit v2 on v1

v2 whole, which is shorter than its diff:
```python
import functools

import jax
import jax.numpy as jnp
from jax import lax
from jax.experimental import pallas as pl
from jax.experimental.pallas import tpu as pltpu
from jax.sharding import PartitionSpec as P

WIN = 64
QUAD = 4
F32 = jnp.float32
BF16 = jnp.bfloat16
KEY_US, OWN_US, GRAD_US, STUDENT_US = 20.0, 20.0, 20.0, 20.0


def nt(a, b):
    return lax.dot_general(a, b, (((1,), (1,)), ((), ())), preferred_element_type=F32)


def nn(a, b):
    return lax.dot_general(a, b, (((1,), (0,)), ((), ())), preferred_element_type=F32)


def split2(a):
    high = a.astype(BF16)
    return high, (a - high.astype(F32)).astype(BF16)


def identity(n):
    return (
        lax.broadcasted_iota(jnp.int32, (n, n), 0) == lax.broadcasted_iota(jnp.int32, (n, n), 1)
    ).astype(BF16)


def phi_t(x, w):
    proj = nt(w, x)
    up = jnp.exp(proj - jnp.max(proj, axis=0, keepdims=True))
    down = jnp.exp(jnp.min(proj, axis=0, keepdims=True) - proj)
    up = up * (1.0 / jnp.sum(up, axis=0, keepdims=True))
    down = down * (1.0 / jnp.sum(down, axis=0, keepdims=True))
    return up, down


def phi_pull(up, down, grad):
    half = up.shape[0]
    g_up, g_down = grad[:half], grad[half:]
    d = up * (g_up - jnp.sum(up * g_up, axis=0, keepdims=True))
    return d - down * (g_down - jnp.sum(down * g_down, axis=0, keepdims=True))


def extended(vt):
    row = lax.broadcasted_iota(jnp.int32, (16, vt.shape[1]), 0)
    return jnp.concatenate([vt, (row == 0).astype(BF16)], axis=0)


def place_in_group():
    place = lax.axis_index("ctx")
    group = lax.div(place, QUAD)
    return lax.rem(place, QUAD), group > 0, group < lax.axis_size("ctx") // QUAD - 1


def transposed(x):
    return nt(identity(x.shape[1]), x)


def pack_kernel(*refs):
    (x_ref, y_ref), outs, (held_x, held_y, wide, held, sems) = refs[:2], refs[2:-5], refs[-5:]
    copies = [
        pltpu.make_async_copy(src, dst, sems.at[n])
        for n, (src, dst) in enumerate(((x_ref, held_x), (y_ref, held_y)))
    ]
    for copy in copies:
        copy.start()
    mine, _, _ = place_in_group()
    for a, (copy, ref) in enumerate(zip(copies, (held_x, held_y))):
        copy.wait()
        tok, heads, d = ref.shape
        per = heads // QUAD
        wide[a] = ref[...].astype(F32).reshape(tok * heads, d)
        for h in range(heads):
            held[h // per, a, h % per] = wide[a, pl.ds(h, tok, stride=heads), :].astype(BF16)
    for j, out in enumerate(outs):
        out[...] = held[lax.bitwise_xor(mine, j)]


def key_kernel(c0, c1, c2, c3, wk_ref, kv_ref, msg_ref):
    mine, _, _ = place_in_group()
    narr, per, tok, d = c0.shape
    for j, c in enumerate((c0, c1, c2, c3)):
        kv_ref[:, :, lax.bitwise_xor(mine, j)] = c[...]
    total = QUAD * tok
    for hh in range(per):
        k = kv_ref[0, hh].reshape(total, d)
        v = kv_ref[1, hh].reshape(total, d)
        feat = jnp.concatenate(phi_t(k, wk_ref[per * mine + hh]), axis=0)
        lane = lax.broadcasted_iota(jnp.int32, feat.shape, 1)
        feat = jnp.where(lane < total - WIN, feat, 0.0).astype(BF16)
        state = nt(extended(transposed(v).astype(BF16)), feat).astype(BF16)
        rows = state.shape[0]
        msg_ref[hh, :rows] = state
        msg_ref[hh, rows : rows + WIN] = k[total - WIN :]
        msg_ref[hh, rows + WIN :] = v[total - WIN :]


def own_kernel(kv_ref, c0, c1, c2, c3, wq_ref, wk_ref, qt_ref, win_ref, top_ref, lin_ref, fq_ref, up_ref, down_ref):
    mine, _, _ = place_in_group()
    narr, per, tok, d = c0.shape
    total = QUAD * tok
    scale = 1.0 / d**0.5
    for j, c in enumerate((c0, c1, c2, c3)):
        qt_ref[:, :, lax.bitwise_xor(mine, j)] = c[...]
    row = lax.broadcasted_iota(jnp.int32, (tok + WIN, tok), 0)
    col = lax.broadcasted_iota(jnp.int32, (tok + WIN, tok), 1)
    inside = (row > col) & (row <= col + WIN)
    causal = (row <= col)[:tok]
    for hh in range(per):
        q = qt_ref[0, hh].reshape(total, d)
        none = jnp.zeros((WIN, d), BF16)
        k = jnp.concatenate([none, kv_ref[0, hh].reshape(total, d)], axis=0)
        v = jnp.concatenate([none, kv_ref[1, hh].reshape(total, d)], axis=0)
        up, down = phi_t(q, wq_ref[per * mine + hh])
        up_ref[hh], down_ref[hh] = up, down
        fq = jnp.concatenate([up, down], axis=0).astype(BF16)
        fq_ref[hh] = fq
        fk = jnp.concatenate(phi_t(k[:total], wk_ref[per * mine + hh]), axis=0)
        lane = lax.broadcasted_iota(jnp.int32, fk.shape, 1)
        fk = jnp.where(lane >= WIN, fk, 0.0).astype(BF16)
        fk_rows = jnp.concatenate(
            [transposed(fk[:, b * tok : (b + 1) * tok]).astype(BF16) for b in range(QUAD)], axis=0
        )
        vt = extended(transposed(v).astype(BF16))
        for b in range(QUAD):
            lo, hi = b * tok, (b + 1) * tok
            score = nt(k[lo : hi + WIN], q[lo:hi]) * scale
            keep = inside if b else inside & (row >= WIN)
            score = jnp.where(keep, score, -jnp.inf)
            top = jnp.max(score, axis=0, keepdims=True)
            weight = jnp.exp(score - top).astype(BF16)
            win_ref[hh, :, lo:hi] = nn(vt[:, lo : hi + WIN], weight)
            top_ref[hh, :, lo:hi] = jnp.broadcast_to(top, (8, tok))
            amat = nn(fk_rows[:hi], fq[:, lo:hi])
            last = jnp.where(causal, amat[lo:], 0.0)
            amat = jnp.concatenate([amat[:lo], last], axis=0).astype(BF16) if b else last.astype(BF16)
            lin_ref[hh, :, lo:hi] = nn(vt[:, :hi], amat)


def out_kernel(qt_ref, win_ref, top_ref, lin_ref, fq_ref, msg_ref, wk_ref, out_ref, later_ref, grad_ref, loss_ref):
    mine, has_past, _ = place_in_group()
    narr, per, _, tok, d = qt_ref.shape
    total = QUAD * tok
    scale = 1.0 / d**0.5
    token = lax.broadcasted_iota(jnp.int32, (1, total), 1)
    early = jnp.logical_and(token < WIN, jnp.logical_not(has_past))
    row = lax.broadcasted_iota(jnp.int32, (WIN, total), 0)
    col = lax.broadcasted_iota(jnp.int32, (WIN, total), 1)
    loss = jnp.zeros((8, total), F32)
    for hh in range(per):
        fq = fq_ref[hh]
        state = jnp.where(has_past, msg_ref[hh, : d + 16].astype(F32), 0.0).astype(BF16)
        halo_k = msg_ref[hh, d + 16 : d + 16 + WIN]
        vt = extended(transposed(msg_ref[hh, d + 16 + WIN :]).astype(BF16))
        fk = jnp.concatenate(phi_t(halo_k, wk_ref[per * mine + hh]), axis=0)
        fk = jnp.where(has_past, fk, 0.0).astype(BF16)
        amat = nn(transposed(fk).astype(BF16), fq)
        amat = jnp.where(row <= col, amat, 0.0).astype(BF16)
        lin = lin_ref[hh] + nn(state, fq) + nn(vt, amat)
        score = nt(halo_k, qt_ref[0, hh, 0]) * scale
        keep = (row > col)[:, :tok] & has_past
        score = jnp.where(keep, score, -jnp.inf)
        old = top_ref[hh, :1, :tok]
        first = jnp.maximum(old, jnp.max(score, axis=0, keepdims=True))
        weight = jnp.exp(score - first).astype(BF16)
        win = win_ref[hh, :, :tok] * jnp.exp(old - first) + nn(vt, weight)
        win = jnp.concatenate([win, win_ref[hh, :, tok:]], axis=1)
        top = jnp.concatenate([first, top_ref[hh, :1, tok:]], axis=1)
        win_scale = jnp.where(early, 1.0, jnp.exp(jnp.minimum(top, 0.0)))
        lin_scale = jnp.where(early, 0.0, jnp.exp(-jnp.maximum(top, 0.0)))
        both = win_scale * win + lin_scale * lin
        inverse = 1.0 / both[d : d + 1]
        out = both[:d] * inverse
        out_ref[hh] = out.astype(BF16)
        teach = jnp.concatenate([transposed(qt_ref[1, hh, b]) for b in range(QUAD)], axis=1)
        diff = out - teach
        loss = loss + jnp.sum((diff * diff).reshape(d // 8, 8, total), axis=0)
        g = diff * (2.0 / d)
        coef = lin_scale * inverse
        g_num = coef * g
        g_den = -coef * jnp.sum(g * out, axis=0, keepdims=True)
        pad = lax.broadcasted_iota(jnp.int32, (16, total), 0)
        g_ext = jnp.concatenate([g_num, jnp.where(pad == 0, g_den, 0.0)], axis=0).astype(BF16)
        grad_ref[hh] = g_ext
        later_ref[hh] = nt(g_ext, fq).astype(BF16)
    loss_ref[...] = loss


def grad_kernel(kv_ref, qt_ref, msg_ref, grad_ref, out_ref, fq_ref, qup_ref, qdown_ref, wk_ref, diff_ref,
                s0, s1, s2, s3, gq_ref, gk_ref, k_ref, v_ref, kup_ref, kdown_ref, loss_ref, outs):
    loss_ref[...] = sum(diff_ref[:, b * loss_ref.shape[1] : (b + 1) * loss_ref.shape[1]] for b in range(QUAD))
    mine, has_past, _ = place_in_group()
    narr, per, _, tok, d = qt_ref.shape
    total = QUAD * tok
    causal = lax.broadcasted_iota(jnp.int32, (tok, tok), 0) <= lax.broadcasted_iota(jnp.int32, (tok, tok), 1)
    for hh in range(per):
        state = jnp.where(has_past, msg_ref[hh, : d + 16].astype(F32), 0.0).astype(BF16)
        k = jnp.concatenate([msg_ref[hh, d + 16 : d + 16 + WIN], kv_ref[0, hh].reshape(total, d)[: total - WIN]], axis=0)
        v = jnp.concatenate([msg_ref[hh, d + 16 + WIN :], kv_ref[1, hh].reshape(total, d)[: total - WIN]], axis=0)
        k_ref[hh], v_ref[hh] = k, v
        up, down = phi_t(k, wk_ref[per * mine + hh])
        kup_ref[hh], kdown_ref[hh] = up, down
        fk = jnp.concatenate([up, down], axis=0)
        lane = lax.broadcasted_iota(jnp.int32, fk.shape, 1)
        valid = (lane >= WIN) | has_past
        fk = jnp.where(valid, fk, 0.0).astype(BF16)
        fq = fq_ref[hh]
        g_ext = grad_ref[hh]
        g_num, g_den = g_ext[:d], g_ext[d : d + 1].astype(F32)
        grad_q = nn(transposed(state).astype(BF16), g_ext)
        grad_k = []
        for c in range(QUAD):
            lo, hi = c * tok, (c + 1) * tok
            mix = nn(v[lo:hi], g_num[:, lo:]) + g_den[:, lo:]
            first = jnp.where(causal, mix[:, :tok], 0.0)
            mix = (jnp.concatenate([first, mix[:, tok:]], axis=1) if hi < total else first).astype(BF16)
            more = nn(fk[:, lo:hi], mix)
            grad_q = grad_q + (jnp.concatenate([jnp.zeros((more.shape[0], lo), F32), more], axis=1) if c else more)
            grad_k.append(nt(fq[:, lo:], mix))
        grad_k = jnp.where(valid, jnp.concatenate(grad_k, axis=1), 0.0)
        for x, ups, downs, grad, ref in (
            (qt_ref[0, hh].reshape(total, d), qup_ref[hh], qdown_ref[hh], grad_q, gq_ref),
            (k, up, down, grad_k, gk_ref),
        ):
            high, low = split2(phi_pull(ups, downs, grad))
            ref[hh] = nn(high, x) + nn(low, x)
        for b in range(QUAD):
            outs[b, hh] = transposed(out_ref[hh, :, b * tok : (b + 1) * tok]).astype(BF16)
    for j, s in enumerate((s0, s1, s2, s3)):
        s[...] = outs[lax.bitwise_xor(mine, j)]


def put_loss(out_ref, first, loss):
    high, low = split2(loss)
    out_ref[first:] = jnp.concatenate([high, low], axis=0)


def take_loss(ref, first):
    return ref[first : first + 8].astype(F32) + ref[first + 8 : first + 16].astype(F32)


def last_kernel(later_ref, k_ref, v_ref, kup_ref, kdown_ref, gq_ref, gk_ref, l0, l1, l2, l3, out_ref):
    _, has_past, has_future = place_in_group()
    per, total, d = k_ref.shape
    half = gq_ref.shape[1]
    for hh in range(per):
        after = transposed(later_ref[hh])
        grad = nt(after[:, :d].astype(BF16), v_ref[hh]) + after[:, d : d + 1]
        lane = lax.broadcasted_iota(jnp.int32, grad.shape, 1)
        grad = jnp.where(((lane >= WIN) | has_past) & has_future, grad, 0.0)
        high, low = split2(phi_pull(kup_ref[hh], kdown_ref[hh], grad))
        more = nn(high, k_ref[hh]) + nn(low, k_ref[hh])
        out_ref[hh * half : (hh + 1) * half] = gq_ref[hh].astype(BF16)
        out_ref[(per + hh) * half : (per + hh + 1) * half] = (gk_ref[hh] + more).astype(BF16)
    put_loss(out_ref, 2 * per * half, (l0[...] + l1[...]) + (l2[...] + l3[...]))


def sum_kernel(*refs):
    *parts, out_ref = refs
    first = out_ref.shape[0] - 16
    total = sum(part[:first].astype(F32) for part in parts)
    out_ref[:first] = total.astype(BF16)
    put_loss(out_ref, first, sum(take_loss(part, first) for part in parts))


def student_kernel(s0, s1, s2, s3, student, held, wide):
    mine, _, _ = place_in_group()
    per, tok, d = s0.shape
    for j, s in enumerate((s0, s1, s2, s3)):
        held[lax.bitwise_xor(mine, j)] = s[...]
    heads = QUAD * per
    for h in range(heads):
        wide[pl.ds(h, tok, stride=heads), :] = held[h // per, h % per].astype(F32)
    student[...] = wide[...].reshape(tok, heads, d).astype(BF16)


def finish_kernel(entries, g0, g1, g2, g3, loss, gq, gk):
    mine, _, _ = place_in_group()
    heads, half, d = gq.shape
    per = heads // QUAD
    first = 2 * per * half
    l0, l1, l2, l3 = [take_loss(g, first) for g in (g0, g1, g2, g3)]
    loss[0, 0] = jnp.sum((l0 + l1) + (l2 + l3)) / entries
    for j, g in enumerate((g0, g1, g2, g3)):
        here = pl.ds(per * lax.bitwise_xor(mine, j), per)
        gq[here] = g[: per * half].astype(F32).reshape(per, half, d)
        gk[here] = g[per * half : first].astype(F32).reshape(per, half, d)


def call(kernel, out_shape, scratch=(), ins=1, space=pltpu.VMEM, micros=1.0):
    vmem = pl.BlockSpec(memory_space=pltpu.VMEM)
    return pl.pallas_call(
        kernel,
        out_shape=out_shape,
        in_specs=[pl.BlockSpec(memory_space=space)] * ins,
        out_specs=jax.tree.map(
            lambda o: pl.BlockSpec(memory_space=pltpu.SMEM) if o.shape == (1, 1) else vmem, out_shape
        ),
        scratch_shapes=list(scratch),
        cost_estimate=pl.CostEstimate(flops=int(micros * 1e9), bytes_accessed=0, transcendentals=0),
        compiler_params=pltpu.CompilerParams(vmem_limit_bytes=24 * 2**20),
    )


def shape(*dims, dtype=BF16):
    return jax.ShapeDtypeStruct(dims, dtype)


def flip(x, axis, by):
    return lax.ppermute(x, axis, [(i, i ^ by) for i in range(lax.axis_size(axis))])


def state_over_groups(msg, d, wk_pair, group, groups, members):
    if groups == 2:
        return flip(msg, "ctx", QUAD)
    every = lax.all_gather(msg, "ctx", axis_index_groups=members)
    k, v = every[:, :, d + 16 : d + 16 + WIN], every[:, :, d + 16 + WIN :]
    proj = jnp.einsum("gptd,pfd->gptf", k, wk_pair, preferred_element_type=F32)
    feat = jnp.concatenate([jax.nn.softmax(proj, axis=-1), jax.nn.softmax(-proj, axis=-1)], axis=-1)
    tail = jnp.einsum("gptd,gptf->gpdf", v.astype(F32), feat, precision=lax.Precision.HIGHEST)
    place = jnp.arange(groups)[:, None, None, None]
    norm = jnp.sum(feat, axis=2)[:, :, None, :]
    tail = jnp.concatenate([tail, jnp.pad(norm, ((0, 0), (0, 0), (0, 15), (0, 0)))], axis=2)
    state = jnp.sum(jnp.where(place < group, every[:, :, : d + 16].astype(F32), 0.0), axis=0)
    state = state + jnp.sum(jnp.where(place < group - 1, tail, 0.0), axis=0)
    halo = lax.dynamic_index_in_dim(every, jnp.maximum(group - 1, 0), 0, keepdims=False)
    return jnp.concatenate([state.astype(BF16), halo[:, d + 16 :]], axis=1)


def later_over_groups(later, group, groups, members):
    if groups == 2:
        return flip(later, "ctx", QUAD)
    every = lax.all_gather(later, "ctx", axis_index_groups=members).astype(F32)
    place = jnp.arange(groups)[:, None, None, None]
    return jnp.sum(jnp.where(place > group, every, 0.0), axis=0).astype(BF16)


def sum_over_groups(part, groups, members):
    if groups == 2:
        return [part, flip(part, "ctx", QUAD)]
    every = lax.all_gather(part, "ctx", axis_index_groups=members)
    return [every[g] for g in range(groups)]


def per_device(queries, keys, values, teacher, wq, wk):
    tok, heads, d = queries.shape
    half = wq.shape[1]
    per = heads // QUAD
    total = QUAD * tok
    shards = lax.axis_size("ctx")
    groups = shards // QUAD
    group = lax.axis_index("ctx") // QUAD
    members = [[g * QUAD + p for g in range(groups)] for p in range(QUAD)]

    block = shape(2, per, tok, d)
    pack = call(
        pack_kernel, [block] * QUAD,
        [
            pltpu.VMEM((tok, heads, d), BF16),
            pltpu.VMEM((tok, heads, d), BF16),
            pltpu.VMEM((2, tok * heads, d), F32),
            pltpu.VMEM((QUAD, 2, per, tok, d), BF16),
            pltpu.SemaphoreType.DMA((2,)),
        ],
        ins=2, space=pltpu.HBM,
    )
    kv = pack(keys, values)
    kv = [kv[0]] + [flip(kv[j], "ctx", j) for j in range(1, QUAD)]
    qt = pack(queries, teacher)
    qt = [qt[0]] + [flip(qt[j], "ctx", j) for j in range(1, QUAD)]

    rows = d + 16 + 2 * WIN
    kv, msg = call(
        key_kernel, [shape(2, per, QUAD, tok, d), shape(per, rows, d)], ins=5, micros=KEY_US
    )(*kv, wk)
    wk_pair = (
        lax.dynamic_slice_in_dim(wk, per * (lax.axis_index("ctx") % QUAD), per, 0) if groups != 2 else None
    )
    msg = state_over_groups(msg, d, wk_pair, group, groups, members)

    sums = shape(per, d + 16, total, dtype=F32)
    part = shape(per, half, total, dtype=F32)
    grad = shape(per, half, d, dtype=F32)
    qt, win, top, lin, fq, q_up, q_down = call(
        own_kernel,
        [shape(2, per, QUAD, tok, d), sums, shape(per, 8, total, dtype=F32), sums,
         shape(per, 2 * half, total), part, part],
        ins=7, micros=OWN_US,
    )(kv, *qt, wq, wk)
    out, later, g_out, squares = call(
        out_kernel,
        [shape(per, d, total), shape(per, d + 16, 2 * half), shape(per, d + 16, total), shape(8, total, dtype=F32)],
        ins=7, micros=2.0,
    )(qt, win, top, lin, fq, msg, wk)
    later = later_over_groups(later, group, groups, members)
    *out, gq, gk, k, v, k_up, k_down, loss = call(
        grad_kernel,
        [shape(per, tok, d)] * QUAD + [grad, grad, shape(per, total, d), shape(per, total, d), part, part,
         shape(8, tok, dtype=F32)],
        [pltpu.VMEM((QUAD, per, tok, d), BF16)],
        ins=10, micros=GRAD_US,
    )(kv, qt, msg, g_out, out, fq, q_up, q_down, wk, squares)
    losses = [loss] + [flip(loss, "head", j) for j in range(1, lax.axis_size("head"))]
    rows = 2 * per * half + 16
    grads = call(last_kernel, shape(rows, d), ins=11)(later, k, v, k_up, k_down, gq, gk, *losses)
    grads = sum_over_groups(grads, groups, members)
    grads = call(sum_kernel, shape(rows, d), ins=len(grads))(*grads)
    grads = [grads] + [flip(grads, "ctx", j) for j in range(1, QUAD)]
    out = [out[0]] + [flip(out[j], "ctx", j) for j in range(1, QUAD)]
    entries = tok * shards * heads * lax.axis_size("head") * d
    student = call(
        student_kernel, shape(tok, heads, d),
        [pltpu.VMEM((QUAD, per, tok, d), BF16), pltpu.VMEM((tok * heads, d), F32)],
        ins=4, micros=STUDENT_US,
    )(*out)
    whole = shape(heads, half, d, dtype=F32)
    loss, grad_q, grad_k = call(
        functools.partial(finish_kernel, entries), [shape(1, 1, dtype=F32), whole, whole], ins=4
    )(*grads)
    return student, loss.reshape(()), grad_q, grad_k


def solution(mesh):
    wide = P("ctx", "head", None)
    narrow = P("head", None, None)
    return jax.shard_map(
        per_device,
        mesh=mesh,
        in_specs=(wide, wide, wide, wide, narrow, narrow),
        out_specs=(wide, P(), narrow, narrow),
        check_vma=False,
    )
```

time: 62.2 us -> 50 us (0.80)
  waiting for transfers between devices: 22.2 us -> 12.4 us
  Pallas kernels: 14.2 us -> 11 us
  starting transfers between devices: 22.9 us -> 23.8 us
    ppermute x18, waiting for transfers between devices: 22.2 us -> 12.4 us  [flip(): lax.ppermute(x, axis, [(i, i ^ by) for i in range(lax.axis_size(axis))])]
    pallas_call x7 -> x10, Pallas kernels: 14.2 us -> 11 us  [the longest x1 2.92 us: per_device(): call(own_kernel, [shape(2, per, QUAD, tok, d), sums, shape(per, 8, total,...]
    ppermute x18, starting transfers between devices: 22.9 us -> 23.8 us  [flip(): lax.ppermute(x, axis, [(i, i ^ by) for i in range(lax.axis_size(axis))])]
  transfers between devices with their start and end apart: 18 -> 18, of which waited for: 12 -> 10; matrix products, arithmetic and copies ran while one was open for 0% -> 0% of each run, Pallas kernels for 2% -> 15%
where the time goes in v2:
time: 50 us; the launch traced here: 49.9 us
  starting transfers between devices  23.8 us (48%)
  waiting for transfers between devices  12.4 us (25%)
  Pallas kernels  11 us (22%)
  local copies, waits for them, and re-layouts  1.91 us (4%)
  between operations  0.73 us (1%)
    ppermute x18, starting transfers between devices, flip(): lax.ppermute(x, axis, [(i, i ^ by) for i in range(lax.axis_size(axis))])  23.8 us
    ppermute x18, waiting for transfers between devices, flip(): lax.ppermute(x, axis, [(i, i ^ by) for i in range(lax.axis_size(axis))])  12.4 us
    pallas_call x1, Pallas kernels, per_device(): call(own_kernel, [shape(2, per, QUAD, tok, d), sums, shape(per, 8, total,...  2.92 us
    pallas_call x1, Pallas kernels, per_device(): call(grad_kernel, [shape(per, tok, d)] * QUAD + [grad, grad, shape(per, t...  2.51 us
    unnamed x12, local copies, waits for them, and re-layouts  1.91 us
    pallas_call x1, Pallas kernels, per_device(): call(out_kernel, [shape(per, d, total), shape(per, d + 16, 2 * half), sha...  1.63 us
  transfers between devices with their start and end apart: 18, of which 10 were waited for; matrix products, arithmetic and copies ran while one was open for 0% of the time, Pallas kernels for 15%

profile of v2, /device:TPU:0, one launch (start us, length us, event | category | flops | bytes accessed | tf_op | source)
XLA Modules:
  0.0 49.9 jit_solution(14921725516297612674)
XLA Ops:
  0.6 0.0 copy-start
  0.6 0.9 %copy-done = bf16[128,8,128]{2,1,0:T(8,128)(2,1)S(1)} copy-done((bf16[128,8,128]{2,1,0:T(8,128)(2,1)S(1)}, bf16[128,8,128]{2,1,0:T(8,128)(2,1)}, u32[]{:S(2)}) %copy-start) | copy-done | bytes 262168
  1.6 0.0 copy-start.1
  1.6 0.9 %copy-done.1 = bf16[128,8,128]{2,1,0:T(8,128)(2,1)S(1)} copy-done((bf16[128,8,128]{2,1,0:T(8,128)(2,1)S(1)}, bf16[128,8,128]{2,1,0:T(8,128)(2,1)}, u32[]{:S(2)}) %copy-start.1) | copy-done | bytes 262168
  2.5 0.0 copy-start.2
  2.5 0.0 copy-start.3
  2.5 0.3 shard_map.93
  2.9 3.0 %collective-permute-start = (bf16[2,2,128,128]{3,2,1,0:T(8,128)(2,1)S(1)}, bf16[2,2,128,128]{3,2,1,0:T(8,128)(2,1)S(1)}, u32[]{:S(2)}, u32[]{:S(2)}) collective-permute-start(bf16[2,2,128,128]{3,2,1,0:T(8,128)(2,1)S(1)} %get-tuple-element.40), channel_id=1, source_target_pairs={{0,4},{4,0},{8,12},{12,8},{16,20},{20,16},{24,28},{28,24},{1,5},{5... | collective-permute-start | bytes 393224 | tf_op jit(solution)/shard_map/ppermute | solution.py:318
  5.9 1.6 %collective-permute-start.1 = (bf16[2,2,128,128]{3,2,1,0:T(8,128)(2,1)S(1)}, bf16[2,2,128,128]{3,2,1,0:T(8,128)(2,1)S(1)}, u32[]{:S(2)}, u32[]{:S(2)}) collective-permute-start(bf16[2,2,128,128]{3,2,1,0:T(8,128)(2,1)S(1)} %get-tuple-element.41), channel_id=1, source_target_pairs={{0,8},{4,12},{8,0},{12,4},{16,24},{20,28},{24,16},{28,20},{1,9},{5... | collective-permute-start | bytes 393224 | tf_op jit(solution)/shard_map/ppermute | solution.py:318
  7.5 0.0 copy-start.5
  7.5 0.0 collective-permute-start.2
  7.5 0.0 copy-done.2
  7.5 0.0 copy-done.3
  7.5 0.3 shard_map.95
  7.8 2.0 %collective-permute-start.3 = (bf16[2,2,128,128]{3,2,1,0:T(8,128)(2,1)S(1)}, bf16[2,2,128,128]{3,2,1,0:T(8,128)(2,1)S(1)}, u32[]{:S(2)}, u32[]{:S(2)}) collective-permute-start(bf16[2,2,128,128]{3,2,1,0:T(8,128)(2,1)S(1)} %get-tuple-element.45), channel_id=1, source_target_pairs={{0,4},{4,0},{8,12},{12,8},{16,20},{20,16},{24,28},{28,24},{1,5},{5... | collective-permute-start | bytes 393224 | tf_op jit(solution)/shard_map/ppermute | solution.py:318
  9.8 1.6 %collective-permute-start.4 = (bf16[2,2,128,128]{3,2,1,0:T(8,128)(2,1)S(1)}, bf16[2,2,128,128]{3,2,1,0:T(8,128)(2,1)S(1)}, u32[]{:S(2)}, u32[]{:S(2)}) collective-permute-start(bf16[2,2,128,128]{3,2,1,0:T(8,128)(2,1)S(1)} %get-tuple-element.46), channel_id=1, source_target_pairs={{0,8},{4,12},{8,0},{12,4},{16,24},{20,28},{24,16},{28,20},{1,9},{5... | collective-permute-start | bytes 393224 | tf_op jit(solution)/shard_map/ppermute | solution.py:318
  11.4 0.0 collective-permute-done.c1
  11.4 1.0 %collective-permute-start.5 = (bf16[2,2,128,128]{3,2,1,0:T(8,128)(2,1)S(1)}, bf16[2,2,128,128]{3,2,1,0:T(8,128)(2,1)S(1)}, u32[]{:S(2)}, u32[]{:S(2)}) collective-permute-start(bf16[2,2,128,128]{3,2,1,0:T(8,128)(2,1)S(1)} %get-tuple-element.47), channel_id=1, source_target_pairs={{0,12},{4,8},{8,4},{12,0},{16,28},{20,24},{24,20},{28,16},{1,13},{... | collective-permute-start | bytes 393224 | tf_op jit(solution)/shard_map/ppermute | solution.py:318
  12.4 0.0 collective-permute-done.1.c2
  12.4 2.4 %collective-permute-done.2.c3 = bf16[2,2,128,128]{3,2,1,0:T(8,128)(2,1)S(1)} collective-permute-done((bf16[2,2,128,128]{3,2,1,0:T(8,128)(2,1)S(1)}, bf16[2,2,128,128]{3,2,1,0:T(8,128)(2,1)S(1)}, u32[]{:S(2)}, u32[]{:S(2)}) %collective-permute-start.2) | collective-permute-done | bytes 131104 | tf_op jit(solution)/shard_map/ppermute | solution.py:318
  14.9 0.0 copy-done.5
  14.9 0.0 copy-start.4
  14.9 0.7 %shard_map.94 = (bf16[2,2,4,128,128]{4,3,2,1,0:T(8,128)(2,1)S(1)}, bf16[2,272,128]{2,1,0:T(8,128)(2,1)S(1)}) custom-call(bf16[2,2,128,128]{3,2,1,0:T(8,128)(2,1)S(1)} %get-tuple-element.39.c0, bf16[2,2,128,128]{3,2,1,0:T(8,128)(2,1)S(1)} %collective-permute-done.c1, bf16[2,2,128,128]{3,2,1,0:T(8,128)(2,1)S(1)} %collective-permute-done.1.c2, ...), custom_call_target="tpu_custom_call" | custom-call | flops 20000000000 | tf_op jit(solution)/shard_map/pallas_call | solution.py:381
  15.6 2.6 %collective-permute-start.6 = (bf16[2,272,128]{2,1,0:T(8,128)(2,1)S(1)}, bf16[2,272,128]{2,1,0:T(8,128)(2,1)S(1)}, u32[]{:S(2)}, u32[]{:S(2)}) collective-permute-start(bf16[2,272,128]{2,1,0:T(8,128)(2,1)S(1)} %get-tuple-element.49), channel_id=1, source_target_pairs={{0,16},{4,20},{8,24},{12,28},{16,0},{20,4},{24,8},{28,12},{1,17},{... | collective-permute-start | bytes 417800 | tf_op jit(solution)/shard_map/ppermute | solution.py:318
  18.2 0.0 collective-permute-done.3.c1
  18.2 1.2 %collective-permute-done.4.c2 = bf16[2,2,128,128]{3,2,1,0:T(8,128)(2,1)S(1)} collective-permute-done((bf16[2,2,128,128]{3,2,1,0:T(8,128)(2,1)S(1)}, bf16[2,2,128,128]{3,2,1,0:T(8,128)(2,1)S(1)}, u32[]{:S(2)}, u32[]{:S(2)}) %collective-permute-start.4) | collective-permute-done | bytes 131104 | tf_op jit(solution)/shard_map/ppermute | solution.py:318
  19.4 1.2 %collective-permute-done.5.c3 = bf16[2,2,128,128]{3,2,1,0:T(8,128)(2,1)S(1)} collective-permute-done((bf16[2,2,128,128]{3,2,1,0:T(8,128)(2,1)S(1)}, bf16[2,2,128,128]{3,2,1,0:T(8,128)(2,1)S(1)}, u32[]{:S(2)}, u32[]{:S(2)}) %collective-permute-start.5) | collective-permute-done | bytes 131104 | tf_op jit(solution)/shard_map/ppermute | solution.py:318
  20.6 0.0 copy-done.4
  20.6 2.9 %shard_map.96 = (bf16[2,2,4,128,128]{4,3,2,1,0:T(8,128)(2,1)S(1)}, f32[2,144,512]{2,1,0:T(8,128)S(1)}, f32[2,8,512]{2,1,0:T(8,128)S(1)}, f32[2,144,512]{2,1,0:T(...) custom-call(bf16[2,2,4,128,128]{4,3,2,1,0:T(8,128)(2,1)S(1)} %get-tuple-element.4, ...), custom_call_target="tpu_custom_call" | custom-call | flops 20000000000 | tf_op jit(solution)/shard_map/pallas_call | solution.py:392
  23.6 0.9 %collective-permute-done.6.msg_ref = bf16[2,272,128]{2,1,0:T(8,128)(2,1)S(1)} collective-permute-done((bf16[2,272,128]{2,1,0:T(8,128)(2,1)S(1)}, bf16[2,272,128]{2,1,0:T(8,128)(2,1)S(1)}, u32[]{:S(2)}, u32[]{:S(2)}) %collective-permute-start.6) | collective-permute-done | bytes 139296 | tf_op jit(solution)/shard_map/ppermute | solution.py:318
  24.4 1.6 %shard_map.97 = (bf16[2,128,512]{2,1,0:T(8,128)(2,1)S(1)}, bf16[2,144,128]{2,1,0:T(8,128)(2,1)S(1)}, bf16[2,144,512]{2,1,0:T(8,128)(2,1)S(1)}, f32[8,512]{1,0:T(8,128)S(1)}) custom-call(bf16[2,2,4,128,128]{4,3,2,1,0:T(8,128)(2,1)S(1)} %get-tuple-element.48.qt_ref, f32[2,144,512]{2,1,0:T(8,128)S(1)} %get-tuple-element.50.win_ref, ...), custom_call_target="tpu_custom_call" | custom-call | flops 2000000000 | tf_op jit(solution)/shard_map/pallas_call | solution.py:398
  26.1 1.6 %collective-permute-start.10 = (bf16[2,144,128]{2,1,0:T(8,128)(2,1)S(1)}, bf16[2,144,128]{2,1,0:T(8,128)(2,1)S(1)}, u32[]{:S(2)}, u32[]{:S(2)}) collective-permute-start(bf16[2,144,128]{2,1,0:T(8,128)(2,1)S(1)} %get-tuple-element.63), channel_id=1, source_target_pairs={{0,16},{4,20},{8,24},{12,28},{16,0},{20,4},{24,8},{28,12},{1,17},{... | collective-permute-start | bytes 221192 | tf_op jit(solution)/shard_map/ppermute | solution.py:318
  27.7 2.5 %shard_map.98 = (bf16[2,128,128]{2,1,0:T(8,128)(2,1)S(1)}, bf16[2,128,128]{2,1,0:T(8,128)(2,1)S(1)}, bf16[2,128,128]{2,1,0:T(8,128)(2,1)S(1)}, bf16[2,128,128]{2...) custom-call(bf16[2,2,4,128,128]{4,3,2,1,0:T(8,128)(2,1)S(1)} %get-tu, ...), custom_call_target="tpu_custom_call" | custom-call | flops 20000000000 | tf_op jit(solution)/shard_map/pallas_call | solution.py:404
  30.2 0.1 collective-permute-start.13
  30.3 1.6 %collective-permute-start.12 = (f32[8,128]{1,0:T(8,128)S(1)}, f32[8,128]{1,0:T(8,128)S(1)}, u32[]{:S(2)}, u32[]{:S(2)}) collective-permute-start(f32[8,128]{1,0:T(8,128)S(1)} %get-tuple-element.70.l0), channel_id=1, source_target_pairs={{0,2},{1,3},{2,0},{3,1},{4,6},{5,7},{6,4},{7,5},{8,10},{9,11},{10,... | collective-permute-start | bytes 12296 | tf_op jit(solution)/shard_map/ppermute | solution.py:318
  31.8 0.3 collective-permute-start.11
  32.1 1.2 %collective-permute-done.13.l3 = f32[8,128]{1,0:T(8,128)S(1)} collective-permute-done((f32[8,128]{1,0:T(8,128)S(1)}, f32[8,128]{1,0:T(8,128)S(1)}, u32[]{:S(2)}, u32[]{:S(2)}) %collective-permute-start.13) | collective-permute-done | bytes 4128 | tf_op jit(solution)/shard_map/ppermute | solution.py:318
  33.3 0.7 %collective-permute-done.12.l2 = f32[8,128]{1,0:T(8,128)S(1)} collective-permute-done((f32[8,128]{1,0:T(8,128)S(1)}, f32[8,128]{1,0:T(8,128)S(1)}, u32[]{:S(2)}, u32[]{:S(2)}) %collective-permute-start.12) | collective-permute-done | bytes 4128 | tf_op jit(solution)/shard_map/ppermute | solution.py:318
  34.0 0.0 collective-permute-done.11.l1
  34.0 0.0 collective-permute-done.10.later_ref
  34.0 0.9 %shard_map.100.refs_0_ = bf16[272,128]{1,0:T(8,128)(2,1)S(1)} custom-call(bf16[2,144,128]{2,1,0:T(8,128)(2,1)S(1)} %collective-permute-done.10.later_ref, bf16[2,512,128]{2,1,0:T(8,128)(2,1)S(1)} %get-tuple-element.64.k_ref, bf16[2,512,128]{2,1,0:T(8,128)(2,1)S(1)} %get-tuple-element.65.v_ref, f32[2,64,512]{2,1,0:T(8,128)S(1)} %get-tuple-element.66.kup_ref, ...), custom_call_target="tpu_custom_call" | custom-call | flops 1000000000 | tf_op jit(solution)/shard_map/pallas_call | solution.py:413
  34.8 1.5 %collective-permute-start.14 = (bf16[272,128]{1,0:T(8,128)(2,1)S(1)}, bf16[272,128]{1,0:T(8,128)(2,1)S(1)}, u32[]{:S(2)}, u32[]{:S(2)}) collective-permute-start(bf16[272,128]{1,0:T(8,128)(2,1)S(1)} %shard_map.100.refs_0_), channel_id=1, source_target_pairs={{0,16},{4,20},{8,24},{12,28},{16,0},{20,4},{24,8},{28,12},{1,17},{... | collective-permute-start | bytes 208904 | tf_op jit(solution)/shard_map/ppermute | solution.py:318
  36.3 1.4 %collective-permute-start.7 = (bf16[2,128,128]{2,1,0:T(8,128)(2,1)S(1)}, bf16[2,128,128]{2,1,0:T(8,128)(2,1)S(1)}, u32[]{:S(2)}, u32[]{:S(2)}) collective-permute-start(bf16[2,128,128]{2,1,0:T(8,128)(2,1)S(1)} %get-tuple-element.60), channel_id=1, source_target_pairs={{0,4},{4,0},{8,12},{12,8},{16,20},{20,16},{24,28},{28,24},{1,5},{5... | collective-permute-start | bytes 196616 | tf_op jit(solution)/shard_map/ppermute | solution.py:318
  37.7 0.9 %collective-permute-start.8 = (bf16[2,128,128]{2,1,0:T(8,128)(2,1)S(1)}, bf16[2,128,128]{2,1,0:T(8,128)(2,1)S(1)}, u32[]{:S(2)}, u32[]{:S(2)}) collective-permute-start(bf16[2,128,128]{2,1,0:T(8,128)(2,1)S(1)} %get-tuple-element.61), channel_id=1, source_target_pairs={{0,8},{4,12},{8,0},{12,4},{16,24},{20,28},{24,16},{28,20},{1,9},{5... | collective-permute-start | bytes 196616 | tf_op jit(solution)/shard_map/ppermute | solution.py:318
  38.6 1.2 %collective-permute-start.9 = (bf16[2,128,128]{2,1,0:T(8,128)(2,1)S(1)}, bf16[2,128,128]{2,1,0:T(8,128)(2,1)S(1)}, u32[]{:S(2)}, u32[]{:S(2)}) collective-permute-start(bf16[2,128,128]{2,1,0:T(8,128)(2,1)S(1)} %get-tuple-element.62), channel_id=1, source_target_pairs={{0,12},{4,8},{8,4},{12,0},{16,28},{20,24},{24,20},{28,16},{1,13},{... | collective-permute-start | bytes 196616 | tf_op jit(solution)/shard_map/ppermute | solution.py:318
  39.8 2.1 %collective-permute-done.14.refs_1_ = bf16[272,128]{1,0:T(8,128)(2,1)S(1)} collective-permute-done((bf16[272,128]{1,0:T(8,128)(2,1)S(1)}, bf16[272,128]{1,0:T(8,128)(2,1)S(1)}, u32[]{:S(2)}, u32[]{:S(2)}) %collective-permute-start.14) | collective-permute-done | bytes 69664 | tf_op jit(solution)/shard_map/ppermute | solution.py:318
  41.9 2.1 %collective-permute-start.17 = (bf16[272,128]{1,0:T(8,128)(2,1)S(1)}, bf16[272,128]{1,0:T(8,128)(2,1)S(1)}, u32[]{:S(2)}, u32[]{:S(2)}) collective-permute-start(bf16[272,128]{1,0:T(8,128)(2,1)S(1)} %shard_map.101.g0), channel_id=1, source_target_pairs={{0,12},{4,8},{8,4},{12,0},{16,28},{20,24},{24,20},{28,16},{1,13},{... | collective-permute-start | bytes 208904 | tf_op jit(solution)/shard_map/ppermute | solution.py:318
  44.0 0.8 %collective-permute-start.16 = (bf16[272,128]{1,0:T(8,128)(2,1)S(1)}, bf16[272,128]{1,0:T(8,128)(2,1)S(1)}, u32[]{:S(2)}, u32[]{:S(2)}) collective-permute-start(bf16[272,128]{1,0:T(8,128)(2,1)S(1)} %shard_map.101.g0), channel_id=1, source_target_pairs={{0,8},{4,12},{8,0},{12,4},{16,24},{20,28},{24,16},{28,20},{1,9},{5... | collective-permute-start | bytes 208904 | tf_op jit(solution)/shard_map/ppermute | solution.py:318
  44.7 0.0 collective-permute-done.7.s1
  44.7 0.7 %collective-permute-start.15 = (bf16[272,128]{1,0:T(8,128)(2,1)S(1)}, bf16[272,128]{1,0:T(8,128)(2,1)S(1)}, u32[]{:S(2)}, u32[]{:S(2)}) collective-permute-start(bf16[272,128]{1,0:T(8,128)(2,1)S(1)} %shard_map.101.g0), channel_id=1, source_target_pairs={{0,4},{4,0},{8,12},{12,8},{16,20},{20,16},{24,28},{28,24},{1,5},{5... | collective-permute-start | bytes 208904 | tf_op jit(solution)/shard_map/ppermute | solution.py:318
  45.4 0.0 collective-permute-done.8.s2
  45.4 0.0 collective-permute-done.9.s3
  45.4 0.9 %shard_map.99 = bf16[128,8,128]{2,1,0:T(8,128)(2,1)} custom-call(bf16[2,128,128]{2,1,0:T(8,128)(2,1)S(1)} %get-tuple-element.59.s0, bf16[2,128,128]{2,1,0:T(8,128)(2,1)S(1)} %collective-permute-done.7.s1, bf16[2,128,128]{2,1,0:T(8,128)(2,1)S(1)} %collective-permute-done.8.s2, bf16[2,128,128]{2,1,0:T(8,128)(2,1)S(1)} %collective-permute-done.9.s3), custom_call_target="tpu_custom_call" | custom-call | flops 20000000000 | tf_op jit(solution)/shard_map/pallas_call | solution.py:419
  46.3 0.8 %collective-permute-done.17.g3 = bf16[272,128]{1,0:T(8,128)(2,1)S(1)} collective-permute-done((bf16[272,128]{1,0:T(8,128)(2,1)S(1)}, bf16[272,128]{1,0:T(8,128)(2,1)S(1)}, u32[]{:S(2)}, u32[]{:S(2)}) %collective-permute-start.17) | collective-permute-done | bytes 69664 | tf_op jit(solution)/shard_map/ppermute | solution.py:318
  47.1 1.1 %collective-permute-done.16.g2 = bf16[272,128]{1,0:T(8,128)(2,1)S(1)} collective-permute-done((bf16[272,128]{1,0:T(8,128)(2,1)S(1)}, bf16[272,128]{1,0:T(8,128)(2,1)S(1)}, u32[]{:S(2)}, u32[]{:S(2)}) %collective-permute-start.16) | collective-permute-done | bytes 69664 | tf_op jit(solution)/shard_map/ppermute | solution.py:318
  48.3 0.8 %collective-permute-done.15.g1 = bf16[272,128]{1,0:T(8,128)(2,1)S(1)} collective-permute-done((bf16[272,128]{1,0:T(8,128)(2,1)S(1)}, bf16[272,128]{1,0:T(8,128)(2,1)S(1)}, u32[]{:S(2)}, u32[]{:S(2)}) %collective-permute-start.15) | collective-permute-done | bytes 69664 | tf_op jit(solution)/shard_map/ppermute | solution.py:318
  49.0 0.8 %shard_map.102 = (f32[1,1]{1,0:T(1,128)}, f32[8,64,128]{2,1,0:T(8,128)}, f32[8,64,128]{2,1,0:T(8,128)}) custom-call(bf16[272,128]{1,0:T(8,128)(2,1)S(1)} %shard_map.101.g0, bf16[272,128]{1,0:T(8,128)(2,1)S(1)} %collective-permute-done.15.g1, bf16[272,128]{1,0:T(8,128)(2,1)S(1)} %collective-permute-done.16.g2, bf16[272,128]{1,0:T(8,128)(2,1)S(1)} %collective-permute-done.17.g3), custom_call_target="tpu_custom_call" | custom-call | flops 1000000000 | tf_op jit(solution)/shard_map/pallas_call | solution.py:425
  (1 shorter events, 0.0 us)
Async XLA Ops:
  0.6 1.0 %copy-start = (bf16[128,8,128]{2,1,0:T(8,128)(2,1)S(1)}, bf16[128,8,128]{2,1,0:T(8,128)(2,1)}, u32[]{:S(2)}) copy-start(bf16[128,8,128]{2,1,0:T(8,128)(2,1)} %refs_0_.2) | copy-start | bytes 786436
  1.6 0.9 %copy-start.1 = (bf16[128,8,128]{2,1,0:T(8,128)(2,1)S(1)}, bf16[128,8,128]{2,1,0:T(8,128)(2,1)}, u32[]{:S(2)}) copy-start(bf16[128,8,128]{2,1,0:T(8,128)(2,1)} %refs_1_.2) | copy-start | bytes 786436
  2.5 5.0 %copy-start.2 = (bf16[128,8,128]{2,1,0:T(8,128)(2,1)S(1)}, bf16[128,8,128]{2,1,0:T(8,128)(2,1)}, u32[]{:S(2)}) copy-start(bf16[128,8,128]{2,1,0:T(8,128)(2,1)} %refs_0_.3) | copy-start | bytes 786436
  2.5 5.0 %copy-start.3 = (bf16[128,8,128]{2,1,0:T(8,128)(2,1)S(1)}, bf16[128,8,128]{2,1,0:T(8,128)(2,1)}, u32[]{:S(2)}) copy-start(bf16[128,8,128]{2,1,0:T(8,128)(2,1)} %refs_1_.3) | copy-start | bytes 786436
  2.9 8.5 %collective-permute-start = (bf16[2,2,128,128]{3,2,1,0:T(8,128)(2,1)S(1)}, bf16[2,2,128,128]{3,2,1,0:T(8,128)(2,1)S(1)}, u32[]{:S(2)}, u32[]{:S(2)}) collective-permute-start(bf16[2,2,128,128]{3,2,1,0:T(8,128)(2,1)S(1)} %get-tuple-element.40), channel_id=1, source_target_pairs={{0,4},{4,0},{8,12},{12,8},{16,20},{20,16},{24,28},{28,24},{1,5},{5... | collective-permute-start | bytes 393224 | tf_op jit(solution)/shard_map/ppermute | solution.py:318
  5.9 6.5 %collective-permute-start.1 = (bf16[2,2,128,128]{3,2,1,0:T(8,128)(2,1)S(1)}, bf16[2,2,128,128]{3,2,1,0:T(8,128)(2,1)S(1)}, u32[]{:S(2)}, u32[]{:S(2)}) collective-permute-start(bf16[2,2,128,128]{3,2,1,0:T(8,128)(2,1)S(1)} %get-tuple-element.41), channel_id=1, source_target_pairs={{0,8},{4,12},{8,0},{12,4},{16,24},{20,28},{24,16},{28,20},{1,9},{5... | collective-permute-start | bytes 393224 | tf_op jit(solution)/shard_map/ppermute | solution.py:318
  7.5 7.4 %copy-start.5 = (bf16[8,64,128]{2,1,0:T(8,128)(2,1)S(1)}, bf16[8,64,128]{2,1,0:T(8,128)(2,1)}, u32[]{:S(2)}) copy-start(bf16[8,64,128]{2,1,0:T(8,128)(2,1)} %wk_ref.7) | copy-start | bytes 393220
  7.5 7.4 %collective-permute-start.2 = (bf16[2,2,128,128]{3,2,1,0:T(8,128)(2,1)S(1)}, bf16[2,2,128,128]{3,2,1,0:T(8,128)(2,1)S(1)}, u32[]{:S(2)}, u32[]{:S(2)}) collective-permute-start(bf16[2,2,128,128]{3,2,1,0:T(8,128)(2,1)S(1)} %get-tuple-element.42), channel_id=1, source_target_pairs={{0,12},{4,8},{8,4},{12,0},{16,28},{20,24},{24,20},{28,16},{1,13},{... | collective-permute-start | bytes 393224 | tf_op jit(solution)/shard_map/ppermute | solution.py:318
  7.8 10.3 %collective-permute-start.3 = (bf16[2,2,128,128]{3,2,1,0:T(8,128)(2,1)S(1)}, bf16[2,2,128,128]{3,2,1,0:T(8,128)(2,1)S(1)}, u32[]{:S(2)}, u32[]{:S(2)}) collective-permute-start(bf16[2,2,128,128]{3,2,1,0:T(8,128)(2,1)S(1)} %get-tuple-element.45), channel_id=1, source_target_pairs={{0,4},{4,0},{8,12},{12,8},{16,20},{20,16},{24,28},{28,24},{1,5},{5... | collective-permute-start | bytes 393224 | tf_op jit(solution)/shard_map/ppermute | solution.py:318
  9.8 9.6 %collective-permute-start.4 = (bf16[2,2,128,128]{3,2,1,0:T(8,128)(2,1)S(1)}, bf16[2,2,128,128]{3,2,1,0:T(8,128)(2,1)S(1)}, u32[]{:S(2)}, u32[]{:S(2)}) collective-permute-start(bf16[2,2,128,128]{3,2,1,0:T(8,128)(2,1)S(1)} %get-tuple-element.46), channel_id=1, source_target_pairs={{0,8},{4,12},{8,0},{12,4},{16,24},{20,28},{24,16},{28,20},{1,9},{5... | collective-permute-start | bytes 393224 | tf_op jit(solution)/shard_map/ppermute | solution.py:318
  11.4 9.2 %collective-permute-start.5 = (bf16[2,2,128,128]{3,2,1,0:T(8,128)(2,1)S(1)}, bf16[2,2,128,128]{3,2,1,0:T(8,128)(2,1)S(1)}, u32[]{:S(2)}, u32[]{:S(2)}) collective-permute-start(bf16[2,2,128,128]{3,2,1,0:T(8,128)(2,1)S(1)} %get-tuple-element.47), channel_id=1, source_target_pairs={{0,12},{4,8},{8,4},{12,0},{16,28},{20,24},{24,20},{28,16},{1,13},{... | collective-permute-start | bytes 393224 | tf_op jit(solution)/shard_map/ppermute | solution.py:318
  14.9 5.8 %copy-start.4 = (bf16[8,64,128]{2,1,0:T(8,128)(2,1)S(1)}, bf16[8,64,128]{2,1,0:T(8,128)(2,1)}, u32[]{:S(2)}) copy-start(bf16[8,64,128]{2,1,0:T(8,128)(2,1)} %wq_ref.1) | copy-start | bytes 393220
  15.6 8.9 %collective-permute-start.6 = (bf16[2,272,128]{2,1,0:T(8,128)(2,1)S(1)}, bf16[2,272,128]{2,1,0:T(8,128)(2,1)S(1)}, u32[]{:S(2)}, u32[]{:S(2)}) collective-permute-start(bf16[2,272,128]{2,1,0:T(8,128)(2,1)S(1)} %get-tuple-element.49), channel_id=1, source_target_pairs={{0,16},{4,20},{8,24},{12,28},{16,0},{20,4},{24,8},{28,12},{1,17},{... | collective-permute-start | bytes 417800 | tf_op jit(solution)/shard_map/ppermute | solution.py:318
  26.1 7.9 %collective-permute-start.10 = (bf16[2,144,128]{2,1,0:T(8,128)(2,1)S(1)}, bf16[2,144,128]{2,1,0:T(8,128)(2,1)S(1)}, u32[]{:S(2)}, u32[]{:S(2)}) collective-permute-start(bf16[2,144,128]{2,1,0:T(8,128)(2,1)S(1)} %get-tuple-element.63), channel_id=1, source_target_pairs={{0,16},{4,20},{8,24},{12,28},{16,0},{20,4},{24,8},{28,12},{1,17},{... | collective-permute-start | bytes 221192 | tf_op jit(solution)/shard_map/ppermute | solution.py:318
  30.2 3.1 %collective-permute-start.13 = (f32[8,128]{1,0:T(8,128)S(1)}, f32[8,128]{1,0:T(8,128)S(1)}, u32[]{:S(2)}, u32[]{:S(2)}) collective-permute-start(f32[8,128]{1,0:T(8,128)S(1)} %get-tuple-element.70.l0), channel_id=1, source_target_pairs={{0,3},{1,2},{2,1},{3,0},{4,7},{5,6},{6,5},{7,4},{8,11},{9,10},{10,... | collective-permute-start | bytes 12296 | tf_op jit(solution)/shard_map/ppermute | solution.py:318
  30.3 3.7 %collective-permute-start.12 = (f32[8,128]{1,0:T(8,128)S(1)}, f32[8,128]{1,0:T(8,128)S(1)}, u32[]{:S(2)}, u32[]{:S(2)}) collective-permute-start(f32[8,128]{1,0:T(8,128)S(1)} %get-tuple-element.70.l0), channel_id=1, source_target_pairs={{0,2},{1,3},{2,0},{3,1},{4,6},{5,7},{6,4},{7,5},{8,10},{9,11},{10,... | collective-permute-start | bytes 12296 | tf_op jit(solution)/shard_map/ppermute | solution.py:318
  31.8 2.1 %collective-permute-start.11 = (f32[8,128]{1,0:T(8,128)S(1)}, f32[8,128]{1,0:T(8,128)S(1)}, u32[]{:S(2)}, u32[]{:S(2)}) collective-permute-start(f32[8,128]{1,0:T(8,128)S(1)} %get-tuple-element.70.l0), channel_id=1, source_target_pairs={{0,1},{1,0},{2,3},{3,2},{4,5},{5,4},{6,7},{7,6},{8,9},{9,8},{10,11... | collective-permute-start | bytes 12296 | tf_op jit(solution)/shard_map/ppermute | solution.py:318
  34.8 7.0 %collective-permute-start.14 = (bf16[272,128]{1,0:T(8,128)(2,1)S(1)}, bf16[272,128]{1,0:T(8,128)(2,1)S(1)}, u32[]{:S(2)}, u32[]{:S(2)}) collective-permute-start(bf16[272,128]{1,0:T(8,128)(2,1)S(1)} %shard_map.100.refs_0_), channel_id=1, source_target_pairs={{0,16},{4,20},{8,24},{12,28},{16,0},{20,4},{24,8},{28,12},{1,17},{... | collective-permute-start | bytes 208904 | tf_op jit(solution)/shard_map/ppermute | solution.py:318
  36.3 8.4 %collective-permute-start.7 = (bf16[2,128,128]{2,1,0:T(8,128)(2,1)S(1)}, bf16[2,128,128]{2,1,0:T(8,128)(2,1)S(1)}, u32[]{:S(2)}, u32[]{:S(2)}) collective-permute-start(bf16[2,128,128]{2,1,0:T(8,128)(2,1)S(1)} %get-tuple-element.60), channel_id=1, source_target_pairs={{0,4},{4,0},{8,12},{12,8},{16,20},{20,16},{24,28},{28,24},{1,5},{5... | collective-permute-start | bytes 196616 | tf_op jit(solution)/shard_map/ppermute | solution.py:318
  37.7 7.7 %collective-permute-start.8 = (bf16[2,128,128]{2,1,0:T(8,128)(2,1)S(1)}, bf16[2,128,128]{2,1,0:T(8,128)(2,1)S(1)}, u32[]{:S(2)}, u32[]{:S(2)}) collective-permute-start(bf16[2,128,128]{2,1,0:T(8,128)(2,1)S(1)} %get-tuple-element.61), channel_id=1, source_target_pairs={{0,8},{4,12},{8,0},{12,4},{16,24},{20,28},{24,16},{28,20},{1,9},{5... | collective-permute-start | bytes 196616 | tf_op jit(solution)/shard_map/ppermute | solution.py:318
  38.6 6.8 %collective-permute-start.9 = (bf16[2,128,128]{2,1,0:T(8,128)(2,1)S(1)}, bf16[2,128,128]{2,1,0:T(8,128)(2,1)S(1)}, u32[]{:S(2)}, u32[]{:S(2)}) collective-permute-start(bf16[2,128,128]{2,1,0:T(8,128)(2,1)S(1)} %get-tuple-element.62), channel_id=1, source_target_pairs={{0,12},{4,8},{8,4},{12,0},{16,28},{20,24},{24,20},{28,16},{1,13},{... | collective-permute-start | bytes 196616 | tf_op jit(solution)/shard_map/ppermute | solution.py:318
  41.9 5.3 %collective-permute-start.17 = (bf16[272,128]{1,0:T(8,128)(2,1)S(1)}, bf16[272,128]{1,0:T(8,128)(2,1)S(1)}, u32[]{:S(2)}, u32[]{:S(2)}) collective-permute-start(bf16[272,128]{1,0:T(8,128)(2,1)S(1)} %shard_map.101.g0), channel_id=1, source_target_pairs={{0,12},{4,8},{8,4},{12,0},{16,28},{20,24},{24,20},{28,16},{1,13},{... | collective-permute-start | bytes 208904 | tf_op jit(solution)/shard_map/ppermute | solution.py:318
  44.0 4.3 %collective-permute-start.16 = (bf16[272,128]{1,0:T(8,128)(2,1)S(1)}, bf16[272,128]{1,0:T(8,128)(2,1)S(1)}, u32[]{:S(2)}, u32[]{:S(2)}) collective-permute-start(bf16[272,128]{1,0:T(8,128)(2,1)S(1)} %shard_map.101.g0), channel_id=1, source_target_pairs={{0,8},{4,12},{8,0},{12,4},{16,24},{20,28},{24,16},{28,20},{1,9},{5... | collective-permute-start | bytes 208904 | tf_op jit(solution)/shard_map/ppermute | solution.py:318
  44.7 4.3 %collective-permute-start.15 = (bf16[272,128]{1,0:T(8,128)(2,1)S(1)}, bf16[272,128]{1,0:T(8,128)(2,1)S(1)}, u32[]{:S(2)}, u32[]{:S(2)}) collective-permute-start(bf16[272,128]{1,0:T(8,128)(2,1)S(1)} %shard_map.101.g0), channel_id=1, source_target_pairs={{0,4},{4,0},{8,12},{12,8},{16,20},{20,16},{24,28},{28,24},{1,5},{5... | collective-permute-start | bytes 208904 | tf_op jit(solution)/shard_map/ppermute | solution.py:318

commit v3 on v2

--- a/solution.py
+++ b/solution.py
@@ -11,7 +11,8 @@
 QUAD = 4
 F32 = jnp.float32
 BF16 = jnp.bfloat16
-KEY_US, OWN_US, GRAD_US, STUDENT_US = 20.0, 20.0, 20.0, 20.0
+SPREAD = (0, 3, 1, 2)
+KEY_US, OWN_US, GRAD_US, STUDENT_US = 20.0, 20.0, 0.2, 20.0
 
 
 def nt(a, b):
@@ -65,17 +66,12 @@
 
 
 def pack_kernel(*refs):
-    (x_ref, y_ref), outs, (held_x, held_y, wide, held, sems) = refs[:2], refs[2:-5], refs[-5:]
-    copies = [
-        pltpu.make_async_copy(src, dst, sems.at[n])
-        for n, (src, dst) in enumerate(((x_ref, held_x), (y_ref, held_y)))
-    ]
-    for copy in copies:
-        copy.start()
+    x_ref, outs, (wide, held) = refs[0], refs[-2 - QUAD : -2], refs[-2:]
     mine, _, _ = place_in_group()
-    for a, (copy, ref) in enumerate(zip(copies, (held_x, held_y))):
-        copy.wait()
-        tok, heads, d = ref.shape
+    tok, heads, d = x_ref.shape
+    tok = tok // 2
+    for a in range(2):
+        ref = x_ref.at[a * tok : (a + 1) * tok]
         per = heads // QUAD
         wide[a] = ref[...].astype(F32).reshape(tok * heads, d)
         for h in range(heads):
@@ -84,10 +80,19 @@
         out[...] = held[lax.bitwise_xor(mine, j)]
 
 
+def put_loss(out_ref, first, loss):
+    high, low = split2(loss)
+    out_ref[first:] = jnp.concatenate([high, low], axis=0)
+
+
+def take_loss(ref, first):
+    return ref[first : first + 8].astype(F32) + ref[first + 8 : first + 16].astype(F32)
+
+
 def key_kernel(c0, c1, c2, c3, wk_ref, kv_ref, msg_ref):
     mine, _, _ = place_in_group()
     narr, per, tok, d = c0.shape
-    for j, c in enumerate((c0, c1, c2, c3)):
+    for j, c in zip(SPREAD, (c0, c1, c2, c3)):
         kv_ref[:, :, lax.bitwise_xor(mine, j)] = c[...]
     total = QUAD * tok
     for hh in range(per):
@@ -103,12 +108,12 @@
         msg_ref[hh, rows + WIN :] = v[total - WIN :]
 
 
-def own_kernel(kv_ref, c0, c1, c2, c3, wq_ref, wk_ref, qt_ref, win_ref, top_ref, lin_ref, fq_ref, up_ref, down_ref):
+def own_kernel(kv_ref, c0, c1, c2, c3, wq_ref, wk_ref, qt_ref, teach_ref, win_ref, top_ref, lin_ref, fq_ref, up_ref, down_ref):
     mine, _, _ = place_in_group()
     narr, per, tok, d = c0.shape
     total = QUAD * tok
     scale = 1.0 / d**0.5
-    for j, c in enumerate((c0, c1, c2, c3)):
+    for j, c in zip(SPREAD, (c0, c1, c2, c3)):
         qt_ref[:, :, lax.bitwise_xor(mine, j)] = c[...]
     row = lax.broadcasted_iota(jnp.int32, (tok + WIN, tok), 0)
     col = lax.broadcasted_iota(jnp.int32, (tok + WIN, tok), 1)
@@ -143,9 +148,10 @@
             last = jnp.where(causal, amat[lo:], 0.0)
             amat = jnp.concatenate([amat[:lo], last], axis=0).astype(BF16) if b else last.astype(BF16)
             lin_ref[hh, :, lo:hi] = nn(vt[:, :hi], amat)
-
-
-def out_kernel(qt_ref, win_ref, top_ref, lin_ref, fq_ref, msg_ref, wk_ref, out_ref, later_ref, grad_ref, loss_ref):
+            teach_ref[hh, :, lo:hi] = transposed(qt_ref[1, hh, b])
+
+
+def out_kernel(qt_ref, teach_ref, win_ref, top_ref, lin_ref, fq_ref, msg_ref, wk_ref, s0, s1, s2, s3, later_ref, grad_ref, loss_ref, outs):
     mine, has_past, _ = place_in_group()
     narr, per, _, tok, d = qt_ref.shape
     total = QUAD * tok
@@ -179,9 +185,10 @@
         both = win_scale * win + lin_scale * lin
         inverse = 1.0 / both[d : d + 1]
         out = both[:d] * inverse
-        out_ref[hh] = out.astype(BF16)
-        teach = jnp.concatenate([transposed(qt_ref[1, hh, b]) for b in range(QUAD)], axis=1)
-        diff = out - teach
+        out_rows = out.astype(BF16)
+        for b in range(QUAD):
+            outs[b, hh] = transposed(out_rows[:, b * tok : (b + 1) * tok]).astype(BF16)
+        diff = out - teach_ref[hh]
         loss = loss + jnp.sum((diff * diff).reshape(d // 8, 8, total), axis=0)
         g = diff * (2.0 / d)
         coef = lin_scale * inverse
@@ -191,12 +198,14 @@
         g_ext = jnp.concatenate([g_num, jnp.where(pad == 0, g_den, 0.0)], axis=0).astype(BF16)
         grad_ref[hh] = g_ext
         later_ref[hh] = nt(g_ext, fq).astype(BF16)
+    loss = sum(loss[:, b * tok : (b + 1) * tok] for b in range(QUAD))
     loss_ref[...] = loss
-
-
-def grad_kernel(kv_ref, qt_ref, msg_ref, grad_ref, out_ref, fq_ref, qup_ref, qdown_ref, wk_ref, diff_ref,
-                s0, s1, s2, s3, gq_ref, gk_ref, k_ref, v_ref, kup_ref, kdown_ref, loss_ref, outs):
-    loss_ref[...] = sum(diff_ref[:, b * loss_ref.shape[1] : (b + 1) * loss_ref.shape[1]] for b in range(QUAD))
+    for j, s in enumerate((s0, s1, s2, s3)):
+        s[...] = outs[lax.bitwise_xor(mine, j)]
+
+
+def grad_kernel(kv_ref, qt_ref, msg_ref, grad_ref, fq_ref, qup_ref, qdown_ref, wk_ref,
+                gq_ref, gk_ref, k_ref, v_ref, kup_ref, kdown_ref):
     mine, has_past, _ = place_in_group()
     narr, per, _, tok, d = qt_ref.shape
     total = QUAD * tok
@@ -232,19 +241,6 @@
         ):
             high, low = split2(phi_pull(ups, downs, grad))
             ref[hh] = nn(high, x) + nn(low, x)
-        for b in range(QUAD):
-            outs[b, hh] = transposed(out_ref[hh, :, b * tok : (b + 1) * tok]).astype(BF16)
-    for j, s in enumerate((s0, s1, s2, s3)):
-        s[...] = outs[lax.bitwise_xor(mine, j)]
-
-
-def put_loss(out_ref, first, loss):
-    high, low = split2(loss)
-    out_ref[first:] = jnp.concatenate([high, low], axis=0)
-
-
-def take_loss(ref, first):
-    return ref[first : first + 8].astype(F32) + ref[first + 8 : first + 16].astype(F32)
 
 
 def last_kernel(later_ref, k_ref, v_ref, kup_ref, kdown_ref, gq_ref, gk_ref, l0, l1, l2, l3, out_ref):
@@ -316,6 +312,10 @@
 
 def flip(x, axis, by):
     return lax.ppermute(x, axis, [(i, i ^ by) for i in range(lax.axis_size(axis))])
+
+
+def spread(parts):
+    return [flip(parts[j], "ctx", j) if j else parts[j] for j in SPREAD]
 
 
 def state_over_groups(msg, d, wk_pair, group, groups, members):
@@ -364,18 +364,14 @@
     pack = call(
         pack_kernel, [block] * QUAD,
         [
-            pltpu.VMEM((tok, heads, d), BF16),
-            pltpu.VMEM((tok, heads, d), BF16),
             pltpu.VMEM((2, tok * heads, d), F32),
             pltpu.VMEM((QUAD, 2, per, tok, d), BF16),
-            pltpu.SemaphoreType.DMA((2,)),
         ],
-        ins=2, space=pltpu.HBM,
+        ins=1,
     )
-    kv = pack(keys, values)
-    kv = [kv[0]] + [flip(kv[j], "ctx", j) for j in range(1, QUAD)]
-    qt = pack(queries, teacher)
-    qt = [qt[0]] + [flip(qt[j], "ctx", j) for j in range(1, QUAD)]
+    kv = pack(jnp.concatenate([keys, values]))
+    kv = spread(kv)
+    qt = spread(pack(jnp.concatenate([queries, teacher])))
 
     rows = d + 16 + 2 * WIN
     kv, msg = call(
@@ -389,38 +385,40 @@
     sums = shape(per, d + 16, total, dtype=F32)
     part = shape(per, half, total, dtype=F32)
     grad = shape(per, half, d, dtype=F32)
-    qt, win, top, lin, fq, q_up, q_down = call(
+    qt, teach, win, top, lin, fq, q_up, q_down = call(
         own_kernel,
-        [shape(2, per, QUAD, tok, d), sums, shape(per, 8, total, dtype=F32), sums,
+        [shape(2, per, QUAD, tok, d), shape(per, d, total, dtype=F32), sums, shape(per, 8, total, dtype=F32), sums,
          shape(per, 2 * half, total), part, part],
         ins=7, micros=OWN_US,
     )(kv, *qt, wq, wk)
-    out, later, g_out, squares = call(
+    block = shape(per, tok, d)
+    s0, s1, s2, s3, later, g_out, loss = call(
         out_kernel,
-        [shape(per, d, total), shape(per, d + 16, 2 * half), shape(per, d + 16, total), shape(8, total, dtype=F32)],
-        ins=7, micros=2.0,
-    )(qt, win, top, lin, fq, msg, wk)
+        [block] * QUAD + [shape(per, d + 16, 2 * half), shape(per, d + 16, total), shape(8, tok, dtype=F32)],
+        [pltpu.VMEM((QUAD, per, tok, d), BF16)],
+        ins=8, micros=2.0,
+    )(qt, teach, win, top, lin, fq, msg, wk)
     later = later_over_groups(later, group, groups, members)
-    *out, gq, gk, k, v, k_up, k_down, loss = call(
+    s1, s2, s3 = [flip(s, "ctx", j) for j, s in ((1, s1), (2, s2), (3, s3))]
+    losses = [loss] + [flip(loss, "head", j) for j in range(1, lax.axis_size("head"))]
+    gq, gk, k, v, k_up, k_down = call(
         grad_kernel,
-        [shape(per, tok, d)] * QUAD + [grad, grad, shape(per, total, d), shape(per, total, d), part, part,
-         shape(8, tok, dtype=F32)],
-        [pltpu.VMEM((QUAD, per, tok, d), BF16)],
-        ins=10, micros=GRAD_US,
-    )(kv, qt, msg, g_out, out, fq, q_up, q_down, wk, squares)
-    losses = [loss] + [flip(loss, "head", j) for j in range(1, lax.axis_size("head"))]
+        [grad, grad, shape(per, total, d), shape(per, total, d), part, part],
+        ins=8, micros=GRAD_US,
+    )(kv, qt, msg, g_out, fq, q_up, q_down, wk)
     rows = 2 * per * half + 16
-    grads = call(last_kernel, shape(rows, d), ins=11)(later, k, v, k_up, k_down, gq, gk, *losses)
+    grads = call(last_kernel, shape(rows, d), ins=11)(
+        later, k, v, k_up, k_down, gq, gk, *losses
+    )
     grads = sum_over_groups(grads, groups, members)
     grads = call(sum_kernel, shape(rows, d), ins=len(grads))(*grads)
     grads = [grads] + [flip(grads, "ctx", j) for j in range(1, QUAD)]
-    out = [out[0]] + [flip(out[j], "ctx", j) for j in range(1, QUAD)]
     entries = tok * shards * heads * lax.axis_size("head") * d
     student = call(
         student_kernel, shape(tok, heads, d),
         [pltpu.VMEM((QUAD, per, tok, d), BF16), pltpu.VMEM((tok * heads, d), F32)],
         ins=4, micros=STUDENT_US,
-    )(*out)
+    )(s0, s1, s2, s3)
     whole = shape(heads, half, d, dtype=F32)
     loss, grad_q, grad_k = call(
         functools.partial(finish_kernel, entries), [shape(1, 1, dtype=F32), whole, whole], ins=4

time: 50 us -> 47.1 us (0.942)
  waiting for transfers between devices: 12.4 us -> 10.3 us
  local copies, waits for them, and re-layouts: 1.91 us -> 0.02 us
  other arithmetic: 0 us -> 1.12 us
    ppermute x18, waiting for transfers between devices: 12.4 us -> 10.3 us  [flip(): lax.ppermute(x, axis, [(i, i ^ by) for i in range(lax.axis_size(axis))])]
    unnamed x12 -> x8, local copies, waits for them, and re-layouts: 1.91 us -> 0.02 us
    concatenate x0 -> x2, other arithmetic: none -> 1.12 us  [the longest x1 1.08 us: per_device(): kv = pack(jnp.concatenate([keys, values]))]
  transfers between devices with their start and end apart: 18 -> 18, of which waited for: 10 -> 9; matrix products, arithmetic and copies ran while one was open for 0% -> 0% of each run, Pallas kernels for 15% -> 16%
where the time goes in v3:
time: 47.1 us; the launch traced here: 46.9 us
  starting transfers between devices  23.7 us (50%)
  Pallas kernels  11.1 us (24%)
  waiting for transfers between devices  10.3 us (22%)
  other arithmetic  1.12 us (2%)
  between operations  0.75 us (2%)
    ppermute x18, starting transfers between devices, flip(): lax.ppermute(x, axis, [(i, i ^ by) for i in range(lax.axis_size(axis))])  23.7 us
    ppermute x18, waiting for transfers between devices, flip(): lax.ppermute(x, axis, [(i, i ^ by) for i in range(lax.axis_size(axis))])  10.3 us
    pallas_call x1, Pallas kernels, per_device(): call(own_kernel, [shape(2, per, QUAD, tok, d), shape(per, d, total, dtype...  3.09 us
    pallas_call x1, Pallas kernels, per_device(): call(grad_kernel, [grad, grad, shape(per, total, d), shape(per, total, d)...  2.33 us
    pallas_call x1, Pallas kernels, per_device(): call(out_kernel, [block] * QUAD + [shape(per, d + 16, 2 * half), shape(pe...  1.87 us
    concatenate x1, other arithmetic, per_device(): kv = pack(jnp.concatenate([keys, values]))  1.08 us
  transfers between devices with their start and end apart: 18, of which 9 were waited for; matrix products, arithmetic and copies ran while one was open for 0% of the time, Pallas kernels for 16%

profile of v3, /device:TPU:0, one launch (start us, length us, event | category | flops | bytes accessed | tf_op | source)
XLA Modules:
  0.0 46.9 jit_solution(4441402764059392199)
XLA Ops:
  0.6 1.1 %pad_maximum_fusion.refs_0_ = bf16[256,8,128]{2,1,0:T(8,128)(2,1)S(1)} fusion(bf16[128,8,128]{2,1,0:T(8,128)(2,1)} %param.8, bf16[128,8,128]{2,1,0:T(8,128)(2,1)} %param.7), kind=kLoop, calls=%fused_computation | loop fusion | flops 262144 | bytes 1048576 | tf_op jit(solution)/shard_map/concatenate | solution.py:372
  1.7 0.0 copy-start.2
  1.7 0.0 copy-start.3
  1.7 0.3 shard_map.93
  2.0 4.0 %collective-permute-start = (bf16[2,2,128,128]{3,2,1,0:T(8,128)(2,1)S(1)}, bf16[2,2,128,128]{3,2,1,0:T(8,128)(2,1)S(1)}, u32[]{:S(2)}, u32[]{:S(2)}) collective-permute-start(bf16[2,2,128,128]{3,2,1,0:T(8,128)(2,1)S(1)} %get-tuple-element.39), channel_id=1, source_target_pairs={{0,12},{4,8},{8,4},{12,0},{16,28},{20,24},{24,20},{28,16},{1,13},{... | collective-permute-start | bytes 393224 | tf_op jit(solution)/shard_map/ppermute | solution.py:314
  6.1 0.5 %collective-permute-start.1 = (bf16[2,2,128,128]{3,2,1,0:T(8,128)(2,1)S(1)}, bf16[2,2,128,128]{3,2,1,0:T(8,128)(2,1)S(1)}, u32[]{:S(2)}, u32[]{:S(2)}) collective-permute-start(bf16[2,2,128,128]{3,2,1,0:T(8,128)(2,1)S(1)} %get-tuple-element.40), channel_id=1, source_target_pairs={{0,4},{4,0},{8,12},{12,8},{16,20},{20,16},{24,28},{28,24},{1,5},{5... | collective-permute-start | bytes 393224 | tf_op jit(solution)/shard_map/ppermute | solution.py:314
  6.6 0.1 collective-permute-start.2
  6.7 0.0 copy-done.2
  6.7 0.0 copy-done.3
  6.8 0.0 copy-start
  6.8 0.3 shard_map.95
  7.0 2.9 %collective-permute-start.3 = (bf16[2,2,128,128]{3,2,1,0:T(8,128)(2,1)S(1)}, bf16[2,2,128,128]{3,2,1,0:T(8,128)(2,1)S(1)}, u32[]{:S(2)}, u32[]{:S(2)}) collective-permute-start(bf16[2,2,128,128]{3,2,1,0:T(8,128)(2,1)S(1)} %get-tuple-element.44), channel_id=1, source_target_pairs={{0,12},{4,8},{8,4},{12,0},{16,28},{20,24},{24,20},{28,16},{1,13},{... | collective-permute-start | bytes 393224 | tf_op jit(solution)/shard_map/ppermute | solution.py:314
  9.9 0.5 %collective-permute-start.4 = (bf16[2,2,128,128]{3,2,1,0:T(8,128)(2,1)S(1)}, bf16[2,2,128,128]{3,2,1,0:T(8,128)(2,1)S(1)}, u32[]{:S(2)}, u32[]{:S(2)}) collective-permute-start(bf16[2,2,128,128]{3,2,1,0:T(8,128)(2,1)S(1)} %get-tuple-element.45), channel_id=1, source_target_pairs={{0,4},{4,0},{8,12},{12,8},{16,20},{20,16},{24,28},{28,24},{1,5},{5... | collective-permute-start | bytes 393224 | tf_op jit(solution)/shard_map/ppermute | solution.py:314
  10.5 0.0 collective-permute-done.c1
  10.5 1.9 %collective-permute-start.5 = (bf16[2,2,128,128]{3,2,1,0:T(8,128)(2,1)S(1)}, bf16[2,2,128,128]{3,2,1,0:T(8,128)(2,1)S(1)}, u32[]{:S(2)}, u32[]{:S(2)}) collective-permute-start(bf16[2,2,128,128]{3,2,1,0:T(8,128)(2,1)S(1)} %get-tuple-element.46), channel_id=1, source_target_pairs={{0,8},{4,12},{8,0},{12,4},{16,24},{20,28},{24,16},{28,20},{1,9},{5... | collective-permute-start | bytes 393224 | tf_op jit(solution)/shard_map/ppermute | solution.py:314
  12.4 1.5 %collective-permute-done.1.c2 = bf16[2,2,128,128]{3,2,1,0:T(8,128)(2,1)S(1)} collective-permute-done((bf16[2,2,128,128]{3,2,1,0:T(8,128)(2,1)S(1)}, bf16[2,2,128,128]{3,2,1,0:T(8,128)(2,1)S(1)}, u32[]{:S(2)}, u32[]{:S(2)}) %collective-permute-start.1) | collective-permute-done | bytes 131104 | tf_op jit(solution)/shard_map/ppermute | solution.py:314
  13.9 0.0 collective-permute-done.2.c3
  13.9 0.0 copy-done
  13.9 0.0 copy-start.1
  13.9 0.7 %shard_map.94 = (bf16[2,2,4,128,128]{4,3,2,1,0:T(8,128)(2,1)S(1)}, bf16[2,272,128]{2,1,0:T(8,128)(2,1)S(1)}) custom-call(bf16[2,2,128,128]{3,2,1,0:T(8,128)(2,1)S(1)} %get-tuple-element.38.c0, bf16[2,2,128,128]{3,2,1,0:T(8,128)(2,1)S(1)} %collective-permute-done.c1, bf16[2,2,128,128]{3,2,1,0:T(8,128)(2,1)S(1)} %collective-permute-done.1.c2, ...), custom_call_target="tpu_custom_call" | custom-call | flops 20000000000 | tf_op jit(solution)/shard_map/pallas_call | solution.py:377
  14.5 2.8 %collective-permute-start.6 = (bf16[2,272,128]{2,1,0:T(8,128)(2,1)S(1)}, bf16[2,272,128]{2,1,0:T(8,128)(2,1)S(1)}, u32[]{:S(2)}, u32[]{:S(2)}) collective-permute-start(bf16[2,272,128]{2,1,0:T(8,128)(2,1)S(1)} %get-tuple-element.53), channel_id=1, source_target_pairs={{0,16},{4,20},{8,24},{12,28},{16,0},{20,4},{24,8},{28,12},{1,17},{... | collective-permute-start | bytes 417800 | tf_op jit(solution)/shard_map/ppermute | solution.py:314
  17.3 0.0 collective-permute-done.3.c1
  17.3 0.7 %collective-permute-done.4.c2 = bf16[2,2,128,128]{3,2,1,0:T(8,128)(2,1)S(1)} collective-permute-done((bf16[2,2,128,128]{3,2,1,0:T(8,128)(2,1)S(1)}, bf16[2,2,128,128]{3,2,1,0:T(8,128)(2,1)S(1)}, u32[]{:S(2)}, u32[]{:S(2)}) %collective-permute-start.4) | collective-permute-done | bytes 131104 | tf_op jit(solution)/shard_map/ppermute | solution.py:314
  18.0 0.2 collective-permute-done.5.c3
  18.1 0.0 copy-done.1
  18.2 3.1 %shard_map.96 = (bf16[2,2,4,128,128]{4,3,2,1,0:T(8,128)(2,1)S(1)}, f32[2,128,512]{2,1,0:T(8,128)S(1)}, f32[2,144,512]{2,1,0:T(8,128)S(1)}, f32[2,8,512]{2,1,0:T(...) custom-call(bf16[2,2,4,128,128]{4,3,2,1,0:T(8,128)(2,1)S(1)} %get-tu, ...), custom_call_target="tpu_custom_call" | custom-call | flops 20000000000 | tf_op jit(solution)/shard_map/pallas_call | solution.py:388
  21.3 2.8 %collective-permute-done.6.msg_ref = bf16[2,272,128]{2,1,0:T(8,128)(2,1)S(1)} collective-permute-done((bf16[2,272,128]{2,1,0:T(8,128)(2,1)S(1)}, bf16[2,272,128]{2,1,0:T(8,128)(2,1)S(1)}, u32[]{:S(2)}, u32[]{:S(2)}) %collective-permute-start.6) | collective-permute-done | bytes 139296 | tf_op jit(solution)/shard_map/ppermute | solution.py:314
  24.0 1.9 %shard_map.97 = (bf16[2,128,128]{2,1,0:T(8,128)(2,1)S(1)}, bf16[2,128,128]{2,1,0:T(8,128)(2,1)S(1)}, bf16[2,128,128]{2,1,0:T(8,128)(2,1)S(1)}, bf16[2,128,128]{2...) custom-call(bf16[2,2,4,128,128]{4,3,2,1,0:T(8,128)(2,1)S(1)} %get-tu, ...), custom_call_target="tpu_custom_call" | custom-call | flops 2000000000 | tf_op jit(solution)/shard_map/pallas_call | solution.py:395
  25.9 1.0 %collective-permute-start.10 = (bf16[2,144,128]{2,1,0:T(8,128)(2,1)S(1)}, bf16[2,144,128]{2,1,0:T(8,128)(2,1)S(1)}, u32[]{:S(2)}, u32[]{:S(2)}) collective-permute-start(bf16[2,144,128]{2,1,0:T(8,128)(2,1)S(1)} %get-tuple-element.58), channel_id=1, source_target_pairs={{0,16},{4,20},{8,24},{12,28},{16,0},{20,4},{24,8},{28,12},{1,17},{... | collective-permute-start | bytes 221192 | tf_op jit(solution)/shard_map/ppermute | solution.py:314
  26.9 0.0 collective-permute-start.13
  26.9 1.5 %collective-permute-start.12 = (f32[8,128]{1,0:T(8,128)S(1)}, f32[8,128]{1,0:T(8,128)S(1)}, u32[]{:S(2)}, u32[]{:S(2)}) collective-permute-start(f32[8,128]{1,0:T(8,128)S(1)} %get-tuple-element.68.l0), channel_id=1, source_target_pairs={{0,2},{1,3},{2,0},{3,1},{4,6},{5,7},{6,4},{7,5},{8,10},{9,11},{10,... | collective-permute-start | bytes 12296 | tf_op jit(solution)/shard_map/ppermute | solution.py:314
  28.4 0.3 collective-permute-start.11
  28.8 2.3 %shard_map.99 = (f32[2,64,128]{2,1,0:T(8,128)S(1)}, f32[2,64,128]{2,1,0:T(8,128)S(1)}, bf16[2,512,128]{2,1,0:T(8,128)(2,1)S(1)}, bf16[2,512,128]{2,1,0:T(8,128)(...) custom-call(bf16[2,2,4,128,128]{4,3,2,1,0:T(8,128)(2,1)S(1)} %get-tuple-element.42.kv_ref, ...), custom_call_target="tpu_custom_call" | custom-call | flops 200000000 | tf_op jit(solution)/shard_map/pallas_call | solution.py:404
  31.1 0.0 collective-permute-done.13.l3
  31.1 0.0 collective-permute-done.12.l2
  31.1 0.0 collective-permute-done.11.l1
  31.2 1.1 %collective-permute-done.10.later_ref = bf16[2,144,128]{2,1,0:T(8,128)(2,1)S(1)} collective-permute-done((bf16[2,144,128]{2,1,0:T(8,128)(2,1)S(1)}, bf16[2,144,128]{2,1,0:T(8,128)(2,1)S(1)}, u32[]{:S(2)}, u32[]{:S(2)}) %collective-permute-start.10) | collective-permute-done | bytes 73760 | tf_op jit(solution)/shard_map/ppermute | solution.py:314
  32.3 0.8 %shard_map.100.refs_0_ = bf16[272,128]{1,0:T(8,128)(2,1)S(1)} custom-call(bf16[2,144,128]{2,1,0:T(8,128)(2,1)S(1)} %collective-permute-done.10.later_ref, bf16[2,512,128]{2,1,0:T(8,128)(2,1)S(1)} %get-tuple-element.62.k_ref, bf16[2,512,128]{2,1,0:T(8,128)(2,1)S(1)} %get-tuple-element.63.v_ref, f32[2,64,512]{2,1,0:T(8,128)S(1)} %get-tuple-element.64.kup_ref, ...), custom_call_target="tpu_custom_call" | custom-call | flops 1000000000 | tf_op jit(solution)/shard_map/pallas_call | solution.py:410
  33.2 0.9 %collective-permute-start.14 = (bf16[272,128]{1,0:T(8,128)(2,1)S(1)}, bf16[272,128]{1,0:T(8,128)(2,1)S(1)}, u32[]{:S(2)}, u32[]{:S(2)}) collective-permute-start(bf16[272,128]{1,0:T(8,128)(2,1)S(1)} %shard_map.100.refs_0_), channel_id=1, source_target_pairs={{0,16},{4,20},{8,24},{12,28},{16,0},{20,4},{24,8},{28,12},{1,17},{... | collective-permute-start | bytes 208904 | tf_op jit(solution)/shard_map/ppermute | solution.py:314
  34.1 1.2 %collective-permute-start.7 = (bf16[2,128,128]{2,1,0:T(8,128)(2,1)S(1)}, bf16[2,128,128]{2,1,0:T(8,128)(2,1)S(1)}, u32[]{:S(2)}, u32[]{:S(2)}) collective-permute-start(bf16[2,128,128]{2,1,0:T(8,128)(2,1)S(1)} %get-tuple-element.55), channel_id=1, source_target_pairs={{0,4},{4,0},{8,12},{12,8},{16,20},{20,16},{24,28},{28,24},{1,5},{5... | collective-permute-start | bytes 196616 | tf_op jit(solution)/shard_map/ppermute | solution.py:314
  35.2 1.0 %collective-permute-start.8 = (bf16[2,128,128]{2,1,0:T(8,128)(2,1)S(1)}, bf16[2,128,128]{2,1,0:T(8,128)(2,1)S(1)}, u32[]{:S(2)}, u32[]{:S(2)}) collective-permute-start(bf16[2,128,128]{2,1,0:T(8,128)(2,1)S(1)} %get-tuple-element.56), channel_id=1, source_target_pairs={{0,8},{4,12},{8,0},{12,4},{16,24},{20,28},{24,16},{28,20},{1,9},{5... | collective-permute-start | bytes 196616 | tf_op jit(solution)/shard_map/ppermute | solution.py:314
  36.2 1.4 %collective-permute-start.9 = (bf16[2,128,128]{2,1,0:T(8,128)(2,1)S(1)}, bf16[2,128,128]{2,1,0:T(8,128)(2,1)S(1)}, u32[]{:S(2)}, u32[]{:S(2)}) collective-permute-start(bf16[2,128,128]{2,1,0:T(8,128)(2,1)S(1)} %get-tuple-element.57), channel_id=1, source_target_pairs={{0,12},{4,8},{8,4},{12,0},{16,28},{20,24},{24,20},{28,16},{1,13},{... | collective-permute-start | bytes 196616 | tf_op jit(solution)/shard_map/ppermute | solution.py:314
  37.6 1.9 %collective-permute-done.14.refs_1_ = bf16[272,128]{1,0:T(8,128)(2,1)S(1)} collective-permute-done((bf16[272,128]{1,0:T(8,128)(2,1)S(1)}, bf16[272,128]{1,0:T(8,128)(2,1)S(1)}, u32[]{:S(2)}, u32[]{:S(2)}) %collective-permute-start.14) | collective-permute-done | bytes 69664 | tf_op jit(solution)/shard_map/ppermute | solution.py:314
  39.5 0.2 collective-permute-start.17
  39.7 2.1 %collective-permute-start.16 = (bf16[272,128]{1,0:T(8,128)(2,1)S(1)}, bf16[272,128]{1,0:T(8,128)(2,1)S(1)}, u32[]{:S(2)}, u32[]{:S(2)}) collective-permute-start(bf16[272,128]{1,0:T(8,128)(2,1)S(1)} %shard_map.101.g0), channel_id=1, source_target_pairs={{0,8},{4,12},{8,0},{12,4},{16,24},{20,28},{24,16},{28,20},{1,9},{5... | collective-permute-start | bytes 208904 | tf_op jit(solution)/shard_map/ppermute | solution.py:314
  41.8 0.0 collective-permute-done.7.s1
  41.8 1.2 %collective-permute-start.15 = (bf16[272,128]{1,0:T(8,128)(2,1)S(1)}, bf16[272,128]{1,0:T(8,128)(2,1)S(1)}, u32[]{:S(2)}, u32[]{:S(2)}) collective-permute-start(bf16[272,128]{1,0:T(8,128)(2,1)S(1)} %shard_map.101.g0), channel_id=1, source_target_pairs={{0,4},{4,0},{8,12},{12,8},{16,20},{20,16},{24,28},{28,24},{1,5},{5... | collective-permute-start | bytes 208904 | tf_op jit(solution)/shard_map/ppermute | solution.py:314
  43.0 0.0 collective-permute-done.8.s2
  43.0 0.0 collective-permute-done.9.s3
  43.1 0.9 %shard_map.98 = bf16[128,8,128]{2,1,0:T(8,128)(2,1)} custom-call(bf16[2,128,128]{2,1,0:T(8,128)(2,1)S(1)} %get-tuple-element.54.s0, bf16[2,128,128]{2,1,0:T(8,128)(2,1)S(1)} %collective-permute-done.7.s1, bf16[2,128,128]{2,1,0:T(8,128)(2,1)S(1)} %collective-permute-done.8.s2, bf16[2,128,128]{2,1,0:T(8,128)(2,1)S(1)} %collective-permute-done.9.s3), custom_call_target="tpu_custom_call" | custom-call | flops 20000000000 | tf_op jit(solution)/shard_map/pallas_call | solution.py:417
  43.9 0.8 %collective-permute-done.17.g3 = bf16[272,128]{1,0:T(8,128)(2,1)S(1)} collective-permute-done((bf16[272,128]{1,0:T(8,128)(2,1)S(1)}, bf16[272,128]{1,0:T(8,128)(2,1)S(1)}, u32[]{:S(2)}, u32[]{:S(2)}) %collective-permute-start.17) | collective-permute-done | bytes 69664 | tf_op jit(solution)/shard_map/ppermute | solution.py:314
  44.8 0.1 collective-permute-done.16.g2
  44.8 1.3 %collective-permute-done.15.g1 = bf16[272,128]{1,0:T(8,128)(2,1)S(1)} collective-permute-done((bf16[272,128]{1,0:T(8,128)(2,1)S(1)}, bf16[272,128]{1,0:T(8,128)(2,1)S(1)}, u32[]{:S(2)}, u32[]{:S(2)}) %collective-permute-start.15) | collective-permute-done | bytes 69664 | tf_op jit(solution)/shard_map/ppermute | solution.py:314
  46.1 0.8 %shard_map.102 = (f32[1,1]{1,0:T(1,128)}, f32[8,64,128]{2,1,0:T(8,128)}, f32[8,64,128]{2,1,0:T(8,128)}) custom-call(bf16[272,128]{1,0:T(8,128)(2,1)S(1)} %shard_map.101.g0, bf16[272,128]{1,0:T(8,128)(2,1)S(1)} %collective-permute-done.15.g1, bf16[272,128]{1,0:T(8,128)(2,1)S(1)} %collective-permute-done.16.g2, bf16[272,128]{1,0:T(8,128)(2,1)S(1)} %collective-permute-done.17.g3), custom_call_target="tpu_custom_call" | custom-call | flops 1000000000 | tf_op jit(solution)/shard_map/pallas_call | solution.py:423
  (2 shorter events, 0.1 us)
Async XLA Ops:
  1.7 5.0 %copy-start.2 = (bf16[128,8,128]{2,1,0:T(8,128)(2,1)S(1)}, bf16[128,8,128]{2,1,0:T(8,128)(2,1)}, u32[]{:S(2)}) copy-start(bf16[128,8,128]{2,1,0:T(8,128)(2,1)} %param.9) | copy-start | bytes 786436
  1.7 5.0 %copy-start.3 = (bf16[128,8,128]{2,1,0:T(8,128)(2,1)S(1)}, bf16[128,8,128]{2,1,0:T(8,128)(2,1)}, u32[]{:S(2)}) copy-start(bf16[128,8,128]{2,1,0:T(8,128)(2,1)} %param.6) | copy-start | bytes 786436
  2.0 8.4 %collective-permute-start = (bf16[2,2,128,128]{3,2,1,0:T(8,128)(2,1)S(1)}, bf16[2,2,128,128]{3,2,1,0:T(8,128)(2,1)S(1)}, u32[]{:S(2)}, u32[]{:S(2)}) collective-permute-start(bf16[2,2,128,128]{3,2,1,0:T(8,128)(2,1)S(1)} %get-tuple-element.39), channel_id=1, source_target_pairs={{0,12},{4,8},{8,4},{12,0},{16,28},{20,24},{24,20},{28,16},{1,13},{... | collective-permute-start | bytes 393224 | tf_op jit(solution)/shard_map/ppermute | solution.py:314
  6.1 7.8 %collective-permute-start.1 = (bf16[2,2,128,128]{3,2,1,0:T(8,128)(2,1)S(1)}, bf16[2,2,128,128]{3,2,1,0:T(8,128)(2,1)S(1)}, u32[]{:S(2)}, u32[]{:S(2)}) collective-permute-start(bf16[2,2,128,128]{3,2,1,0:T(8,128)(2,1)S(1)} %get-tuple-element.40), channel_id=1, source_target_pairs={{0,4},{4,0},{8,12},{12,8},{16,20},{20,16},{24,28},{28,24},{1,5},{5... | collective-permute-start | bytes 393224 | tf_op jit(solution)/shard_map/ppermute | solution.py:314
  6.6 7.3 %collective-permute-start.2 = (bf16[2,2,128,128]{3,2,1,0:T(8,128)(2,1)S(1)}, bf16[2,2,128,128]{3,2,1,0:T(8,128)(2,1)S(1)}, u32[]{:S(2)}, u32[]{:S(2)}) collective-permute-start(bf16[2,2,128,128]{3,2,1,0:T(8,128)(2,1)S(1)} %get-tuple-element.41), channel_id=1, source_target_pairs={{0,8},{4,12},{8,0},{12,4},{16,24},{20,28},{24,16},{28,20},{1,9},{5... | collective-permute-start | bytes 393224 | tf_op jit(solution)/shard_map/ppermute | solution.py:314
  6.8 7.1 %copy-start = (bf16[8,64,128]{2,1,0:T(8,128)(2,1)S(1)}, bf16[8,64,128]{2,1,0:T(8,128)(2,1)}, u32[]{:S(2)}) copy-start(bf16[8,64,128]{2,1,0:T(8,128)(2,1)} %wk_ref.7) | copy-start | bytes 393220
  7.0 10.3 %collective-permute-start.3 = (bf16[2,2,128,128]{3,2,1,0:T(8,128)(2,1)S(1)}, bf16[2,2,128,128]{3,2,1,0:T(8,128)(2,1)S(1)}, u32[]{:S(2)}, u32[]{:S(2)}) collective-permute-start(bf16[2,2,128,128]{3,2,1,0:T(8,128)(2,1)S(1)} %get-tuple-element.44), channel_id=1, source_target_pairs={{0,12},{4,8},{8,4},{12,0},{16,28},{20,24},{24,20},{28,16},{1,13},{... | collective-permute-start | bytes 393224 | tf_op jit(solution)/shard_map/ppermute | solution.py:314
  9.9 8.0 %collective-permute-start.4 = (bf16[2,2,128,128]{3,2,1,0:T(8,128)(2,1)S(1)}, bf16[2,2,128,128]{3,2,1,0:T(8,128)(2,1)S(1)}, u32[]{:S(2)}, u32[]{:S(2)}) collective-permute-start(bf16[2,2,128,128]{3,2,1,0:T(8,128)(2,1)S(1)} %get-tuple-element.45), channel_id=1, source_target_pairs={{0,4},{4,0},{8,12},{12,8},{16,20},{20,16},{24,28},{28,24},{1,5},{5... | collective-permute-start | bytes 393224 | tf_op jit(solution)/shard_map/ppermute | solution.py:314
  10.5 7.7 %collective-permute-start.5 = (bf16[2,2,128,128]{3,2,1,0:T(8,128)(2,1)S(1)}, bf16[2,2,128,128]{3,2,1,0:T(8,128)(2,1)S(1)}, u32[]{:S(2)}, u32[]{:S(2)}) collective-permute-start(bf16[2,2,128,128]{3,2,1,0:T(8,128)(2,1)S(1)} %get-tuple-element.46), channel_id=1, source_target_pairs={{0,8},{4,12},{8,0},{12,4},{16,24},{20,28},{24,16},{28,20},{1,9},{5... | collective-permute-start | bytes 393224 | tf_op jit(solution)/shard_map/ppermute | solution.py:314
  13.9 4.3 %copy-start.1 = (bf16[8,64,128]{2,1,0:T(8,128)(2,1)S(1)}, bf16[8,64,128]{2,1,0:T(8,128)(2,1)}, u32[]{:S(2)}) copy-start(bf16[8,64,128]{2,1,0:T(8,128)(2,1)} %wq_ref.1) | copy-start | bytes 393220
  14.5 9.5 %collective-permute-start.6 = (bf16[2,272,128]{2,1,0:T(8,128)(2,1)S(1)}, bf16[2,272,128]{2,1,0:T(8,128)(2,1)S(1)}, u32[]{:S(2)}, u32[]{:S(2)}) collective-permute-start(bf16[2,272,128]{2,1,0:T(8,128)(2,1)S(1)} %get-tuple-element.53), channel_id=1, source_target_pairs={{0,16},{4,20},{8,24},{12,28},{16,0},{20,4},{24,8},{28,12},{1,17},{... | collective-permute-start | bytes 417800 | tf_op jit(solution)/shard_map/ppermute | solution.py:314
  25.9 6.4 %collective-permute-start.10 = (bf16[2,144,128]{2,1,0:T(8,128)(2,1)S(1)}, bf16[2,144,128]{2,1,0:T(8,128)(2,1)S(1)}, u32[]{:S(2)}, u32[]{:S(2)}) collective-permute-start(bf16[2,144,128]{2,1,0:T(8,128)(2,1)S(1)} %get-tuple-element.58), channel_id=1, source_target_pairs={{0,16},{4,20},{8,24},{12,28},{16,0},{20,4},{24,8},{28,12},{1,17},{... | collective-permute-start | bytes 221192 | tf_op jit(solution)/shard_map/ppermute | solution.py:314
  26.9 4.2 %collective-permute-start.13 = (f32[8,128]{1,0:T(8,128)S(1)}, f32[8,128]{1,0:T(8,128)S(1)}, u32[]{:S(2)}, u32[]{:S(2)}) collective-permute-start(f32[8,128]{1,0:T(8,128)S(1)} %get-tuple-element.68.l0), channel_id=1, source_target_pairs={{0,3},{1,2},{2,1},{3,0},{4,7},{5,6},{6,5},{7,4},{8,11},{9,10},{10,... | collective-permute-start | bytes 12296 | tf_op jit(solution)/shard_map/ppermute | solution.py:314
  26.9 4.2 %collective-permute-start.12 = (f32[8,128]{1,0:T(8,128)S(1)}, f32[8,128]{1,0:T(8,128)S(1)}, u32[]{:S(2)}, u32[]{:S(2)}) collective-permute-start(f32[8,128]{1,0:T(8,128)S(1)} %get-tuple-element.68.l0), channel_id=1, source_target_pairs={{0,2},{1,3},{2,0},{3,1},{4,6},{5,7},{6,4},{7,5},{8,10},{9,11},{10,... | collective-permute-start | bytes 12296 | tf_op jit(solution)/shard_map/ppermute | solution.py:314
  28.4 2.7 %collective-permute-start.11 = (f32[8,128]{1,0:T(8,128)S(1)}, f32[8,128]{1,0:T(8,128)S(1)}, u32[]{:S(2)}, u32[]{:S(2)}) collective-permute-start(f32[8,128]{1,0:T(8,128)S(1)} %get-tuple-element.68.l0), channel_id=1, source_target_pairs={{0,1},{1,0},{2,3},{3,2},{4,5},{5,4},{6,7},{7,6},{8,9},{9,8},{10,11... | collective-permute-start | bytes 12296 | tf_op jit(solution)/shard_map/ppermute | solution.py:314
  33.2 6.3 %collective-permute-start.14 = (bf16[272,128]{1,0:T(8,128)(2,1)S(1)}, bf16[272,128]{1,0:T(8,128)(2,1)S(1)}, u32[]{:S(2)}, u32[]{:S(2)}) collective-permute-start(bf16[272,128]{1,0:T(8,128)(2,1)S(1)} %shard_map.100.refs_0_), channel_id=1, source_target_pairs={{0,16},{4,20},{8,24},{12,28},{16,0},{20,4},{24,8},{28,12},{1,17},{... | collective-permute-start | bytes 208904 | tf_op jit(solution)/shard_map/ppermute | solution.py:314
  34.1 7.7 %collective-permute-start.7 = (bf16[2,128,128]{2,1,0:T(8,128)(2,1)S(1)}, bf16[2,128,128]{2,1,0:T(8,128)(2,1)S(1)}, u32[]{:S(2)}, u32[]{:S(2)}) collective-permute-start(bf16[2,128,128]{2,1,0:T(8,128)(2,1)S(1)} %get-tuple-element.55), channel_id=1, source_target_pairs={{0,4},{4,0},{8,12},{12,8},{16,20},{20,16},{24,28},{28,24},{1,5},{5... | collective-permute-start | bytes 196616 | tf_op jit(solution)/shard_map/ppermute | solution.py:314
  35.2 7.8 %collective-permute-start.8 = (bf16[2,128,128]{2,1,0:T(8,128)(2,1)S(1)}, bf16[2,128,128]{2,1,0:T(8,128)(2,1)S(1)}, u32[]{:S(2)}, u32[]{:S(2)}) collective-permute-start(bf16[2,128,128]{2,1,0:T(8,128)(2,1)S(1)} %get-tuple-element.56), channel_id=1, source_target_pairs={{0,8},{4,12},{8,0},{12,4},{16,24},{20,28},{24,16},{28,20},{1,9},{5... | collective-permute-start | bytes 196616 | tf_op jit(solution)/shard_map/ppermute | solution.py:314
  36.2 6.9 %collective-permute-start.9 = (bf16[2,128,128]{2,1,0:T(8,128)(2,1)S(1)}, bf16[2,128,128]{2,1,0:T(8,128)(2,1)S(1)}, u32[]{:S(2)}, u32[]{:S(2)}) collective-permute-start(bf16[2,128,128]{2,1,0:T(8,128)(2,1)S(1)} %get-tuple-element.57), channel_id=1, source_target_pairs={{0,12},{4,8},{8,4},{12,0},{16,28},{20,24},{24,20},{28,16},{1,13},{... | collective-permute-start | bytes 196616 | tf_op jit(solution)/shard_map/ppermute | solution.py:314
  39.5 5.3 %collective-permute-start.17 = (bf16[272,128]{1,0:T(8,128)(2,1)S(1)}, bf16[272,128]{1,0:T(8,128)(2,1)S(1)}, u32[]{:S(2)}, u32[]{:S(2)}) collective-permute-start(bf16[272,128]{1,0:T(8,128)(2,1)S(1)} %shard_map.101.g0), channel_id=1, source_target_pairs={{0,12},{4,8},{8,4},{12,0},{16,28},{20,24},{24,20},{28,16},{1,13},{... | collective-permute-start | bytes 208904 | tf_op jit(solution)/shard_map/ppermute | solution.py:314
  39.7 5.1 %collective-permute-start.16 = (bf16[272,128]{1,0:T(8,128)(2,1)S(1)}, bf16[272,128]{1,0:T(8,128)(2,1)S(1)}, u32[]{:S(2)}, u32[]{:S(2)}) collective-permute-start(bf16[272,128]{1,0:T(8,128)(2,1)S(1)} %shard_map.101.g0), channel_id=1, source_target_pairs={{0,8},{4,12},{8,0},{12,4},{16,24},{20,28},{24,16},{28,20},{1,9},{5... | collective-permute-start | bytes 208904 | tf_op jit(solution)/shard_map/ppermute | solution.py:314
  41.8 4.3 %collective-permute-start.15 = (bf16[272,128]{1,0:T(8,128)(2,1)S(1)}, bf16[272,128]{1,0:T(8,128)(2,1)S(1)}, u32[]{:S(2)}, u32[]{:S(2)}) collective-permute-start(bf16[272,128]{1,0:T(8,128)(2,1)S(1)} %shard_map.101.g0), channel_id=1, source_target_pairs={{0,4},{4,0},{8,12},{12,8},{16,20},{20,16},{24,28},{28,24},{1,5},{5... | collective-permute-start | bytes 208904 | tf_op jit(solution)/shard_map/ppermute | solution.py:314

commit v4 on v3

--- a/solution.py
+++ b/solution.py
@@ -12,7 +12,7 @@
 F32 = jnp.float32
 BF16 = jnp.bfloat16
 SPREAD = (0, 3, 1, 2)
-KEY_US, OWN_US, GRAD_US, STUDENT_US = 20.0, 20.0, 0.2, 20.0
+KEY_US, FEATURE_US, OWN_US, OUT_US, GRAD_US, STUDENT_US = 20.0, 1.0, 20.0, 1.0, 0.2, 20.0
 
 
 def nt(a, b):
@@ -89,7 +89,7 @@
     return ref[first : first + 8].astype(F32) + ref[first + 8 : first + 16].astype(F32)
 
 
-def key_kernel(c0, c1, c2, c3, wk_ref, kv_ref, msg_ref):
+def key_kernel(c0, c1, c2, c3, wk_ref, kv_ref, *msg_refs):
     mine, _, _ = place_in_group()
     narr, per, tok, d = c0.shape
     for j, c in zip(SPREAD, (c0, c1, c2, c3)):
@@ -103,12 +103,29 @@
         feat = jnp.where(lane < total - WIN, feat, 0.0).astype(BF16)
         state = nt(extended(transposed(v).astype(BF16)), feat).astype(BF16)
         rows = state.shape[0]
-        msg_ref[hh, :rows] = state
-        msg_ref[hh, rows : rows + WIN] = k[total - WIN :]
-        msg_ref[hh, rows + WIN :] = v[total - WIN :]
-
-
-def own_kernel(kv_ref, c0, c1, c2, c3, wq_ref, wk_ref, qt_ref, teach_ref, win_ref, top_ref, lin_ref, fq_ref, up_ref, down_ref):
+        msg_refs[hh][0, :rows] = state
+        msg_refs[hh][0, rows : rows + WIN] = k[total - WIN :]
+        msg_refs[hh][0, rows + WIN :] = v[total - WIN :]
+
+
+def feature_kernel(kv_ref, wk_ref, fk_ref, rows_ref, vt_ref):
+    mine, _, _ = place_in_group()
+    _, per, _, tok, d = kv_ref.shape
+    total = QUAD * tok
+    none = jnp.zeros((WIN, d), BF16)
+    for hh in range(per):
+        k = jnp.concatenate([none, kv_ref[0, hh].reshape(total, d)[: total - WIN]], axis=0)
+        v = jnp.concatenate([none, kv_ref[1, hh].reshape(total, d), none], axis=0)
+        fk = jnp.concatenate(phi_t(k, wk_ref[per * mine + hh]), axis=0)
+        lane = lax.broadcasted_iota(jnp.int32, fk.shape, 1)
+        fk = jnp.where(lane >= WIN, fk, 0.0).astype(BF16)
+        fk_ref[hh] = fk
+        for b in range(QUAD):
+            rows_ref[hh, b * tok : (b + 1) * tok] = transposed(fk[:, b * tok : (b + 1) * tok]).astype(BF16)
+        vt_ref[hh] = extended(transposed(v).astype(BF16))
+
+
+def own_kernel(kv_ref, rows_ref, vt_ref, c0, c1, c2, c3, wq_ref, qt_ref, teach_ref, win_ref, top_ref, lin_ref, fq_ref, up_ref, down_ref):
     mine, _, _ = place_in_group()
     narr, per, tok, d = c0.shape
     total = QUAD * tok
@@ -123,18 +140,12 @@
         q = qt_ref[0, hh].reshape(total, d)
         none = jnp.zeros((WIN, d), BF16)
         k = jnp.concatenate([none, kv_ref[0, hh].reshape(total, d)], axis=0)
-        v = jnp.concatenate([none, kv_ref[1, hh].reshape(total, d)], axis=0)
         up, down = phi_t(q, wq_ref[per * mine + hh])
         up_ref[hh], down_ref[hh] = up, down
         fq = jnp.concatenate([up, down], axis=0).astype(BF16)
         fq_ref[hh] = fq
-        fk = jnp.concatenate(phi_t(k[:total], wk_ref[per * mine + hh]), axis=0)
-        lane = lax.broadcasted_iota(jnp.int32, fk.shape, 1)
-        fk = jnp.where(lane >= WIN, fk, 0.0).astype(BF16)
-        fk_rows = jnp.concatenate(
-            [transposed(fk[:, b * tok : (b + 1) * tok]).astype(BF16) for b in range(QUAD)], axis=0
-        )
-        vt = extended(transposed(v).astype(BF16))
+        fk_rows = rows_ref[hh]
+        vt = vt_ref[hh]
         for b in range(QUAD):
             lo, hi = b * tok, (b + 1) * tok
             score = nt(k[lo : hi + WIN], q[lo:hi]) * scale
@@ -151,7 +162,8 @@
             teach_ref[hh, :, lo:hi] = transposed(qt_ref[1, hh, b])
 
 
-def out_kernel(qt_ref, teach_ref, win_ref, top_ref, lin_ref, fq_ref, msg_ref, wk_ref, s0, s1, s2, s3, later_ref, grad_ref, loss_ref, outs):
+def out_kernel(hh, qt_ref, teach_ref, win_ref, top_ref, lin_ref, fq_ref, msg_ref, wk_ref, *refs):
+    *before, out_ref, later_ref, grad_ref, loss_ref = refs
     mine, has_past, _ = place_in_group()
     narr, per, _, tok, d = qt_ref.shape
     total = QUAD * tok
@@ -160,60 +172,58 @@
     early = jnp.logical_and(token < WIN, jnp.logical_not(has_past))
     row = lax.broadcasted_iota(jnp.int32, (WIN, total), 0)
     col = lax.broadcasted_iota(jnp.int32, (WIN, total), 1)
-    loss = jnp.zeros((8, total), F32)
-    for hh in range(per):
-        fq = fq_ref[hh]
-        state = jnp.where(has_past, msg_ref[hh, : d + 16].astype(F32), 0.0).astype(BF16)
-        halo_k = msg_ref[hh, d + 16 : d + 16 + WIN]
-        vt = extended(transposed(msg_ref[hh, d + 16 + WIN :]).astype(BF16))
-        fk = jnp.concatenate(phi_t(halo_k, wk_ref[per * mine + hh]), axis=0)
-        fk = jnp.where(has_past, fk, 0.0).astype(BF16)
-        amat = nn(transposed(fk).astype(BF16), fq)
-        amat = jnp.where(row <= col, amat, 0.0).astype(BF16)
-        lin = lin_ref[hh] + nn(state, fq) + nn(vt, amat)
-        score = nt(halo_k, qt_ref[0, hh, 0]) * scale
-        keep = (row > col)[:, :tok] & has_past
-        score = jnp.where(keep, score, -jnp.inf)
-        old = top_ref[hh, :1, :tok]
-        first = jnp.maximum(old, jnp.max(score, axis=0, keepdims=True))
-        weight = jnp.exp(score - first).astype(BF16)
-        win = win_ref[hh, :, :tok] * jnp.exp(old - first) + nn(vt, weight)
-        win = jnp.concatenate([win, win_ref[hh, :, tok:]], axis=1)
-        top = jnp.concatenate([first, top_ref[hh, :1, tok:]], axis=1)
-        win_scale = jnp.where(early, 1.0, jnp.exp(jnp.minimum(top, 0.0)))
-        lin_scale = jnp.where(early, 0.0, jnp.exp(-jnp.maximum(top, 0.0)))
-        both = win_scale * win + lin_scale * lin
-        inverse = 1.0 / both[d : d + 1]
-        out = both[:d] * inverse
-        out_rows = out.astype(BF16)
-        for b in range(QUAD):
-            outs[b, hh] = transposed(out_rows[:, b * tok : (b + 1) * tok]).astype(BF16)
-        diff = out - teach_ref[hh]
-        loss = loss + jnp.sum((diff * diff).reshape(d // 8, 8, total), axis=0)
-        g = diff * (2.0 / d)
-        coef = lin_scale * inverse
-        g_num = coef * g
-        g_den = -coef * jnp.sum(g * out, axis=0, keepdims=True)
-        pad = lax.broadcasted_iota(jnp.int32, (16, total), 0)
-        g_ext = jnp.concatenate([g_num, jnp.where(pad == 0, g_den, 0.0)], axis=0).astype(BF16)
-        grad_ref[hh] = g_ext
-        later_ref[hh] = nt(g_ext, fq).astype(BF16)
+    fq = fq_ref[hh]
+    state = jnp.where(has_past, msg_ref[0, : d + 16].astype(F32), 0.0).astype(BF16)
+    halo_k = msg_ref[0, d + 16 : d + 16 + WIN]
+    vt = extended(transposed(msg_ref[0, d + 16 + WIN :]).astype(BF16))
+    fk = jnp.concatenate(phi_t(halo_k, wk_ref[per * mine + hh]), axis=0)
+    fk = jnp.where(has_past, fk, 0.0).astype(BF16)
+    amat = nn(transposed(fk).astype(BF16), fq)
+    amat = jnp.where(row <= col, amat, 0.0).astype(BF16)
+    lin = lin_ref[hh] + nn(state, fq) + nn(vt, amat)
+    score = nt(halo_k, qt_ref[0, hh, 0]) * scale
+    keep = (row > col)[:, :tok] & has_past
+    score = jnp.where(keep, score, -jnp.inf)
+    old = top_ref[hh, :1, :tok]
+    first = jnp.maximum(old, jnp.max(score, axis=0, keepdims=True))
+    weight = jnp.exp(score - first).astype(BF16)
+    win = win_ref[hh, :, :tok] * jnp.exp(old - first) + nn(vt, weight)
+    win = jnp.concatenate([win, win_ref[hh, :, tok:]], axis=1)
+    top = jnp.concatenate([first, top_ref[hh, :1, tok:]], axis=1)
+    win_scale = jnp.where(early, 1.0, jnp.exp(jnp.minimum(top, 0.0)))
+    lin_scale = jnp.where(early, 0.0, jnp.exp(-jnp.maximum(top, 0.0)))
+    both = win_scale * win + lin_scale * lin
+    inverse = 1.0 / both[d : d + 1]
+    out = both[:d] * inverse
+    out_ref[...] = out.astype(BF16)
+    diff = out - teach_ref[hh]
+    loss = jnp.sum((diff * diff).reshape(d // 8, 8, total), axis=0)
     loss = sum(loss[:, b * tok : (b + 1) * tok] for b in range(QUAD))
-    loss_ref[...] = loss
-    for j, s in enumerate((s0, s1, s2, s3)):
-        s[...] = outs[lax.bitwise_xor(mine, j)]
-
-
-def grad_kernel(kv_ref, qt_ref, msg_ref, grad_ref, fq_ref, qup_ref, qdown_ref, wk_ref,
-                gq_ref, gk_ref, k_ref, v_ref, kup_ref, kdown_ref):
+    loss_ref[...] = loss + before[1][...] if before else loss
+    if before:
+        later_ref[:hh] = before[0][...]
+    g = diff * (2.0 / d)
+    coef = lin_scale * inverse
+    g_num = coef * g
+    g_den = -coef * jnp.sum(g * out, axis=0, keepdims=True)
+    pad = lax.broadcasted_iota(jnp.int32, (16, total), 0)
+    g_ext = jnp.concatenate([g_num, jnp.where(pad == 0, g_den, 0.0)], axis=0).astype(BF16)
+    grad_ref[...] = g_ext
+    later_ref[hh] = nt(g_ext, fq).astype(BF16)
+
+
+def grad_kernel(per, *refs):
+    msg_refs, grad_refs, out_refs = refs[:per], refs[per : 2 * per], refs[2 * per : 3 * per]
+    kv_ref, qt_ref, fq_ref, qup_ref, qdown_ref, wk_ref = refs[3 * per : 3 * per + 6]
+    s0, s1, s2, s3, gq_ref, gk_ref, k_ref, v_ref, kup_ref, kdown_ref, outs = refs[3 * per + 6 :]
     mine, has_past, _ = place_in_group()
-    narr, per, _, tok, d = qt_ref.shape
+    _, _, _, tok, d = qt_ref.shape
     total = QUAD * tok
     causal = lax.broadcasted_iota(jnp.int32, (tok, tok), 0) <= lax.broadcasted_iota(jnp.int32, (tok, tok), 1)
     for hh in range(per):
-        state = jnp.where(has_past, msg_ref[hh, : d + 16].astype(F32), 0.0).astype(BF16)
-        k = jnp.concatenate([msg_ref[hh, d + 16 : d + 16 + WIN], kv_ref[0, hh].reshape(total, d)[: total - WIN]], axis=0)
-        v = jnp.concatenate([msg_ref[hh, d + 16 + WIN :], kv_ref[1, hh].reshape(total, d)[: total - WIN]], axis=0)
+        state = jnp.where(has_past, msg_refs[hh][0, : d + 16].astype(F32), 0.0).astype(BF16)
+        k = jnp.concatenate([msg_refs[hh][0, d + 16 : d + 16 + WIN], kv_ref[0, hh].reshape(total, d)[: total - WIN]], axis=0)
+        v = jnp.concatenate([msg_refs[hh][0, d + 16 + WIN :], kv_ref[1, hh].reshape(total, d)[: total - WIN]], axis=0)
         k_ref[hh], v_ref[hh] = k, v
         up, down = phi_t(k, wk_ref[per * mine + hh])
         kup_ref[hh], kdown_ref[hh] = up, down
@@ -222,7 +232,7 @@
         valid = (lane >= WIN) | has_past
         fk = jnp.where(valid, fk, 0.0).astype(BF16)
         fq = fq_ref[hh]
-        g_ext = grad_ref[hh]
+        g_ext = grad_refs[hh][...]
         g_num, g_den = g_ext[:d], g_ext[d : d + 1].astype(F32)
         grad_q = nn(transposed(state).astype(BF16), g_ext)
         grad_k = []
@@ -241,12 +251,16 @@
         ):
             high, low = split2(phi_pull(ups, downs, grad))
             ref[hh] = nn(high, x) + nn(low, x)
-
-
-def last_kernel(later_ref, k_ref, v_ref, kup_ref, kdown_ref, gq_ref, gk_ref, l0, l1, l2, l3, out_ref):
+        for b in range(QUAD):
+            outs[b, hh] = transposed(out_refs[hh][:, b * tok : (b + 1) * tok]).astype(BF16)
+    for j, s in enumerate((s0, s1, s2, s3)):
+        s[...] = outs[lax.bitwise_xor(mine, j)]
+
+
+def last_kernel(*refs):
+    later_ref, k_ref, v_ref, kup_ref, kdown_ref, gq_ref, gk_ref, l0, l1, l2, l3, out_ref = refs
     _, has_past, has_future = place_in_group()
-    per, total, d = k_ref.shape
-    half = gq_ref.shape[1]
+    per, half, d = gq_ref.shape
     for hh in range(per):
         after = transposed(later_ref[hh])
         grad = nt(after[:, :d].astype(BF16), v_ref[hh]) + after[:, d : d + 1]
@@ -318,9 +332,10 @@
     return [flip(parts[j], "ctx", j) if j else parts[j] for j in SPREAD]
 
 
-def state_over_groups(msg, d, wk_pair, group, groups, members):
+def state_over_groups(msg, d, wk, head, group, groups, members):
     if groups == 2:
         return flip(msg, "ctx", QUAD)
+    wk_pair = lax.dynamic_slice_in_dim(wk, head, 1, 0)
     every = lax.all_gather(msg, "ctx", axis_index_groups=members)
     k, v = every[:, :, d + 16 : d + 16 + WIN], every[:, :, d + 16 + WIN :]
     proj = jnp.einsum("gptd,pfd->gptf", k, wk_pair, preferred_element_type=F32)
@@ -374,38 +389,45 @@
     qt = spread(pack(jnp.concatenate([queries, teacher])))
 
     rows = d + 16 + 2 * WIN
-    kv, msg = call(
-        key_kernel, [shape(2, per, QUAD, tok, d), shape(per, rows, d)], ins=5, micros=KEY_US
+    kv, *msgs = call(
+        key_kernel, [shape(2, per, QUAD, tok, d)] + [shape(1, rows, d)] * per, ins=5, micros=KEY_US
     )(*kv, wk)
-    wk_pair = (
-        lax.dynamic_slice_in_dim(wk, per * (lax.axis_index("ctx") % QUAD), per, 0) if groups != 2 else None
-    )
-    msg = state_over_groups(msg, d, wk_pair, group, groups, members)
+    first = per * (lax.axis_index("ctx") % QUAD)
+    msgs = [state_over_groups(msg, d, wk, first + hh, group, groups, members) for hh, msg in enumerate(msgs)]
 
     sums = shape(per, d + 16, total, dtype=F32)
     part = shape(per, half, total, dtype=F32)
     grad = shape(per, half, d, dtype=F32)
+    fk, fk_rows, vt = call(
+        feature_kernel,
+        [shape(per, 2 * half, total), shape(per, total, 2 * half), shape(per, d + 16, total + 2 * WIN)],
+        ins=2, micros=FEATURE_US,
+    )(kv, wk)
     qt, teach, win, top, lin, fq, q_up, q_down = call(
         own_kernel,
         [shape(2, per, QUAD, tok, d), shape(per, d, total, dtype=F32), sums, shape(per, 8, total, dtype=F32), sums,
          shape(per, 2 * half, total), part, part],
-        ins=7, micros=OWN_US,
-    )(kv, *qt, wq, wk)
-    block = shape(per, tok, d)
-    s0, s1, s2, s3, later, g_out, loss = call(
-        out_kernel,
-        [block] * QUAD + [shape(per, d + 16, 2 * half), shape(per, d + 16, total), shape(8, tok, dtype=F32)],
+        ins=8, micros=OWN_US,
+    )(kv, fk_rows, vt, *qt, wq)
+    outs, g_outs, before = [], [], ()
+    for hh in range(per):
+        out, later, g_out, loss = call(
+            functools.partial(out_kernel, hh),
+            [shape(d, total), shape(hh + 1, d + 16, 2 * half), shape(d + 16, total), shape(8, tok, dtype=F32)],
+            ins=8 + len(before), micros=OUT_US,
+        )(qt, teach, win, top, lin, fq, msgs[hh], wk, *before)
+        outs.append(out)
+        g_outs.append(g_out)
+        before = (later, loss)
+    later = later_over_groups(later, group, groups, members)
+    losses = [loss] + [flip(loss, "head", j) for j in range(1, lax.axis_size("head"))]
+    s0, s1, s2, s3, gq, gk, k, v, k_up, k_down = call(
+        functools.partial(grad_kernel, per),
+        [shape(per, tok, d)] * QUAD + [grad, grad, shape(per, total, d), shape(per, total, d), part, part],
         [pltpu.VMEM((QUAD, per, tok, d), BF16)],
-        ins=8, micros=2.0,
-    )(qt, teach, win, top, lin, fq, msg, wk)
-    later = later_over_groups(later, group, groups, members)
+        ins=3 * per + 6, micros=GRAD_US,
+    )(*msgs, *g_outs, *outs, kv, qt, fq, q_up, q_down, wk)
     s1, s2, s3 = [flip(s, "ctx", j) for j, s in ((1, s1), (2, s2), (3, s3))]
-    losses = [loss] + [flip(loss, "head", j) for j in range(1, lax.axis_size("head"))]
-    gq, gk, k, v, k_up, k_down = call(
-        grad_kernel,
-        [grad, grad, shape(per, total, d), shape(per, total, d), part, part],
-        ins=8, micros=GRAD_US,
-    )(kv, qt, msg, g_out, fq, q_up, q_down, wk)
     rows = 2 * per * half + 16
     grads = call(last_kernel, shape(rows, d), ins=11)(
         later, k, v, k_up, k_down, gq, gk, *losses

time: 47.1 us -> 45.8 us (0.972)
  waiting for transfers between devices: 10.3 us -> 7.35 us
  Pallas kernels: 11.1 us -> 12.2 us
    ppermute x18 -> x19, waiting for transfers between devices: 10.3 us -> 7.35 us  [flip(): lax.ppermute(x, axis, [(i, i ^ by) for i in range(lax.axis_size(axis))])]
    pallas_call x3 -> x5, Pallas kernels: 4.87 us -> 6.52 us  [the longest x1 2.51 us: per_device(): call(functools.partial(grad_kernel, per), [shape(per, tok, d)] * QUAD + [...]
    pallas_call x1, Pallas kernels: 3.09 us -> 2.61 us  [per_device(): call(own_kernel, [shape(2, per, QUAD, tok, d), shape(per, d, total, dtype...]
    ppermute x18 -> x19, starting transfers between devices: 23.7 us -> 24.1 us  [flip(): lax.ppermute(x, axis, [(i, i ^ by) for i in range(lax.axis_size(axis))])]
  transfers between devices with their start and end apart: 18 -> 19, of which waited for: 9 -> 6; matrix products, arithmetic and copies ran while one was open for 0% -> 0% of each run, Pallas kernels for 16% -> 20%
where the time goes in v4:
time: 45.8 us; the launch traced here: 45.6 us
  starting transfers between devices  24.1 us (53%)
  Pallas kernels  12.2 us (27%)
  waiting for transfers between devices  7.35 us (16%)
  other arithmetic  1.12 us (2%)
  between operations  0.78 us (2%)
    ppermute x19, starting transfers between devices, flip(): lax.ppermute(x, axis, [(i, i ^ by) for i in range(lax.axis_size(axis))])  24.1 us
    ppermute x19, waiting for transfers between devices, flip(): lax.ppermute(x, axis, [(i, i ^ by) for i in range(lax.axis_size(axis))])  7.35 us
    pallas_call x1, Pallas kernels, per_device(): call(own_kernel, [shape(2, per, QUAD, tok, d), shape(per, d, total, dtype...  2.61 us
    pallas_call x1, Pallas kernels, per_device(): call(functools.partial(grad_kernel, per), [shape(per, tok, d)] * QUAD + [...  2.51 us
    pallas_call x2, Pallas kernels, per_device(): call(functools.partial(out_kernel, hh), [shape(d, total), shape(hh + 1, d...  2.04 us
    pallas_call x1, Pallas kernels, per_device(): call(feature_kernel, [shape(per, 2 * half, total), shape(per, total, 2 *...  1.29 us
    concatenate x1, other arithmetic, per_device(): kv = pack(jnp.concatenate([keys, values]))  1.08 us
  transfers between devices with their start and end apart: 19, of which 6 were waited for; matrix products, arithmetic and copies ran while one was open for 0% of the time, Pallas kernels for 20%

profile of v4, /device:TPU:0, one launch (start us, length us, event | category | flops | bytes accessed | tf_op | source)
XLA Modules:
  0.0 45.6 jit_solution(6517258904761624286)
XLA Ops:
  0.6 1.1 %pad_maximum_fusion.refs_0_ = bf16[256,8,128]{2,1,0:T(8,128)(2,1)S(1)} fusion(bf16[128,8,128]{2,1,0:T(8,128)(2,1)} %param.8, bf16[128,8,128]{2,1,0:T(8,128)(2,1)} %param.7), kind=kLoop, calls=%fused_computation | loop fusion | flops 262144 | bytes 1048576 | tf_op jit(solution)/shard_map/concatenate | solution.py:387
  1.7 0.0 copy-start.2
  1.7 0.0 copy-start.3
  1.7 0.3 shard_map.93
  2.0 4.0 %collective-permute-start = (bf16[2,2,128,128]{3,2,1,0:T(8,128)(2,1)S(1)}, bf16[2,2,128,128]{3,2,1,0:T(8,128)(2,1)S(1)}, u32[]{:S(2)}, u32[]{:S(2)}) collective-permute-start(bf16[2,2,128,128]{3,2,1,0:T(8,128)(2,1)S(1)} %get-tuple-element.47), channel_id=1, source_target_pairs={{0,12},{4,8},{8,4},{12,0},{16,28},{20,24},{24,20},{28,16},{1,13},{... | collective-permute-start | bytes 393224 | tf_op jit(solution)/shard_map/ppermute | solution.py:328
  6.1 0.5 %collective-permute-start.1 = (bf16[2,2,128,128]{3,2,1,0:T(8,128)(2,1)S(1)}, bf16[2,2,128,128]{3,2,1,0:T(8,128)(2,1)S(1)}, u32[]{:S(2)}, u32[]{:S(2)}) collective-permute-start(bf16[2,2,128,128]{3,2,1,0:T(8,128)(2,1)S(1)} %get-tuple-element.48), channel_id=1, source_target_pairs={{0,4},{4,0},{8,12},{12,8},{16,20},{20,16},{24,28},{28,24},{1,5},{5... | collective-permute-start | bytes 393224 | tf_op jit(solution)/shard_map/ppermute | solution.py:328
  6.6 0.1 collective-permute-start.2
  6.7 0.0 copy-done.2
  6.7 0.0 copy-done.3
  6.8 0.0 copy-start
  6.8 0.3 shard_map.96
  7.0 2.9 %collective-permute-start.5 = (bf16[2,2,128,128]{3,2,1,0:T(8,128)(2,1)S(1)}, bf16[2,2,128,128]{3,2,1,0:T(8,128)(2,1)S(1)}, u32[]{:S(2)}, u32[]{:S(2)}) collective-permute-start(bf16[2,2,128,128]{3,2,1,0:T(8,128)(2,1)S(1)} %get-tuple-element.56), channel_id=1, source_target_pairs={{0,12},{4,8},{8,4},{12,0},{16,28},{20,24},{24,20},{28,16},{1,13},{... | collective-permute-start | bytes 393224 | tf_op jit(solution)/shard_map/ppermute | solution.py:328
  9.9 0.5 %collective-permute-start.6 = (bf16[2,2,128,128]{3,2,1,0:T(8,128)(2,1)S(1)}, bf16[2,2,128,128]{3,2,1,0:T(8,128)(2,1)S(1)}, u32[]{:S(2)}, u32[]{:S(2)}) collective-permute-start(bf16[2,2,128,128]{3,2,1,0:T(8,128)(2,1)S(1)} %get-tuple-element.57), channel_id=1, source_target_pairs={{0,4},{4,0},{8,12},{12,8},{16,20},{20,16},{24,28},{28,24},{1,5},{5... | collective-permute-start | bytes 393224 | tf_op jit(solution)/shard_map/ppermute | solution.py:328
  10.5 0.0 collective-permute-done.c1
  10.5 1.9 %collective-permute-start.7 = (bf16[2,2,128,128]{3,2,1,0:T(8,128)(2,1)S(1)}, bf16[2,2,128,128]{3,2,1,0:T(8,128)(2,1)S(1)}, u32[]{:S(2)}, u32[]{:S(2)}) collective-permute-start(bf16[2,2,128,128]{3,2,1,0:T(8,128)(2,1)S(1)} %get-tuple-element.58), channel_id=1, source_target_pairs={{0,8},{4,12},{8,0},{12,4},{16,24},{20,28},{24,16},{28,20},{1,9},{5... | collective-permute-start | bytes 393224 | tf_op jit(solution)/shard_map/ppermute | solution.py:328
  12.4 1.5 %collective-permute-done.1.c2 = bf16[2,2,128,128]{3,2,1,0:T(8,128)(2,1)S(1)} collective-permute-done((bf16[2,2,128,128]{3,2,1,0:T(8,128)(2,1)S(1)}, bf16[2,2,128,128]{3,2,1,0:T(8,128)(2,1)S(1)}, u32[]{:S(2)}, u32[]{:S(2)}) %collective-permute-start.1) | collective-permute-done | bytes 131104 | tf_op jit(solution)/shard_map/ppermute | solution.py:328
  13.9 0.0 collective-permute-done.2.c3
  13.9 0.0 copy-done
  13.9 0.7 %shard_map.94 = (bf16[2,2,4,128,128]{4,3,2,1,0:T(8,128)(2,1)S(1)}, bf16[1,272,128]{2,1,0:T(8,128)(2,1)S(1)}, bf16[1,272,128]{2,1,0:T(8,128)(2,1)S(1)}) custom-call(bf16[2,2,128,128]{3,2,1,0:T(8,128)(2,1)S(1)} %get-tuple-element.46.c0, bf16[2,2,128,128]{3,2,1,0:T(8,128)(2,1)S(1)} %collective-permute-done.c1, ...), custom_call_target="tpu_custom_call" | custom-call | flops 20000000000 | tf_op jit(solution)/shard_map/pallas_call | solution.py:392
  14.5 2.8 %collective-permute-start.3 = (bf16[1,272,128]{2,1,0:T(8,128)(2,1)S(1)}, bf16[1,272,128]{2,1,0:T(8,128)(2,1)S(1)}, u32[]{:S(2)}, u32[]{:S(2)}) collective-permute-start(bf16[1,272,128]{2,1,0:T(8,128)(2,1)S(1)} %get-tuple-element.50), channel_id=1, source_target_pairs={{0,16},{4,20},{8,24},{12,28},{16,0},{20,4},{24,8},{28,12},{1,17},{... | collective-permute-start | bytes 208904 | tf_op jit(solution)/shard_map/ppermute | solution.py:328
  17.3 0.2 collective-permute-start.4
  17.5 0.0 copy-start.1
  17.5 1.3 %shard_map.95 = (bf16[2,128,512]{2,1,0:T(8,128)(2,1)}, bf16[2,512,128]{2,1,0:T(8,128)(2,1)S(1)}, bf16[2,144,640]{2,1,0:T(8,128)(2,1)S(1)}) custom-call(bf16[2,2,4,128,128]{4,3,2,1,0:T(8,128)(2,1)S(1)} %get-tuple-element.52.kv_ref.refs_6_, bf16[8,64,128]{2,1,0:T(8,128)(2,1)S(1)} %copy-done), custom_call_target="tpu_custom_call" | custom-call | flops 1000000000 | tf_op jit(solution)/shard_map/pallas_call | solution.py:401
  18.8 0.0 collective-permute-done.5.c1
  18.8 0.0 collective-permute-done.6.c2
  18.8 0.0 collective-permute-done.7.c3
  18.8 0.0 copy-done.1
  18.8 2.6 %shard_map.97 = (bf16[2,2,4,128,128]{4,3,2,1,0:T(8,128)(2,1)S(1)}, f32[2,128,512]{2,1,0:T(8,128)S(1)}, f32[2,144,512]{2,1,0:T(8,128)S(1)}, f32[2,8,512]{2,1,0:T(...) custom-call(bf16[2,2,4,128,128]{4,3,2,1,0:T(8,128)(2,1)S(1)} %get-tu, ...), custom_call_target="tpu_custom_call" | custom-call | flops 20000000000 | tf_op jit(solution)/shard_map/pallas_call | solution.py:406
  21.5 0.0 collective-permute-done.3.msg_ref.refs_0_
  21.5 1.0 %shard_map.98 = (bf16[128,512]{1,0:T(8,128)(2,1)S(1)}, bf16[1,144,128]{2,1,0:T(8,128)(2,1)S(1)}, bf16[144,512]{1,0:T(8,128)(2,1)S(1)}, f32[8,128]{1,0:T(8,128)S(1)}) custom-call(bf16[2,2,4,128,128]{4,3,2,1,0:T(8,128)(2,1)S(1)} %get-tuple-element.59.qt_ref.refs_7_, f32[2,128,512]{2,1,0:T(8,128)S(1)} %get-tuple-element.60.teach_ref, ...), custom_call_target="tpu_custom_call" | custom-call | flops 1000000000 | tf_op jit(solution)/shard_map/pallas_call | solution.py:414
  22.5 1.8 %collective-permute-done.4.msg_ref.refs_1_ = bf16[1,272,128]{2,1,0:T(8,128)(2,1)S(1)} collective-permute-done((bf16[1,272,128]{2,1,0:T(8,128)(2,1)S(1)}, bf16[1,272,128]{2,1,0:T(8,128)(2,1)S(1)}, u32[]{:S(2)}, u32[]{:S(2)}) %collective-permute-start.4) | collective-permute-done | bytes 69664 | tf_op jit(solution)/shard_map/ppermute | solution.py:328
  24.3 1.0 %shard_map.99 = (bf16[128,512]{1,0:T(8,128)(2,1)S(1)}, bf16[2,144,128]{2,1,0:T(8,128)(2,1)S(1)}, bf16[144,512]{1,0:T(8,128)(2,1)S(1)}, f32[8,128]{1,0:T(8,128)S(1)}) custom-call(bf16[2,2,4,128,128]{4,3,2,1,0:T(8,128)(2,1)S(1)} %get-tuple-element.59.qt_ref.refs_7_, f32[2,128,512]{2,1,0:T(8,128)S(1)} %get-tuple-element.60.teach_ref, ...), custom_call_target="tpu_custom_call" | custom-call | flops 1000000000 | tf_op jit(solution)/shard_map/pallas_call | solution.py:414
  25.3 1.0 %collective-permute-start.11 = (bf16[2,144,128]{2,1,0:T(8,128)(2,1)S(1)}, bf16[2,144,128]{2,1,0:T(8,128)(2,1)S(1)}, u32[]{:S(2)}, u32[]{:S(2)}) collective-permute-start(bf16[2,144,128]{2,1,0:T(8,128)(2,1)S(1)} %get-tuple-element.77), channel_id=1, source_target_pairs={{0,16},{4,20},{8,24},{12,28},{16,0},{20,4},{24,8},{28,12},{1,17},{... | collective-permute-start | bytes 221192 | tf_op jit(solution)/shard_map/ppermute | solution.py:328
  26.3 0.1 collective-permute-start.14
  26.5 1.4 %collective-permute-start.13 = (f32[8,128]{1,0:T(8,128)S(1)}, f32[8,128]{1,0:T(8,128)S(1)}, u32[]{:S(2)}, u32[]{:S(2)}) collective-permute-start(f32[8,128]{1,0:T(8,128)S(1)} %get-tuple-element.84.refs_7_), channel_id=1, source_target_pairs={{0,2},{1,3},{2,0},{3,1},{4,6},{5,7},{6,4},{7,5},{8,10},{9,11},{10,... | collective-permute-start | bytes 12296 | tf_op jit(solution)/shard_map/ppermute | solution.py:328
  27.8 0.3 collective-permute-start.12
  28.2 2.5 %shard_map.100 = (bf16[2,128,128]{2,1,0:T(8,128)(2,1)S(1)}, bf16[2,128,128]{2,1,0:T(8,128)(2,1)S(1)}, bf16[2,128,128]{2,1,0:T(8,128)(2,1)S(1)}, bf16[2,128,128]{...) custom-call(bf16[1,272,128]{2,1,0:T(8,128)(2,1)S(1)} %collective-per, ...), custom_call_target="tpu_custom_call" | custom-call | flops 200000000 | tf_op jit(solution)/shard_map/pallas_call | solution.py:424
  30.7 0.0 collective-permute-done.14.refs_10_
  30.7 0.0 collective-permute-done.13.refs_9_
  30.7 0.0 collective-permute-done.12.refs_8_
  30.7 0.9 %collective-permute-done.11.refs_0_ = bf16[2,144,128]{2,1,0:T(8,128)(2,1)S(1)} collective-permute-done((bf16[2,144,128]{2,1,0:T(8,128)(2,1)S(1)}, bf16[2,144,128]{2,1,0:T(8,128)(2,1)S(1)}, u32[]{:S(2)}, u32[]{:S(2)}) %collective-permute-start.11) | collective-permute-done | bytes 73760 | tf_op jit(solution)/shard_map/ppermute | solution.py:328
  31.6 0.8 %shard_map.102.refs_0_ = bf16[272,128]{1,0:T(8,128)(2,1)S(1)} custom-call(bf16[2,144,128]{2,1,0:T(8,128)(2,1)S(1)} %collective-permute-done.11.refs_0_, bf16[2,512,128]{2,1,0:T(8,128)(2,1)S(1)} %get-tuple-element.78.refs_1_, bf16[2,512,128]{2,1,0:T(8,128)(2,1)S(1)} %get-tuple-element.79.refs_2_, f32[2,64,512]{2,1,0:T(8,128)S(1)} %get-tuple-element.80.refs_3_, ...), custom_call_target="tpu_custom_call" | custom-call | flops 1000000000 | tf_op jit(solution)/shard_map/pallas_call | solution.py:432
  32.5 1.2 %collective-permute-start.15 = (bf16[272,128]{1,0:T(8,128)(2,1)S(1)}, bf16[272,128]{1,0:T(8,128)(2,1)S(1)}, u32[]{:S(2)}, u32[]{:S(2)}) collective-permute-start(bf16[272,128]{1,0:T(8,128)(2,1)S(1)} %shard_map.102.refs_0_), channel_id=1, source_target_pairs={{0,16},{4,20},{8,24},{12,28},{16,0},{20,4},{24,8},{28,12},{1,17},{... | collective-permute-start | bytes 208904 | tf_op jit(solution)/shard_map/ppermute | solution.py:328
  33.6 0.2 collective-permute-start.8
  33.8 2.2 %collective-permute-start.9 = (bf16[2,128,128]{2,1,0:T(8,128)(2,1)S(1)}, bf16[2,128,128]{2,1,0:T(8,128)(2,1)S(1)}, u32[]{:S(2)}, u32[]{:S(2)}) collective-permute-start(bf16[2,128,128]{2,1,0:T(8,128)(2,1)S(1)} %get-tuple-element.75), channel_id=1, source_target_pairs={{0,8},{4,12},{8,0},{12,4},{16,24},{20,28},{24,16},{28,20},{1,9},{5... | collective-permute-start | bytes 196616 | tf_op jit(solution)/shard_map/ppermute | solution.py:328
  36.0 1.1 %collective-permute-start.10 = (bf16[2,128,128]{2,1,0:T(8,128)(2,1)S(1)}, bf16[2,128,128]{2,1,0:T(8,128)(2,1)S(1)}, u32[]{:S(2)}, u32[]{:S(2)}) collective-permute-start(bf16[2,128,128]{2,1,0:T(8,128)(2,1)S(1)} %get-tuple-element.76), channel_id=1, source_target_pairs={{0,12},{4,8},{8,4},{12,0},{16,28},{20,24},{24,20},{28,16},{1,13},{... | collective-permute-start | bytes 196616 | tf_op jit(solution)/shard_map/ppermute | solution.py:328
  37.1 1.6 %collective-permute-done.15.refs_1_ = bf16[272,128]{1,0:T(8,128)(2,1)S(1)} collective-permute-done((bf16[272,128]{1,0:T(8,128)(2,1)S(1)}, bf16[272,128]{1,0:T(8,128)(2,1)S(1)}, u32[]{:S(2)}, u32[]{:S(2)}) %collective-permute-start.15) | collective-permute-done | bytes 69664 | tf_op jit(solution)/shard_map/ppermute | solution.py:328
  38.8 1.7 %collective-permute-start.18 = (bf16[272,128]{1,0:T(8,128)(2,1)S(1)}, bf16[272,128]{1,0:T(8,128)(2,1)S(1)}, u32[]{:S(2)}, u32[]{:S(2)}) collective-permute-start(bf16[272,128]{1,0:T(8,128)(2,1)S(1)} %shard_map.103.g0), channel_id=1, source_target_pairs={{0,12},{4,8},{8,4},{12,0},{16,28},{20,24},{24,20},{28,16},{1,13},{... | collective-permute-start | bytes 208904 | tf_op jit(solution)/shard_map/ppermute | solution.py:328
  40.5 0.0 collective-permute-start.17
  40.5 0.0 collective-permute-done.8.s1
  40.5 1.8 %collective-permute-start.16 = (bf16[272,128]{1,0:T(8,128)(2,1)S(1)}, bf16[272,128]{1,0:T(8,128)(2,1)S(1)}, u32[]{:S(2)}, u32[]{:S(2)}) collective-permute-start(bf16[272,128]{1,0:T(8,128)(2,1)S(1)} %shard_map.103.g0), channel_id=1, source_target_pairs={{0,4},{4,0},{8,12},{12,8},{16,20},{20,16},{24,28},{28,24},{1,5},{5... | collective-permute-start | bytes 208904 | tf_op jit(solution)/shard_map/ppermute | solution.py:328
  42.3 0.0 collective-permute-done.9.s2
  42.3 0.0 collective-permute-done.10.s3
  42.3 0.9 %shard_map.101 = bf16[128,8,128]{2,1,0:T(8,128)(2,1)} custom-call(bf16[2,128,128]{2,1,0:T(8,128)(2,1)S(1)} %get-tuple-element.73.s0, bf16[2,128,128]{2,1,0:T(8,128)(2,1)S(1)} %collective-permute-done.8.s1, bf16[2,128,128]{2,1,0:T(8,128)(2,1)S(1)} %collective-permute-done.9.s2, bf16[2,128,128]{2,1,0:T(8,128)(2,1)S(1)} %collective-permute-done.10.s3), custom_call_target="tpu_custom_call" | custom-call | flops 20000000000 | tf_op jit(solution)/shard_map/pallas_call | solution.py:439
  43.2 0.8 %collective-permute-done.18.g3 = bf16[272,128]{1,0:T(8,128)(2,1)S(1)} collective-permute-done((bf16[272,128]{1,0:T(8,128)(2,1)S(1)}, bf16[272,128]{1,0:T(8,128)(2,1)S(1)}, u32[]{:S(2)}, u32[]{:S(2)}) %collective-permute-start.18) | collective-permute-done | bytes 69664 | tf_op jit(solution)/shard_map/ppermute | solution.py:328
  44.0 0.8 %collective-permute-done.17.g2 = bf16[272,128]{1,0:T(8,128)(2,1)S(1)} collective-permute-done((bf16[272,128]{1,0:T(8,128)(2,1)S(1)}, bf16[272,128]{1,0:T(8,128)(2,1)S(1)}, u32[]{:S(2)}, u32[]{:S(2)}) %collective-permute-start.17) | collective-permute-done | bytes 69664 | tf_op jit(solution)/shard_map/ppermute | solution.py:328
  44.8 0.0 collective-permute-done.16.g1
  44.8 0.8 %shard_map.104 = (f32[1,1]{1,0:T(1,128)}, f32[8,64,128]{2,1,0:T(8,128)}, f32[8,64,128]{2,1,0:T(8,128)}) custom-call(bf16[272,128]{1,0:T(8,128)(2,1)S(1)} %shard_map.103.g0, bf16[272,128]{1,0:T(8,128)(2,1)S(1)} %collective-permute-done.16.g1, bf16[272,128]{1,0:T(8,128)(2,1)S(1)} %collective-permute-done.17.g2, bf16[272,128]{1,0:T(8,128)(2,1)S(1)} %collective-permute-done.18.g3), custom_call_target="tpu_custom_call" | custom-call | flops 1000000000 | tf_op jit(solution)/shard_map/pallas_call | solution.py:445
  (2 shorter events, 0.1 us)
Async XLA Ops:
  1.7 5.0 %copy-start.2 = (bf16[128,8,128]{2,1,0:T(8,128)(2,1)S(1)}, bf16[128,8,128]{2,1,0:T(8,128)(2,1)}, u32[]{:S(2)}) copy-start(bf16[128,8,128]{2,1,0:T(8,128)(2,1)} %param.9) | copy-start | bytes 786436
  1.7 5.0 %copy-start.3 = (bf16[128,8,128]{2,1,0:T(8,128)(2,1)S(1)}, bf16[128,8,128]{2,1,0:T(8,128)(2,1)}, u32[]{:S(2)}) copy-start(bf16[128,8,128]{2,1,0:T(8,128)(2,1)} %param.6) | copy-start | bytes 786436
  2.0 8.4 %collective-permute-start = (bf16[2,2,128,128]{3,2,1,0:T(8,128)(2,1)S(1)}, bf16[2,2,128,128]{3,2,1,0:T(8,128)(2,1)S(1)}, u32[]{:S(2)}, u32[]{:S(2)}) collective-permute-start(bf16[2,2,128,128]{3,2,1,0:T(8,128)(2,1)S(1)} %get-tuple-element.47), channel_id=1, source_target_pairs={{0,12},{4,8},{8,4},{12,0},{16,28},{20,24},{24,20},{28,16},{1,13},{... | collective-permute-start | bytes 393224 | tf_op jit(solution)/shard_map/ppermute | solution.py:328
  6.1 7.8 %collective-permute-start.1 = (bf16[2,2,128,128]{3,2,1,0:T(8,128)(2,1)S(1)}, bf16[2,2,128,128]{3,2,1,0:T(8,128)(2,1)S(1)}, u32[]{:S(2)}, u32[]{:S(2)}) collective-permute-start(bf16[2,2,128,128]{3,2,1,0:T(8,128)(2,1)S(1)} %get-tuple-element.48), channel_id=1, source_target_pairs={{0,4},{4,0},{8,12},{12,8},{16,20},{20,16},{24,28},{28,24},{1,5},{5... | collective-permute-start | bytes 393224 | tf_op jit(solution)/shard_map/ppermute | solution.py:328
  6.6 7.3 %collective-permute-start.2 = (bf16[2,2,128,128]{3,2,1,0:T(8,128)(2,1)S(1)}, bf16[2,2,128,128]{3,2,1,0:T(8,128)(2,1)S(1)}, u32[]{:S(2)}, u32[]{:S(2)}) collective-permute-start(bf16[2,2,128,128]{3,2,1,0:T(8,128)(2,1)S(1)} %get-tuple-element.49), channel_id=1, source_target_pairs={{0,8},{4,12},{8,0},{12,4},{16,24},{20,28},{24,16},{28,20},{1,9},{5... | collective-permute-start | bytes 393224 | tf_op jit(solution)/shard_map/ppermute | solution.py:328
  6.8 7.1 %copy-start = (bf16[8,64,128]{2,1,0:T(8,128)(2,1)S(1)}, bf16[8,64,128]{2,1,0:T(8,128)(2,1)}, u32[]{:S(2)}) copy-start(bf16[8,64,128]{2,1,0:T(8,128)(2,1)} %refs_11_.1) | copy-start | bytes 393220
  7.0 11.8 %collective-permute-start.5 = (bf16[2,2,128,128]{3,2,1,0:T(8,128)(2,1)S(1)}, bf16[2,2,128,128]{3,2,1,0:T(8,128)(2,1)S(1)}, u32[]{:S(2)}, u32[]{:S(2)}) collective-permute-start(bf16[2,2,128,128]{3,2,1,0:T(8,128)(2,1)S(1)} %get-tuple-element.56), channel_id=1, source_target_pairs={{0,12},{4,8},{8,4},{12,0},{16,28},{20,24},{24,20},{28,16},{1,13},{... | collective-permute-start | bytes 393224 | tf_op jit(solution)/shard_map/ppermute | solution.py:328
  9.9 8.9 %collective-permute-start.6 = (bf16[2,2,128,128]{3,2,1,0:T(8,128)(2,1)S(1)}, bf16[2,2,128,128]{3,2,1,0:T(8,128)(2,1)S(1)}, u32[]{:S(2)}, u32[]{:S(2)}) collective-permute-start(bf16[2,2,128,128]{3,2,1,0:T(8,128)(2,1)S(1)} %get-tuple-element.57), channel_id=1, source_target_pairs={{0,4},{4,0},{8,12},{12,8},{16,20},{20,16},{24,28},{28,24},{1,5},{5... | collective-permute-start | bytes 393224 | tf_op jit(solution)/shard_map/ppermute | solution.py:328
  10.5 8.4 %collective-permute-start.7 = (bf16[2,2,128,128]{3,2,1,0:T(8,128)(2,1)S(1)}, bf16[2,2,128,128]{3,2,1,0:T(8,128)(2,1)S(1)}, u32[]{:S(2)}, u32[]{:S(2)}) collective-permute-start(bf16[2,2,128,128]{3,2,1,0:T(8,128)(2,1)S(1)} %get-tuple-element.58), channel_id=1, source_target_pairs={{0,8},{4,12},{8,0},{12,4},{16,24},{20,28},{24,16},{28,20},{1,9},{5... | collective-permute-start | bytes 393224 | tf_op jit(solution)/shard_map/ppermute | solution.py:328
  14.5 6.9 %collective-permute-start.3 = (bf16[1,272,128]{2,1,0:T(8,128)(2,1)S(1)}, bf16[1,272,128]{2,1,0:T(8,128)(2,1)S(1)}, u32[]{:S(2)}, u32[]{:S(2)}) collective-permute-start(bf16[1,272,128]{2,1,0:T(8,128)(2,1)S(1)} %get-tuple-element.50), channel_id=1, source_target_pairs={{0,16},{4,20},{8,24},{12,28},{16,0},{20,4},{24,8},{28,12},{1,17},{... | collective-permute-start | bytes 208904 | tf_op jit(solution)/shard_map/ppermute | solution.py:328
  17.3 6.9 %collective-permute-start.4 = (bf16[1,272,128]{2,1,0:T(8,128)(2,1)S(1)}, bf16[1,272,128]{2,1,0:T(8,128)(2,1)S(1)}, u32[]{:S(2)}, u32[]{:S(2)}) collective-permute-start(bf16[1,272,128]{2,1,0:T(8,128)(2,1)S(1)} %get-tuple-element.51), channel_id=1, source_target_pairs={{0,16},{4,20},{8,24},{12,28},{16,0},{20,4},{24,8},{28,12},{1,17},{... | collective-permute-start | bytes 208904 | tf_op jit(solution)/shard_map/ppermute | solution.py:328
  17.5 1.3 %copy-start.1 = (bf16[8,64,128]{2,1,0:T(8,128)(2,1)S(1)}, bf16[8,64,128]{2,1,0:T(8,128)(2,1)}, u32[]{:S(2)}) copy-start(bf16[8,64,128]{2,1,0:T(8,128)(2,1)} %wq_ref.1) | copy-start | bytes 393220
  25.3 6.3 %collective-permute-start.11 = (bf16[2,144,128]{2,1,0:T(8,128)(2,1)S(1)}, bf16[2,144,128]{2,1,0:T(8,128)(2,1)S(1)}, u32[]{:S(2)}, u32[]{:S(2)}) collective-permute-start(bf16[2,144,128]{2,1,0:T(8,128)(2,1)S(1)} %get-tuple-element.77), channel_id=1, source_target_pairs={{0,16},{4,20},{8,24},{12,28},{16,0},{20,4},{24,8},{28,12},{1,17},{... | collective-permute-start | bytes 221192 | tf_op jit(solution)/shard_map/ppermute | solution.py:328
  26.3 4.4 %collective-permute-start.14 = (f32[8,128]{1,0:T(8,128)S(1)}, f32[8,128]{1,0:T(8,128)S(1)}, u32[]{:S(2)}, u32[]{:S(2)}) collective-permute-start(f32[8,128]{1,0:T(8,128)S(1)} %get-tuple-element.84.refs_7_), channel_id=1, source_target_pairs={{0,3},{1,2},{2,1},{3,0},{4,7},{5,6},{6,5},{7,4},{8,11},{9,10},{10,... | collective-permute-start | bytes 12296 | tf_op jit(solution)/shard_map/ppermute | solution.py:328
  26.5 4.3 %collective-permute-start.13 = (f32[8,128]{1,0:T(8,128)S(1)}, f32[8,128]{1,0:T(8,128)S(1)}, u32[]{:S(2)}, u32[]{:S(2)}) collective-permute-start(f32[8,128]{1,0:T(8,128)S(1)} %get-tuple-element.84.refs_7_), channel_id=1, source_target_pairs={{0,2},{1,3},{2,0},{3,1},{4,6},{5,7},{6,4},{7,5},{8,10},{9,11},{10,... | collective-permute-start | bytes 12296 | tf_op jit(solution)/shard_map/ppermute | solution.py:328
  27.8 2.9 %collective-permute-start.12 = (f32[8,128]{1,0:T(8,128)S(1)}, f32[8,128]{1,0:T(8,128)S(1)}, u32[]{:S(2)}, u32[]{:S(2)}) collective-permute-start(f32[8,128]{1,0:T(8,128)S(1)} %get-tuple-element.84.refs_7_), channel_id=1, source_target_pairs={{0,1},{1,0},{2,3},{3,2},{4,5},{5,4},{6,7},{7,6},{8,9},{9,8},{10,11... | collective-permute-start | bytes 12296 | tf_op jit(solution)/shard_map/ppermute | solution.py:328
  32.5 6.3 %collective-permute-start.15 = (bf16[272,128]{1,0:T(8,128)(2,1)S(1)}, bf16[272,128]{1,0:T(8,128)(2,1)S(1)}, u32[]{:S(2)}, u32[]{:S(2)}) collective-permute-start(bf16[272,128]{1,0:T(8,128)(2,1)S(1)} %shard_map.102.refs_0_), channel_id=1, source_target_pairs={{0,16},{4,20},{8,24},{12,28},{16,0},{20,4},{24,8},{28,12},{1,17},{... | collective-permute-start | bytes 208904 | tf_op jit(solution)/shard_map/ppermute | solution.py:328
  33.6 6.9 %collective-permute-start.8 = (bf16[2,128,128]{2,1,0:T(8,128)(2,1)S(1)}, bf16[2,128,128]{2,1,0:T(8,128)(2,1)S(1)}, u32[]{:S(2)}, u32[]{:S(2)}) collective-permute-start(bf16[2,128,128]{2,1,0:T(8,128)(2,1)S(1)} %get-tuple-element.74), channel_id=1, source_target_pairs={{0,4},{4,0},{8,12},{12,8},{16,20},{20,16},{24,28},{28,24},{1,5},{5... | collective-permute-start | bytes 196616 | tf_op jit(solution)/shard_map/ppermute | solution.py:328
  33.8 8.5 %collective-permute-start.9 = (bf16[2,128,128]{2,1,0:T(8,128)(2,1)S(1)}, bf16[2,128,128]{2,1,0:T(8,128)(2,1)S(1)}, u32[]{:S(2)}, u32[]{:S(2)}) collective-permute-start(bf16[2,128,128]{2,1,0:T(8,128)(2,1)S(1)} %get-tuple-element.75), channel_id=1, source_target_pairs={{0,8},{4,12},{8,0},{12,4},{16,24},{20,28},{24,16},{28,20},{1,9},{5... | collective-permute-start | bytes 196616 | tf_op jit(solution)/shard_map/ppermute | solution.py:328
  36.0 6.3 %collective-permute-start.10 = (bf16[2,128,128]{2,1,0:T(8,128)(2,1)S(1)}, bf16[2,128,128]{2,1,0:T(8,128)(2,1)S(1)}, u32[]{:S(2)}, u32[]{:S(2)}) collective-permute-start(bf16[2,128,128]{2,1,0:T(8,128)(2,1)S(1)} %get-tuple-element.76), channel_id=1, source_target_pairs={{0,12},{4,8},{8,4},{12,0},{16,28},{20,24},{24,20},{28,16},{1,13},{... | collective-permute-start | bytes 196616 | tf_op jit(solution)/shard_map/ppermute | solution.py:328
  38.8 5.3 %collective-permute-start.18 = (bf16[272,128]{1,0:T(8,128)(2,1)S(1)}, bf16[272,128]{1,0:T(8,128)(2,1)S(1)}, u32[]{:S(2)}, u32[]{:S(2)}) collective-permute-start(bf16[272,128]{1,0:T(8,128)(2,1)S(1)} %shard_map.103.g0), channel_id=1, source_target_pairs={{0,12},{4,8},{8,4},{12,0},{16,28},{20,24},{24,20},{28,16},{1,13},{... | collective-permute-start | bytes 208904 | tf_op jit(solution)/shard_map/ppermute | solution.py:328
  40.5 4.3 %collective-permute-start.17 = (bf16[272,128]{1,0:T(8,128)(2,1)S(1)}, bf16[272,128]{1,0:T(8,128)(2,1)S(1)}, u32[]{:S(2)}, u32[]{:S(2)}) collective-permute-start(bf16[272,128]{1,0:T(8,128)(2,1)S(1)} %shard_map.103.g0), channel_id=1, source_target_pairs={{0,8},{4,12},{8,0},{12,4},{16,24},{20,28},{24,16},{28,20},{1,9},{5... | collective-permute-start | bytes 208904 | tf_op jit(solution)/shard_map/ppermute | solution.py:328
  40.5 4.3 %collective-permute-start.16 = (bf16[272,128]{1,0:T(8,128)(2,1)S(1)}, bf16[272,128]{1,0:T(8,128)(2,1)S(1)}, u32[]{:S(2)}, u32[]{:S(2)}) collective-permute-start(bf16[272,128]{1,0:T(8,128)(2,1)S(1)} %shard_map.103.g0), channel_id=1, source_target_pairs={{0,4},{4,0},{8,12},{12,8},{16,20},{20,16},{24,28},{28,24},{1,5},{5... | collective-permute-start | bytes 208904 | tf_op jit(solution)/shard_map/ppermute | solution.py:328

commit v5 on v4

--- a/solution.py
+++ b/solution.py
@@ -11,7 +11,8 @@
 QUAD = 4
 F32 = jnp.float32
 BF16 = jnp.bfloat16
-SPREAD = (0, 3, 1, 2)
+KEYS_FIRST = (0, 3, 1, 2)
+QUERIES_FIRST = (0, 1, 3, 2)
 KEY_US, FEATURE_US, OWN_US, OUT_US, GRAD_US, STUDENT_US = 20.0, 1.0, 20.0, 1.0, 0.2, 20.0
 
 
@@ -80,19 +81,27 @@
         out[...] = held[lax.bitwise_xor(mine, j)]
 
 
+def norm_rows(norm):
+    high, low = split2(norm)
+    row = lax.broadcasted_iota(jnp.int32, (16, norm.shape[1]), 0)
+    both = jnp.where(row == 0, high.astype(F32), jnp.where(row == 1, low.astype(F32), 0.0))
+    return both.astype(BF16)
+
+
 def put_loss(out_ref, first, loss):
     high, low = split2(loss)
     out_ref[first:] = jnp.concatenate([high, low], axis=0)
 
 
 def take_loss(ref, first):
-    return ref[first : first + 8].astype(F32) + ref[first + 8 : first + 16].astype(F32)
+    both = ref[first : first + 16].astype(F32)
+    return both[:8] + both[8:]
 
 
 def key_kernel(c0, c1, c2, c3, wk_ref, kv_ref, *msg_refs):
     mine, _, _ = place_in_group()
     narr, per, tok, d = c0.shape
-    for j, c in zip(SPREAD, (c0, c1, c2, c3)):
+    for j, c in zip(KEYS_FIRST, (c0, c1, c2, c3)):
         kv_ref[:, :, lax.bitwise_xor(mine, j)] = c[...]
     total = QUAD * tok
     for hh in range(per):
@@ -101,9 +110,10 @@
         feat = jnp.concatenate(phi_t(k, wk_ref[per * mine + hh]), axis=0)
         lane = lax.broadcasted_iota(jnp.int32, feat.shape, 1)
         feat = jnp.where(lane < total - WIN, feat, 0.0).astype(BF16)
-        state = nt(extended(transposed(v).astype(BF16)), feat).astype(BF16)
+        state = nt(extended(transposed(v).astype(BF16)), feat)
         rows = state.shape[0]
-        msg_refs[hh][0, :rows] = state
+        msg_refs[hh][0, :d] = state[:d].astype(BF16)
+        msg_refs[hh][0, d:rows] = norm_rows(state[d : d + 1])
         msg_refs[hh][0, rows : rows + WIN] = k[total - WIN :]
         msg_refs[hh][0, rows + WIN :] = v[total - WIN :]
 
@@ -130,12 +140,13 @@
     narr, per, tok, d = c0.shape
     total = QUAD * tok
     scale = 1.0 / d**0.5
-    for j, c in zip(SPREAD, (c0, c1, c2, c3)):
+    for j, c in zip(QUERIES_FIRST, (c0, c1, c2, c3)):
         qt_ref[:, :, lax.bitwise_xor(mine, j)] = c[...]
     row = lax.broadcasted_iota(jnp.int32, (tok + WIN, tok), 0)
     col = lax.broadcasted_iota(jnp.int32, (tok + WIN, tok), 1)
     inside = (row > col) & (row <= col + WIN)
-    causal = (row <= col)[:tok]
+    wide = 2 * tok
+    causal = lax.broadcasted_iota(jnp.int32, (wide, wide), 0) <= lax.broadcasted_iota(jnp.int32, (wide, wide), 1)
     for hh in range(per):
         q = qt_ref[0, hh].reshape(total, d)
         none = jnp.zeros((WIN, d), BF16)
@@ -155,11 +166,13 @@
             weight = jnp.exp(score - top).astype(BF16)
             win_ref[hh, :, lo:hi] = nn(vt[:, lo : hi + WIN], weight)
             top_ref[hh, :, lo:hi] = jnp.broadcast_to(top, (8, tok))
+            teach_ref[hh, :, lo:hi] = transposed(qt_ref[1, hh, b])
+        for lo in range(0, total, wide):
+            hi = lo + wide
             amat = nn(fk_rows[:hi], fq[:, lo:hi])
             last = jnp.where(causal, amat[lo:], 0.0)
-            amat = jnp.concatenate([amat[:lo], last], axis=0).astype(BF16) if b else last.astype(BF16)
+            amat = jnp.concatenate([amat[:lo], last], axis=0).astype(BF16) if lo else last.astype(BF16)
             lin_ref[hh, :, lo:hi] = nn(vt[:, :hi], amat)
-            teach_ref[hh, :, lo:hi] = transposed(qt_ref[1, hh, b])
 
 
 def out_kernel(hh, qt_ref, teach_ref, win_ref, top_ref, lin_ref, fq_ref, msg_ref, wk_ref, *refs):
@@ -178,7 +191,7 @@
     vt = extended(transposed(msg_ref[0, d + 16 + WIN :]).astype(BF16))
     fk = jnp.concatenate(phi_t(halo_k, wk_ref[per * mine + hh]), axis=0)
     fk = jnp.where(has_past, fk, 0.0).astype(BF16)
-    amat = nn(transposed(fk).astype(BF16), fq)
+    amat = lax.dot_general(fk, fq, (((0,), (0,)), ((), ())), preferred_element_type=F32)
     amat = jnp.where(row <= col, amat, 0.0).astype(BF16)
     lin = lin_ref[hh] + nn(state, fq) + nn(vt, amat)
     score = nt(halo_k, qt_ref[0, hh, 0]) * scale
@@ -193,7 +206,7 @@
     win_scale = jnp.where(early, 1.0, jnp.exp(jnp.minimum(top, 0.0)))
     lin_scale = jnp.where(early, 0.0, jnp.exp(-jnp.maximum(top, 0.0)))
     both = win_scale * win + lin_scale * lin
-    inverse = 1.0 / both[d : d + 1]
+    inverse = 1.0 / (both[d : d + 1] + both[d + 1 : d + 2])
     out = both[:d] * inverse
     out_ref[...] = out.astype(BF16)
     diff = out - teach_ref[hh]
@@ -207,9 +220,11 @@
     g_num = coef * g
     g_den = -coef * jnp.sum(g * out, axis=0, keepdims=True)
     pad = lax.broadcasted_iota(jnp.int32, (16, total), 0)
-    g_ext = jnp.concatenate([g_num, jnp.where(pad == 0, g_den, 0.0)], axis=0).astype(BF16)
+    g_ext = jnp.concatenate([g_num, jnp.where(pad <= 1, g_den, 0.0)], axis=0).astype(BF16)
     grad_ref[...] = g_ext
-    later_ref[hh] = nt(g_ext, fq).astype(BF16)
+    feat = fq.shape[0]
+    later_ref[hh, :feat] = nt(fq, g_ext[:d]).astype(BF16)
+    later_ref[hh, feat:] = norm_rows(nt(g_ext[d:], fq)[:1])
 
 
 def grad_kernel(per, *refs):
@@ -219,7 +234,8 @@
     mine, has_past, _ = place_in_group()
     _, _, _, tok, d = qt_ref.shape
     total = QUAD * tok
-    causal = lax.broadcasted_iota(jnp.int32, (tok, tok), 0) <= lax.broadcasted_iota(jnp.int32, (tok, tok), 1)
+    wide = 2 * tok
+    causal = lax.broadcasted_iota(jnp.int32, (wide, wide), 0) <= lax.broadcasted_iota(jnp.int32, (wide, wide), 1)
     for hh in range(per):
         state = jnp.where(has_past, msg_refs[hh][0, : d + 16].astype(F32), 0.0).astype(BF16)
         k = jnp.concatenate([msg_refs[hh][0, d + 16 : d + 16 + WIN], kv_ref[0, hh].reshape(total, d)[: total - WIN]], axis=0)
@@ -233,16 +249,16 @@
         fk = jnp.where(valid, fk, 0.0).astype(BF16)
         fq = fq_ref[hh]
         g_ext = grad_refs[hh][...]
-        g_num, g_den = g_ext[:d], g_ext[d : d + 1].astype(F32)
+        g_num, g_den = g_ext[:d], g_ext[d:].astype(F32)[:1]
         grad_q = nn(transposed(state).astype(BF16), g_ext)
         grad_k = []
-        for c in range(QUAD):
-            lo, hi = c * tok, (c + 1) * tok
+        for lo in range(0, total, wide):
+            hi = lo + wide
             mix = nn(v[lo:hi], g_num[:, lo:]) + g_den[:, lo:]
-            first = jnp.where(causal, mix[:, :tok], 0.0)
-            mix = (jnp.concatenate([first, mix[:, tok:]], axis=1) if hi < total else first).astype(BF16)
+            first = jnp.where(causal, mix[:, :wide], 0.0)
+            mix = (jnp.concatenate([first, mix[:, wide:]], axis=1) if hi < total else first).astype(BF16)
             more = nn(fk[:, lo:hi], mix)
-            grad_q = grad_q + (jnp.concatenate([jnp.zeros((more.shape[0], lo), F32), more], axis=1) if c else more)
+            grad_q = grad_q + (jnp.concatenate([jnp.zeros((more.shape[0], lo), F32), more], axis=1) if lo else more)
             grad_k.append(nt(fq[:, lo:], mix))
         grad_k = jnp.where(valid, jnp.concatenate(grad_k, axis=1), 0.0)
         for x, ups, downs, grad, ref in (
@@ -262,8 +278,9 @@
     _, has_past, has_future = place_in_group()
     per, half, d = gq_ref.shape
     for hh in range(per):
-        after = transposed(later_ref[hh])
-        grad = nt(after[:, :d].astype(BF16), v_ref[hh]) + after[:, d : d + 1]
+        feat = 2 * half
+        norm = transposed(later_ref[hh, feat:])
+        grad = nt(later_ref[hh, :feat], v_ref[hh]) + (norm[:, :1] + norm[:, 1:2])
         lane = lax.broadcasted_iota(jnp.int32, grad.shape, 1)
         grad = jnp.where(((lane >= WIN) | has_past) & has_future, grad, 0.0)
         high, low = split2(phi_pull(kup_ref[hh], kdown_ref[hh], grad))
@@ -328,8 +345,8 @@
     return lax.ppermute(x, axis, [(i, i ^ by) for i in range(lax.axis_size(axis))])
 
 
-def spread(parts):
-    return [flip(parts[j], "ctx", j) if j else parts[j] for j in SPREAD]
+def spread(parts, order):
+    return [flip(parts[j], "ctx", j) if j else parts[j] for j in order]
 
 
 def state_over_groups(msg, d, wk, head, group, groups, members):
@@ -347,7 +364,8 @@
     state = jnp.sum(jnp.where(place < group, every[:, :, : d + 16].astype(F32), 0.0), axis=0)
     state = state + jnp.sum(jnp.where(place < group - 1, tail, 0.0), axis=0)
     halo = lax.dynamic_index_in_dim(every, jnp.maximum(group - 1, 0), 0, keepdims=False)
-    return jnp.concatenate([state.astype(BF16), halo[:, d + 16 :]], axis=1)
+    norm = norm_rows(state[0, d : d + 1] + state[0, d + 1 : d + 2])[None]
+    return jnp.concatenate([state[:, :d].astype(BF16), norm, halo[:, d + 16 :]], axis=1)
 
 
 def later_over_groups(later, group, groups, members):
@@ -355,7 +373,10 @@
         return flip(later, "ctx", QUAD)
     every = lax.all_gather(later, "ctx", axis_index_groups=members).astype(F32)
     place = jnp.arange(groups)[:, None, None, None]
-    return jnp.sum(jnp.where(place > group, every, 0.0), axis=0).astype(BF16)
+    state = jnp.sum(jnp.where(place > group, every, 0.0), axis=0)
+    feat = state.shape[1] - 16
+    norm = jnp.stack([norm_rows(head[feat : feat + 1] + head[feat + 1 : feat + 2]) for head in state])
+    return jnp.concatenate([state[:, :feat].astype(BF16), norm], axis=1)
 
 
 def sum_over_groups(part, groups, members):
@@ -384,9 +405,8 @@
         ],
         ins=1,
     )
-    kv = pack(jnp.concatenate([keys, values]))
-    kv = spread(kv)
-    qt = spread(pack(jnp.concatenate([queries, teacher])))
+    kv = spread(pack(jnp.concatenate([keys, values])), KEYS_FIRST)
+    qt = spread(pack(jnp.concatenate([queries, teacher])), QUERIES_FIRST)
 
     rows = d + 16 + 2 * WIN
     kv, *msgs = call(
@@ -413,7 +433,7 @@
     for hh in range(per):
         out, later, g_out, loss = call(
             functools.partial(out_kernel, hh),
-            [shape(d, total), shape(hh + 1, d + 16, 2 * half), shape(d + 16, total), shape(8, tok, dtype=F32)],
+            [shape(d, total), shape(hh + 1, 2 * half + 16, d), shape(d + 16, total), shape(8, tok, dtype=F32)],
             ins=8 + len(before), micros=OUT_US,
         )(qt, teach, win, top, lin, fq, msgs[hh], wk, *before)
         outs.append(out)

time: 45.8 us -> 45.7 us (level)
  Pallas kernels: 12.2 us -> 11.7 us
    pallas_call x1, Pallas kernels: 2.51 us -> 1.99 us  [per_device(): call(functools.partial(grad_kernel, per), [shape(per, tok, d)] * QUAD + [...]
  transfers between devices with their start and end apart: 19 -> 19, of which waited for: 6 -> 8; matrix products, arithmetic and copies ran while one was open for 0% -> 0% of each run, Pallas kernels for 20% -> 19%
where the time goes in v5:
time: 45.7 us; the launch traced here: 45.5 us
  starting transfers between devices  24.1 us (53%)
  Pallas kernels  11.7 us (26%)
  waiting for transfers between devices  7.76 us (17%)
  other arithmetic  1.12 us (2%)
  between operations  0.77 us (2%)
    ppermute x19, starting transfers between devices, flip(): lax.ppermute(x, axis, [(i, i ^ by) for i in range(lax.axis_size(axis))])  24.1 us
    ppermute x19, waiting for transfers between devices, flip(): lax.ppermute(x, axis, [(i, i ^ by) for i in range(lax.axis_size(axis))])  7.76 us
    pallas_call x1, Pallas kernels, per_device(): call(own_kernel, [shape(2, per, QUAD, tok, d), shape(per, d, total, dtype...  2.64 us
    pallas_call x2, Pallas kernels, per_device(): call(functools.partial(out_kernel, hh), [shape(d, total), shape(hh + 1, 2...  2.01 us
    pallas_call x1, Pallas kernels, per_device(): call(functools.partial(grad_kernel, per), [shape(per, tok, d)] * QUAD + [...  1.99 us
    pallas_call x1, Pallas kernels, per_device(): call(feature_kernel, [shape(per, 2 * half, total), shape(per, total, 2 *...  1.29 us
    concatenate x1, other arithmetic, per_device(): kv = spread(pack(jnp.concatenate([keys, values])), KEYS_FIRST)  1.08 us
  transfers between devices with their start and end apart: 19, of which 8 were waited for; matrix products, arithmetic and copies ran while one was open for 0% of the time, Pallas kernels for 19%

profile of v5, /device:TPU:0, one launch (start us, length us, event | category | flops | bytes accessed | tf_op | source)
XLA Modules:
  0.0 45.5 jit_solution(6489028704919011551)
XLA Ops:
  0.6 1.1 %pad_maximum_fusion.refs_0_ = bf16[256,8,128]{2,1,0:T(8,128)(2,1)S(1)} fusion(bf16[128,8,128]{2,1,0:T(8,128)(2,1)} %param.8, bf16[128,8,128]{2,1,0:T(8,128)(2,1)} %param.7), kind=kLoop, calls=%fused_computation | loop fusion | flops 262144 | bytes 1048576 | tf_op jit(solution)/shard_map/concatenate | solution.py:408
  1.7 0.0 copy-start.2
  1.7 0.0 copy-start.3
  1.7 0.3 shard_map.93
  2.0 4.0 %collective-permute-start = (bf16[2,2,128,128]{3,2,1,0:T(8,128)(2,1)S(1)}, bf16[2,2,128,128]{3,2,1,0:T(8,128)(2,1)S(1)}, u32[]{:S(2)}, u32[]{:S(2)}) collective-permute-start(bf16[2,2,128,128]{3,2,1,0:T(8,128)(2,1)S(1)} %get-tuple-element.47), channel_id=1, source_target_pairs={{0,12},{4,8},{8,4},{12,0},{16,28},{20,24},{24,20},{28,16},{1,13},{... | collective-permute-start | bytes 393224 | tf_op jit(solution)/shard_map/ppermute | solution.py:345
  6.1 0.5 %collective-permute-start.1 = (bf16[2,2,128,128]{3,2,1,0:T(8,128)(2,1)S(1)}, bf16[2,2,128,128]{3,2,1,0:T(8,128)(2,1)S(1)}, u32[]{:S(2)}, u32[]{:S(2)}) collective-permute-start(bf16[2,2,128,128]{3,2,1,0:T(8,128)(2,1)S(1)} %get-tuple-element.48), channel_id=1, source_target_pairs={{0,4},{4,0},{8,12},{12,8},{16,20},{20,16},{24,28},{28,24},{1,5},{5... | collective-permute-start | bytes 393224 | tf_op jit(solution)/shard_map/ppermute | solution.py:345
  6.6 0.1 collective-permute-start.2
  6.7 0.0 copy-done.2
  6.7 0.0 copy-done.3
  6.8 0.0 copy-start
  6.8 0.3 shard_map.96
  7.0 1.9 %collective-permute-start.5 = (bf16[2,2,128,128]{3,2,1,0:T(8,128)(2,1)S(1)}, bf16[2,2,128,128]{3,2,1,0:T(8,128)(2,1)S(1)}, u32[]{:S(2)}, u32[]{:S(2)}) collective-permute-start(bf16[2,2,128,128]{3,2,1,0:T(8,128)(2,1)S(1)} %get-tuple-element.56), channel_id=1, source_target_pairs={{0,4},{4,0},{8,12},{12,8},{16,20},{20,16},{24,28},{28,24},{1,5},{5... | collective-permute-start | bytes 393224 | tf_op jit(solution)/shard_map/ppermute | solution.py:345
  8.9 1.5 %collective-permute-start.6 = (bf16[2,2,128,128]{3,2,1,0:T(8,128)(2,1)S(1)}, bf16[2,2,128,128]{3,2,1,0:T(8,128)(2,1)S(1)}, u32[]{:S(2)}, u32[]{:S(2)}) collective-permute-start(bf16[2,2,128,128]{3,2,1,0:T(8,128)(2,1)S(1)} %get-tuple-element.57), channel_id=1, source_target_pairs={{0,12},{4,8},{8,4},{12,0},{16,28},{20,24},{24,20},{28,16},{1,13},{... | collective-permute-start | bytes 393224 | tf_op jit(solution)/shard_map/ppermute | solution.py:345
  10.5 0.0 collective-permute-done.c1
  10.5 1.9 %collective-permute-start.7 = (bf16[2,2,128,128]{3,2,1,0:T(8,128)(2,1)S(1)}, bf16[2,2,128,128]{3,2,1,0:T(8,128)(2,1)S(1)}, u32[]{:S(2)}, u32[]{:S(2)}) collective-permute-start(bf16[2,2,128,128]{3,2,1,0:T(8,128)(2,1)S(1)} %get-tuple-element.58), channel_id=1, source_target_pairs={{0,8},{4,12},{8,0},{12,4},{16,24},{20,28},{24,16},{28,20},{1,9},{5... | collective-permute-start | bytes 393224 | tf_op jit(solution)/shard_map/ppermute | solution.py:345
  12.4 1.4 %collective-permute-done.1.c2 = bf16[2,2,128,128]{3,2,1,0:T(8,128)(2,1)S(1)} collective-permute-done((bf16[2,2,128,128]{3,2,1,0:T(8,128)(2,1)S(1)}, bf16[2,2,128,128]{3,2,1,0:T(8,128)(2,1)S(1)}, u32[]{:S(2)}, u32[]{:S(2)}) %collective-permute-start.1) | collective-permute-done | bytes 131104 | tf_op jit(solution)/shard_map/ppermute | solution.py:345
  13.8 0.0 collective-permute-done.2.c3
  13.8 0.0 copy-done
  13.8 0.7 %shard_map.94 = (bf16[2,2,4,128,128]{4,3,2,1,0:T(8,128)(2,1)S(1)}, bf16[1,272,128]{2,1,0:T(8,128)(2,1)S(1)}, bf16[1,272,128]{2,1,0:T(8,128)(2,1)S(1)}) custom-call(bf16[2,2,128,128]{3,2,1,0:T(8,128)(2,1)S(1)} %get-tuple-element.46.c0, bf16[2,2,128,128]{3,2,1,0:T(8,128)(2,1)S(1)} %collective-permute-done.c1, ...), custom_call_target="tpu_custom_call" | custom-call | flops 20000000000 | tf_op jit(solution)/shard_map/pallas_call | solution.py:412
  14.5 2.8 %collective-permute-start.3 = (bf16[1,272,128]{2,1,0:T(8,128)(2,1)S(1)}, bf16[1,272,128]{2,1,0:T(8,128)(2,1)S(1)}, u32[]{:S(2)}, u32[]{:S(2)}) collective-permute-start(bf16[1,272,128]{2,1,0:T(8,128)(2,1)S(1)} %get-tuple-element.50), channel_id=1, source_target_pairs={{0,16},{4,20},{8,24},{12,28},{16,0},{20,4},{24,8},{28,12},{1,17},{... | collective-permute-start | bytes 208904 | tf_op jit(solution)/shard_map/ppermute | solution.py:345
  17.3 0.2 collective-permute-start.4
  17.4 0.0 copy-start.1
  17.5 1.3 %shard_map.95 = (bf16[2,128,512]{2,1,0:T(8,128)(2,1)}, bf16[2,512,128]{2,1,0:T(8,128)(2,1)S(1)}, bf16[2,144,640]{2,1,0:T(8,128)(2,1)S(1)}) custom-call(bf16[2,2,4,128,128]{4,3,2,1,0:T(8,128)(2,1)S(1)} %get-tuple-element.52.kv_ref.refs_6_, bf16[8,64,128]{2,1,0:T(8,128)(2,1)S(1)} %copy-done), custom_call_target="tpu_custom_call" | custom-call | flops 1000000000 | tf_op jit(solution)/shard_map/pallas_call | solution.py:421
  18.7 0.0 collective-permute-done.5.c1
  18.7 0.0 collective-permute-done.6.c2
  18.7 0.1 collective-permute-done.7.c3
  18.9 0.0 copy-done.1
  18.9 2.6 %shard_map.97 = (bf16[2,2,4,128,128]{4,3,2,1,0:T(8,128)(2,1)S(1)}, f32[2,128,512]{2,1,0:T(8,128)S(1)}, f32[2,144,512]{2,1,0:T(8,128)S(1)}, f32[2,8,512]{2,1,0:T(...) custom-call(bf16[2,2,4,128,128]{4,3,2,1,0:T(8,128)(2,1)S(1)} %get-tu, ...), custom_call_target="tpu_custom_call" | custom-call | flops 20000000000 | tf_op jit(solution)/shard_map/pallas_call | solution.py:426
  21.5 0.0 collective-permute-done.3.msg_ref.refs_0_
  21.5 1.0 %shard_map.98 = (bf16[128,512]{1,0:T(8,128)(2,1)S(1)}, bf16[1,144,128]{2,1,0:T(8,128)(2,1)S(1)}, bf16[144,512]{1,0:T(8,128)(2,1)S(1)}, f32[8,128]{1,0:T(8,128)S(1)}) custom-call(bf16[2,2,4,128,128]{4,3,2,1,0:T(8,128)(2,1)S(1)} %get-tuple-element.59.qt_ref.refs_7_, f32[2,128,512]{2,1,0:T(8,128)S(1)} %get-tuple-element.60.teach_ref, ...), custom_call_target="tpu_custom_call" | custom-call | flops 1000000000 | tf_op jit(solution)/shard_map/pallas_call | solution.py:434
  22.6 1.7 %collective-permute-done.4.msg_ref.refs_1_ = bf16[1,272,128]{2,1,0:T(8,128)(2,1)S(1)} collective-permute-done((bf16[1,272,128]{2,1,0:T(8,128)(2,1)S(1)}, bf16[1,272,128]{2,1,0:T(8,128)(2,1)S(1)}, u32[]{:S(2)}, u32[]{:S(2)}) %collective-permute-start.4) | collective-permute-done | bytes 69664 | tf_op jit(solution)/shard_map/ppermute | solution.py:345
  24.2 1.0 %shard_map.99 = (bf16[128,512]{1,0:T(8,128)(2,1)S(1)}, bf16[2,144,128]{2,1,0:T(8,128)(2,1)S(1)}, bf16[144,512]{1,0:T(8,128)(2,1)S(1)}, f32[8,128]{1,0:T(8,128)S(1)}) custom-call(bf16[2,2,4,128,128]{4,3,2,1,0:T(8,128)(2,1)S(1)} %get-tuple-element.59.qt_ref.refs_7_, f32[2,128,512]{2,1,0:T(8,128)S(1)} %get-tuple-element.60.teach_ref, ...), custom_call_target="tpu_custom_call" | custom-call | flops 1000000000 | tf_op jit(solution)/shard_map/pallas_call | solution.py:434
  25.2 1.1 %collective-permute-start.11 = (bf16[2,144,128]{2,1,0:T(8,128)(2,1)S(1)}, bf16[2,144,128]{2,1,0:T(8,128)(2,1)S(1)}, u32[]{:S(2)}, u32[]{:S(2)}) collective-permute-start(bf16[2,144,128]{2,1,0:T(8,128)(2,1)S(1)} %get-tuple-element.77), channel_id=1, source_target_pairs={{0,16},{4,20},{8,24},{12,28},{16,0},{20,4},{24,8},{28,12},{1,17},{... | collective-permute-start | bytes 221192 | tf_op jit(solution)/shard_map/ppermute | solution.py:345
  26.3 0.0 collective-permute-start.14
  26.3 1.5 %collective-permute-start.13 = (f32[8,128]{1,0:T(8,128)S(1)}, f32[8,128]{1,0:T(8,128)S(1)}, u32[]{:S(2)}, u32[]{:S(2)}) collective-permute-start(f32[8,128]{1,0:T(8,128)S(1)} %get-tuple-element.84.refs_7_), channel_id=1, source_target_pairs={{0,2},{1,3},{2,0},{3,1},{4,6},{5,7},{6,4},{7,5},{8,10},{9,11},{10,... | collective-permute-start | bytes 12296 | tf_op jit(solution)/shard_map/ppermute | solution.py:345
  27.8 0.3 collective-permute-start.12
  28.1 2.0 %shard_map.100 = (bf16[2,128,128]{2,1,0:T(8,128)(2,1)S(1)}, bf16[2,128,128]{2,1,0:T(8,128)(2,1)S(1)}, bf16[2,128,128]{2,1,0:T(8,128)(2,1)S(1)}, bf16[2,128,128]{...) custom-call(bf16[1,272,128]{2,1,0:T(8,128)(2,1)S(1)} %collective-per, ...), custom_call_target="tpu_custom_call" | custom-call | flops 200000000 | tf_op jit(solution)/shard_map/pallas_call | solution.py:444
  30.1 0.0 collective-permute-done.14.refs_10_
  30.1 0.0 collective-permute-done.13.refs_9_
  30.2 0.0 collective-permute-done.12.refs_8_
  30.2 1.3 %collective-permute-done.11.refs_0_ = bf16[2,144,128]{2,1,0:T(8,128)(2,1)S(1)} collective-permute-done((bf16[2,144,128]{2,1,0:T(8,128)(2,1)S(1)}, bf16[2,144,128]{2,1,0:T(8,128)(2,1)S(1)}, u32[]{:S(2)}, u32[]{:S(2)}) %collective-permute-start.11) | collective-permute-done | bytes 73760 | tf_op jit(solution)/shard_map/ppermute | solution.py:345
  31.5 0.9 %shard_map.102.refs_0_ = bf16[272,128]{1,0:T(8,128)(2,1)S(1)} custom-call(bf16[2,144,128]{2,1,0:T(8,128)(2,1)S(1)} %collective-permute-done.11.refs_0_, bf16[2,512,128]{2,1,0:T(8,128)(2,1)S(1)} %get-tuple-element.78.refs_1_, bf16[2,512,128]{2,1,0:T(8,128)(2,1)S(1)} %get-tuple-element.79.refs_2_, f32[2,64,512]{2,1,0:T(8,128)S(1)} %get-tuple-element.80.refs_3_, ...), custom_call_target="tpu_custom_call" | custom-call | flops 1000000000 | tf_op jit(solution)/shard_map/pallas_call | solution.py:452
  32.3 0.9 %collective-permute-start.15 = (bf16[272,128]{1,0:T(8,128)(2,1)S(1)}, bf16[272,128]{1,0:T(8,128)(2,1)S(1)}, u32[]{:S(2)}, u32[]{:S(2)}) collective-permute-start(bf16[272,128]{1,0:T(8,128)(2,1)S(1)} %shard_map.102.refs_0_), channel_id=1, source_target_pairs={{0,16},{4,20},{8,24},{12,28},{16,0},{20,4},{24,8},{28,12},{1,17},{... | collective-permute-start | bytes 208904 | tf_op jit(solution)/shard_map/ppermute | solution.py:345
  33.3 0.5 %collective-permute-start.8 = (bf16[2,128,128]{2,1,0:T(8,128)(2,1)S(1)}, bf16[2,128,128]{2,1,0:T(8,128)(2,1)S(1)}, u32[]{:S(2)}, u32[]{:S(2)}) collective-permute-start(bf16[2,128,128]{2,1,0:T(8,128)(2,1)S(1)} %get-tuple-element.74), channel_id=1, source_target_pairs={{0,4},{4,0},{8,12},{12,8},{16,20},{20,16},{24,28},{28,24},{1,5},{5... | collective-permute-start | bytes 196616 | tf_op jit(solution)/shard_map/ppermute | solution.py:345
  33.8 2.3 %collective-permute-start.9 = (bf16[2,128,128]{2,1,0:T(8,128)(2,1)S(1)}, bf16[2,128,128]{2,1,0:T(8,128)(2,1)S(1)}, u32[]{:S(2)}, u32[]{:S(2)}) collective-permute-start(bf16[2,128,128]{2,1,0:T(8,128)(2,1)S(1)} %get-tuple-element.75), channel_id=1, source_target_pairs={{0,8},{4,12},{8,0},{12,4},{16,24},{20,28},{24,16},{28,20},{1,9},{5... | collective-permute-start | bytes 196616 | tf_op jit(solution)/shard_map/ppermute | solution.py:345
  36.0 0.9 %collective-permute-start.10 = (bf16[2,128,128]{2,1,0:T(8,128)(2,1)S(1)}, bf16[2,128,128]{2,1,0:T(8,128)(2,1)S(1)}, u32[]{:S(2)}, u32[]{:S(2)}) collective-permute-start(bf16[2,128,128]{2,1,0:T(8,128)(2,1)S(1)} %get-tuple-element.76), channel_id=1, source_target_pairs={{0,12},{4,8},{8,4},{12,0},{16,28},{20,24},{24,20},{28,16},{1,13},{... | collective-permute-start | bytes 196616 | tf_op jit(solution)/shard_map/ppermute | solution.py:345
  37.0 1.7 %collective-permute-done.15.refs_1_ = bf16[272,128]{1,0:T(8,128)(2,1)S(1)} collective-permute-done((bf16[272,128]{1,0:T(8,128)(2,1)S(1)}, bf16[272,128]{1,0:T(8,128)(2,1)S(1)}, u32[]{:S(2)}, u32[]{:S(2)}) %collective-permute-start.15) | collective-permute-done | bytes 69664 | tf_op jit(solution)/shard_map/ppermute | solution.py:345
  38.7 1.1 %collective-permute-start.18 = (bf16[272,128]{1,0:T(8,128)(2,1)S(1)}, bf16[272,128]{1,0:T(8,128)(2,1)S(1)}, u32[]{:S(2)}, u32[]{:S(2)}) collective-permute-start(bf16[272,128]{1,0:T(8,128)(2,1)S(1)} %shard_map.103.g0), channel_id=1, source_target_pairs={{0,12},{4,8},{8,4},{12,0},{16,28},{20,24},{24,20},{28,16},{1,13},{... | collective-permute-start | bytes 208904 | tf_op jit(solution)/shard_map/ppermute | solution.py:345
  39.8 0.4 collective-permute-start.17
  40.2 0.0 collective-permute-done.8.s1
  40.2 2.1 %collective-permute-start.16 = (bf16[272,128]{1,0:T(8,128)(2,1)S(1)}, bf16[272,128]{1,0:T(8,128)(2,1)S(1)}, u32[]{:S(2)}, u32[]{:S(2)}) collective-permute-start(bf16[272,128]{1,0:T(8,128)(2,1)S(1)} %shard_map.103.g0), channel_id=1, source_target_pairs={{0,4},{4,0},{8,12},{12,8},{16,20},{20,16},{24,28},{28,24},{1,5},{5... | collective-permute-start | bytes 208904 | tf_op jit(solution)/shard_map/ppermute | solution.py:345
  42.2 0.0 collective-permute-done.9.s2
  42.2 0.0 collective-permute-done.10.s3
  42.2 0.9 %shard_map.101 = bf16[128,8,128]{2,1,0:T(8,128)(2,1)} custom-call(bf16[2,128,128]{2,1,0:T(8,128)(2,1)S(1)} %get-tuple-element.73.s0, bf16[2,128,128]{2,1,0:T(8,128)(2,1)S(1)} %collective-permute-done.8.s1, bf16[2,128,128]{2,1,0:T(8,128)(2,1)S(1)} %collective-permute-done.9.s2, bf16[2,128,128]{2,1,0:T(8,128)(2,1)S(1)} %collective-permute-done.10.s3), custom_call_target="tpu_custom_call" | custom-call | flops 20000000000 | tf_op jit(solution)/shard_map/pallas_call | solution.py:459
  43.1 0.8 %collective-permute-done.18.g3 = bf16[272,128]{1,0:T(8,128)(2,1)S(1)} collective-permute-done((bf16[272,128]{1,0:T(8,128)(2,1)S(1)}, bf16[272,128]{1,0:T(8,128)(2,1)S(1)}, u32[]{:S(2)}, u32[]{:S(2)}) %collective-permute-start.18) | collective-permute-done | bytes 69664 | tf_op jit(solution)/shard_map/ppermute | solution.py:345
  44.0 0.2 collective-permute-done.17.g2
  44.1 0.6 %collective-permute-done.16.g1 = bf16[272,128]{1,0:T(8,128)(2,1)S(1)} collective-permute-done((bf16[272,128]{1,0:T(8,128)(2,1)S(1)}, bf16[272,128]{1,0:T(8,128)(2,1)S(1)}, u32[]{:S(2)}, u32[]{:S(2)}) %collective-permute-start.16) | collective-permute-done | bytes 69664 | tf_op jit(solution)/shard_map/ppermute | solution.py:345
  44.7 0.8 %shard_map.104 = (f32[1,1]{1,0:T(1,128)}, f32[8,64,128]{2,1,0:T(8,128)}, f32[8,64,128]{2,1,0:T(8,128)}) custom-call(bf16[272,128]{1,0:T(8,128)(2,1)S(1)} %shard_map.103.g0, bf16[272,128]{1,0:T(8,128)(2,1)S(1)} %collective-permute-done.16.g1, bf16[272,128]{1,0:T(8,128)(2,1)S(1)} %collective-permute-done.17.g2, bf16[272,128]{1,0:T(8,128)(2,1)S(1)} %collective-permute-done.18.g3), custom_call_target="tpu_custom_call" | custom-call | flops 1000000000 | tf_op jit(solution)/shard_map/pallas_call | solution.py:465
  (2 shorter events, 0.1 us)
Async XLA Ops:
  1.7 5.0 %copy-start.2 = (bf16[128,8,128]{2,1,0:T(8,128)(2,1)S(1)}, bf16[128,8,128]{2,1,0:T(8,128)(2,1)}, u32[]{:S(2)}) copy-start(bf16[128,8,128]{2,1,0:T(8,128)(2,1)} %param.9) | copy-start | bytes 786436
  1.7 5.0 %copy-start.3 = (bf16[128,8,128]{2,1,0:T(8,128)(2,1)S(1)}, bf16[128,8,128]{2,1,0:T(8,128)(2,1)}, u32[]{:S(2)}) copy-start(bf16[128,8,128]{2,1,0:T(8,128)(2,1)} %param.6) | copy-start | bytes 786436
  2.0 8.4 %collective-permute-start = (bf16[2,2,128,128]{3,2,1,0:T(8,128)(2,1)S(1)}, bf16[2,2,128,128]{3,2,1,0:T(8,128)(2,1)S(1)}, u32[]{:S(2)}, u32[]{:S(2)}) collective-permute-start(bf16[2,2,128,128]{3,2,1,0:T(8,128)(2,1)S(1)} %get-tuple-element.47), channel_id=1, source_target_pairs={{0,12},{4,8},{8,4},{12,0},{16,28},{20,24},{24,20},{28,16},{1,13},{... | collective-permute-start | bytes 393224 | tf_op jit(solution)/shard_map/ppermute | solution.py:345
  6.1 7.7 %collective-permute-start.1 = (bf16[2,2,128,128]{3,2,1,0:T(8,128)(2,1)S(1)}, bf16[2,2,128,128]{3,2,1,0:T(8,128)(2,1)S(1)}, u32[]{:S(2)}, u32[]{:S(2)}) collective-permute-start(bf16[2,2,128,128]{3,2,1,0:T(8,128)(2,1)S(1)} %get-tuple-element.48), channel_id=1, source_target_pairs={{0,4},{4,0},{8,12},{12,8},{16,20},{20,16},{24,28},{28,24},{1,5},{5... | collective-permute-start | bytes 393224 | tf_op jit(solution)/shard_map/ppermute | solution.py:345
  6.6 7.2 %collective-permute-start.2 = (bf16[2,2,128,128]{3,2,1,0:T(8,128)(2,1)S(1)}, bf16[2,2,128,128]{3,2,1,0:T(8,128)(2,1)S(1)}, u32[]{:S(2)}, u32[]{:S(2)}) collective-permute-start(bf16[2,2,128,128]{3,2,1,0:T(8,128)(2,1)S(1)} %get-tuple-element.49), channel_id=1, source_target_pairs={{0,8},{4,12},{8,0},{12,4},{16,24},{20,28},{24,16},{28,20},{1,9},{5... | collective-permute-start | bytes 393224 | tf_op jit(solution)/shard_map/ppermute | solution.py:345
  6.8 7.0 %copy-start = (bf16[8,64,128]{2,1,0:T(8,128)(2,1)S(1)}, bf16[8,64,128]{2,1,0:T(8,128)(2,1)}, u32[]{:S(2)}) copy-start(bf16[8,64,128]{2,1,0:T(8,128)(2,1)} %refs_11_.1) | copy-start | bytes 393220
  7.0 11.7 %collective-permute-start.5 = (bf16[2,2,128,128]{3,2,1,0:T(8,128)(2,1)S(1)}, bf16[2,2,128,128]{3,2,1,0:T(8,128)(2,1)S(1)}, u32[]{:S(2)}, u32[]{:S(2)}) collective-permute-start(bf16[2,2,128,128]{3,2,1,0:T(8,128)(2,1)S(1)} %get-tuple-element.56), channel_id=1, source_target_pairs={{0,4},{4,0},{8,12},{12,8},{16,20},{20,16},{24,28},{28,24},{1,5},{5... | collective-permute-start | bytes 393224 | tf_op jit(solution)/shard_map/ppermute | solution.py:345
  8.9 9.8 %collective-permute-start.6 = (bf16[2,2,128,128]{3,2,1,0:T(8,128)(2,1)S(1)}, bf16[2,2,128,128]{3,2,1,0:T(8,128)(2,1)S(1)}, u32[]{:S(2)}, u32[]{:S(2)}) collective-permute-start(bf16[2,2,128,128]{3,2,1,0:T(8,128)(2,1)S(1)} %get-tuple-element.57), channel_id=1, source_target_pairs={{0,12},{4,8},{8,4},{12,0},{16,28},{20,24},{24,20},{28,16},{1,13},{... | collective-permute-start | bytes 393224 | tf_op jit(solution)/shard_map/ppermute | solution.py:345
  10.5 8.4 %collective-permute-start.7 = (bf16[2,2,128,128]{3,2,1,0:T(8,128)(2,1)S(1)}, bf16[2,2,128,128]{3,2,1,0:T(8,128)(2,1)S(1)}, u32[]{:S(2)}, u32[]{:S(2)}) collective-permute-start(bf16[2,2,128,128]{3,2,1,0:T(8,128)(2,1)S(1)} %get-tuple-element.58), channel_id=1, source_target_pairs={{0,8},{4,12},{8,0},{12,4},{16,24},{20,28},{24,16},{28,20},{1,9},{5... | collective-permute-start | bytes 393224 | tf_op jit(solution)/shard_map/ppermute | solution.py:345
  14.5 7.1 %collective-permute-start.3 = (bf16[1,272,128]{2,1,0:T(8,128)(2,1)S(1)}, bf16[1,272,128]{2,1,0:T(8,128)(2,1)S(1)}, u32[]{:S(2)}, u32[]{:S(2)}) collective-permute-start(bf16[1,272,128]{2,1,0:T(8,128)(2,1)S(1)} %get-tuple-element.50), channel_id=1, source_target_pairs={{0,16},{4,20},{8,24},{12,28},{16,0},{20,4},{24,8},{28,12},{1,17},{... | collective-permute-start | bytes 208904 | tf_op jit(solution)/shard_map/ppermute | solution.py:345
  17.3 6.9 %collective-permute-start.4 = (bf16[1,272,128]{2,1,0:T(8,128)(2,1)S(1)}, bf16[1,272,128]{2,1,0:T(8,128)(2,1)S(1)}, u32[]{:S(2)}, u32[]{:S(2)}) collective-permute-start(bf16[1,272,128]{2,1,0:T(8,128)(2,1)S(1)} %get-tuple-element.51), channel_id=1, source_target_pairs={{0,16},{4,20},{8,24},{12,28},{16,0},{20,4},{24,8},{28,12},{1,17},{... | collective-permute-start | bytes 208904 | tf_op jit(solution)/shard_map/ppermute | solution.py:345
  17.4 1.4 %copy-start.1 = (bf16[8,64,128]{2,1,0:T(8,128)(2,1)S(1)}, bf16[8,64,128]{2,1,0:T(8,128)(2,1)}, u32[]{:S(2)}) copy-start(bf16[8,64,128]{2,1,0:T(8,128)(2,1)} %wq_ref.1) | copy-start | bytes 393220
  25.2 6.3 %collective-permute-start.11 = (bf16[2,144,128]{2,1,0:T(8,128)(2,1)S(1)}, bf16[2,144,128]{2,1,0:T(8,128)(2,1)S(1)}, u32[]{:S(2)}, u32[]{:S(2)}) collective-permute-start(bf16[2,144,128]{2,1,0:T(8,128)(2,1)S(1)} %get-tuple-element.77), channel_id=1, source_target_pairs={{0,16},{4,20},{8,24},{12,28},{16,0},{20,4},{24,8},{28,12},{1,17},{... | collective-permute-start | bytes 221192 | tf_op jit(solution)/shard_map/ppermute | solution.py:345
  26.3 3.9 %collective-permute-start.14 = (f32[8,128]{1,0:T(8,128)S(1)}, f32[8,128]{1,0:T(8,128)S(1)}, u32[]{:S(2)}, u32[]{:S(2)}) collective-permute-start(f32[8,128]{1,0:T(8,128)S(1)} %get-tuple-element.84.refs_7_), channel_id=1, source_target_pairs={{0,3},{1,2},{2,1},{3,0},{4,7},{5,6},{6,5},{7,4},{8,11},{9,10},{10,... | collective-permute-start | bytes 12296 | tf_op jit(solution)/shard_map/ppermute | solution.py:345
  26.3 3.9 %collective-permute-start.13 = (f32[8,128]{1,0:T(8,128)S(1)}, f32[8,128]{1,0:T(8,128)S(1)}, u32[]{:S(2)}, u32[]{:S(2)}) collective-permute-start(f32[8,128]{1,0:T(8,128)S(1)} %get-tuple-element.84.refs_7_), channel_id=1, source_target_pairs={{0,2},{1,3},{2,0},{3,1},{4,6},{5,7},{6,4},{7,5},{8,10},{9,11},{10,... | collective-permute-start | bytes 12296 | tf_op jit(solution)/shard_map/ppermute | solution.py:345
  27.8 2.4 %collective-permute-start.12 = (f32[8,128]{1,0:T(8,128)S(1)}, f32[8,128]{1,0:T(8,128)S(1)}, u32[]{:S(2)}, u32[]{:S(2)}) collective-permute-start(f32[8,128]{1,0:T(8,128)S(1)} %get-tuple-element.84.refs_7_), channel_id=1, source_target_pairs={{0,1},{1,0},{2,3},{3,2},{4,5},{5,4},{6,7},{7,6},{8,9},{9,8},{10,11... | collective-permute-start | bytes 12296 | tf_op jit(solution)/shard_map/ppermute | solution.py:345
  32.3 6.3 %collective-permute-start.15 = (bf16[272,128]{1,0:T(8,128)(2,1)S(1)}, bf16[272,128]{1,0:T(8,128)(2,1)S(1)}, u32[]{:S(2)}, u32[]{:S(2)}) collective-permute-start(bf16[272,128]{1,0:T(8,128)(2,1)S(1)} %shard_map.102.refs_0_), channel_id=1, source_target_pairs={{0,16},{4,20},{8,24},{12,28},{16,0},{20,4},{24,8},{28,12},{1,17},{... | collective-permute-start | bytes 208904 | tf_op jit(solution)/shard_map/ppermute | solution.py:345
  33.3 6.9 %collective-permute-start.8 = (bf16[2,128,128]{2,1,0:T(8,128)(2,1)S(1)}, bf16[2,128,128]{2,1,0:T(8,128)(2,1)S(1)}, u32[]{:S(2)}, u32[]{:S(2)}) collective-permute-start(bf16[2,128,128]{2,1,0:T(8,128)(2,1)S(1)} %get-tuple-element.74), channel_id=1, source_target_pairs={{0,4},{4,0},{8,12},{12,8},{16,20},{20,16},{24,28},{28,24},{1,5},{5... | collective-permute-start | bytes 196616 | tf_op jit(solution)/shard_map/ppermute | solution.py:345
  33.8 8.5 %collective-permute-start.9 = (bf16[2,128,128]{2,1,0:T(8,128)(2,1)S(1)}, bf16[2,128,128]{2,1,0:T(8,128)(2,1)S(1)}, u32[]{:S(2)}, u32[]{:S(2)}) collective-permute-start(bf16[2,128,128]{2,1,0:T(8,128)(2,1)S(1)} %get-tuple-element.75), channel_id=1, source_target_pairs={{0,8},{4,12},{8,0},{12,4},{16,24},{20,28},{24,16},{28,20},{1,9},{5... | collective-permute-start | bytes 196616 | tf_op jit(solution)/shard_map/ppermute | solution.py:345
  36.0 6.2 %collective-permute-start.10 = (bf16[2,128,128]{2,1,0:T(8,128)(2,1)S(1)}, bf16[2,128,128]{2,1,0:T(8,128)(2,1)S(1)}, u32[]{:S(2)}, u32[]{:S(2)}) collective-permute-start(bf16[2,128,128]{2,1,0:T(8,128)(2,1)S(1)} %get-tuple-element.76), channel_id=1, source_target_pairs={{0,12},{4,8},{8,4},{12,0},{16,28},{20,24},{24,20},{28,16},{1,13},{... | collective-permute-start | bytes 196616 | tf_op jit(solution)/shard_map/ppermute | solution.py:345
  38.7 5.3 %collective-permute-start.18 = (bf16[272,128]{1,0:T(8,128)(2,1)S(1)}, bf16[272,128]{1,0:T(8,128)(2,1)S(1)}, u32[]{:S(2)}, u32[]{:S(2)}) collective-permute-start(bf16[272,128]{1,0:T(8,128)(2,1)S(1)} %shard_map.103.g0), channel_id=1, source_target_pairs={{0,12},{4,8},{8,4},{12,0},{16,28},{20,24},{24,20},{28,16},{1,13},{... | collective-permute-start | bytes 208904 | tf_op jit(solution)/shard_map/ppermute | solution.py:345
  39.8 4.3 %collective-permute-start.17 = (bf16[272,128]{1,0:T(8,128)(2,1)S(1)}, bf16[272,128]{1,0:T(8,128)(2,1)S(1)}, u32[]{:S(2)}, u32[]{:S(2)}) collective-permute-start(bf16[272,128]{1,0:T(8,128)(2,1)S(1)} %shard_map.103.g0), channel_id=1, source_target_pairs={{0,8},{4,12},{8,0},{12,4},{16,24},{20,28},{24,16},{28,20},{1,9},{5... | collective-permute-start | bytes 208904 | tf_op jit(solution)/shard_map/ppermute | solution.py:345
  40.2 4.5 %collective-permute-start.16 = (bf16[272,128]{1,0:T(8,128)(2,1)S(1)}, bf16[272,128]{1,0:T(8,128)(2,1)S(1)}, u32[]{:S(2)}, u32[]{:S(2)}) collective-permute-start(bf16[272,128]{1,0:T(8,128)(2,1)S(1)} %shard_map.103.g0), channel_id=1, source_target_pairs={{0,4},{4,0},{8,12},{12,8},{16,20},{20,16},{24,28},{28,24},{1,5},{5... | collective-permute-start | bytes 208904 | tf_op jit(solution)/shard_map/ppermute | solution.py:345
